TPU v7x, 128 devices: a whole 4x4x4 slice. The times are simulated.
128 devices in a mesh: dp: 32 (over z_hi, x, y), tensor: 4 (over z_lo, core).
Axes of the slice: x: 4, y: 4, z: 4 (z_hi: 2, z_lo: 2; z = z_hi * 2 + z_lo), core: 2. Of those that a mesh axis runs over, the one named last changes fastest.
Arguments:
- tokens: bfloat16 [16384, 1536], P(('dp', 'tensor')), may hold values from -6 to 6
- query_weight: bfloat16 [2, 1536, 1536], P(None, 'dp', 'tensor'), may hold values from -0.15625 to 0.15625
- key_weight: bfloat16 [2, 1536, 768], P(None, 'dp', 'tensor'), may hold values from -0.15625 to 0.15625
- value_weight: bfloat16 [2, 1536, 768], P(None, 'dp', 'tensor'), may hold values from -0.15625 to 0.15625
- out_weight: bfloat16 [2, 1536, 1536], P(None, 'tensor', 'dp'), may hold values from -1.25 to 1.25
- gate_weight: bfloat16 [2, 1536, 4096], P(None, 'dp', 'tensor'), may hold values from -0.15625 to 0.15625
- up_weight: bfloat16 [2, 1536, 4096], P(None, 'dp', 'tensor'), may hold values from -0.15625 to 0.15625
- down_weight: bfloat16 [2, 4096, 1536], P(None, 'tensor', 'dp'), may hold values from -0.09375 to 0.09375
- norm_gains: bfloat16 [2, 2, 1536], P(None, None, 'dp'), may hold values from 0.5 to 1.5
- grad_out: bfloat16 [16384, 1536], P(('dp', 'tensor')), may hold values from -6 to 6
Outputs:
- output: bfloat16 [16384, 1536], P(('dp', 'tensor'))
- input_grad: float32 [16384, 1536], P(('dp', 'tensor'))
- query_grad: float32 [2, 1536, 1536], P(None, 'dp', 'tensor')
- key_grad: float32 [2, 1536, 768], P(None, 'dp', 'tensor')
- value_grad: float32 [2, 1536, 768], P(None, 'dp', 'tensor')
- out_proj_grad: float32 [2, 1536, 1536], P(None, 'tensor', 'dp')
- gate_grad: float32 [2, 1536, 4096], P(None, 'dp', 'tensor')
- up_grad: float32 [2, 1536, 4096], P(None, 'dp', 'tensor')
- down_grad: float32 [2, 4096, 1536], P(None, 'tensor', 'dp')
- gains_grad: float32 [2, 2, 1536], P(None, None, 'dp')
All inputs are finite; a program needn't handle non-finite values.
Results may differ from a plain program's by a relative error of at most 0.04.
Values may be sent and summed in bfloat16 or wider, within the bound.
A program may use at most 192 MiB of HBM per device.

v0:
```python
import math

import jax
import jax.numpy as jnp
from jax import lax
from jax.sharding import PartitionSpec as P

HD = 96


norm_eps = 1e-05
rope_base = 100000.0


def rope_tables(seq_rows, head_width):
    half_width = head_width // 2
    position = jnp.arange(seq_rows, dtype=jnp.float32)[:, None]
    exponent = 2.0 * jnp.arange(half_width, dtype=jnp.float32) / head_width
    angles = position * (rope_base ** (-exponent))[None, :]
    return (jnp.cos(angles), jnp.sin(angles))


def rotate(values, cosine_table, sine_table):
    half_width = values.shape[-1] // 2
    first_half = values[..., :half_width]
    second_half = values[..., half_width:]
    cosine_wide = cosine_table[:, None, :]
    sine_wide = sine_table[:, None, :]
    return jnp.concatenate(
        [
            first_half * cosine_wide - second_half * sine_wide,
            second_half * cosine_wide + first_half * sine_wide,
        ],
        axis=-1,
    )


def unrotate(values, cosine_table, sine_table):
    half_width = values.shape[-1] // 2
    first_half = values[..., :half_width]
    second_half = values[..., half_width:]
    cosine_wide = cosine_table[:, None, :]
    sine_wide = sine_table[:, None, :]
    return jnp.concatenate(
        [
            first_half * cosine_wide + second_half * sine_wide,
            second_half * cosine_wide - first_half * sine_wide,
        ],
        axis=-1,
    )


def contract_rows(left_rows, right_rows):
    return lax.dot_general(
        left_rows, right_rows, (((0,), (0,)), ((), ())), preferred_element_type=jnp.float32
    )


def times_transpose(left_rows, weight):
    return lax.dot_general(
        left_rows, weight, (((1,), (1,)), ((), ())), preferred_element_type=jnp.float32
    )


def gather_rows(normed):
    return lax.all_gather(normed, "tensor", axis=0, tiled=True)


def gather_grads(gradient):
    return lax.all_gather(gradient, "tensor", axis=0, tiled=True)


def branch_sum(left_rows, weight):
    return lax.psum_scatter(
        jnp.dot(left_rows, weight, preferred_element_type=jnp.float32).astype(jnp.bfloat16),
        "tensor",
        scatter_dimension=0,
        tiled=True,
    ).astype(jnp.float32)


def input_sum(grad_pairs):
    summed = None
    for grad_part, weight in grad_pairs:
        product = times_transpose(grad_part, weight)
        summed = product if summed is None else summed + product
    return lax.psum_scatter(
        summed.astype(jnp.bfloat16), "tensor", scatter_dimension=0, tiled=True
    ).astype(jnp.float32)


def fetch_weights(shards):
    return (
        lax.all_gather(shards[0], "dp", axis=0, tiled=True),
        lax.all_gather(shards[1], "dp", axis=0, tiled=True),
        lax.all_gather(shards[2], "dp", axis=0, tiled=True),
        lax.all_gather(shards[3], "dp", axis=1, tiled=True),
        lax.all_gather(shards[4], "dp", axis=0, tiled=True),
        lax.all_gather(shards[5], "dp", axis=0, tiled=True),
        lax.all_gather(shards[6], "dp", axis=1, tiled=True),
        lax.all_gather(shards[7], "dp", axis=1, tiled=True),
    )


def fetch_again(shards):
    return (
        lax.all_gather(shards[0], "dp", axis=0, tiled=True),
        lax.all_gather(shards[1], "dp", axis=0, tiled=True),
        lax.all_gather(shards[2], "dp", axis=0, tiled=True),
        lax.all_gather(shards[3], "dp", axis=1, tiled=True),
        lax.all_gather(shards[4], "dp", axis=0, tiled=True),
        lax.all_gather(shards[5], "dp", axis=0, tiled=True),
        lax.all_gather(shards[6], "dp", axis=1, tiled=True),
        lax.all_gather(shards[7], "dp", axis=1, tiled=True),
    )


def norm_forward(rows_in, gain):
    inverse = lax.rsqrt(jnp.mean(rows_in * rows_in, axis=-1, keepdims=True) + norm_eps)
    return (inverse, (rows_in * inverse * gain).astype(jnp.bfloat16))


def norm_backward(rows_in, inverse, gain, grad_normed):
    scaled = rows_in * inverse
    grad_gain = jnp.sum(grad_normed * scaled, axis=0)
    grad_scaled = grad_normed * gain
    grad_input = inverse * (
        grad_scaled - scaled * jnp.mean(grad_scaled * scaled, axis=-1, keepdims=True)
    )
    return (grad_input, grad_gain)


def masked_scores(query_part, key_rows, offset, block_rows, scaling):
    seq_rows = key_rows.shape[0]
    raw_scores = (
        jnp.einsum("qkgd,skd->kgqs", query_part, key_rows, preferred_element_type=jnp.float32)
        * scaling
    )
    row_places = offset + jnp.arange(block_rows, dtype=jnp.int32)
    key_places = jnp.arange(seq_rows, dtype=jnp.int32)
    allowed = row_places[:, None] >= key_places[None, :]
    return jnp.where(allowed, raw_scores, -1e30)


def attend(query_turned, key_turned, value_rows, scaling):
    seq_rows = query_turned.shape[0]
    block_rows = min(512, seq_rows)
    block_count = seq_rows // block_rows
    query_blocks = query_turned.reshape((block_count, block_rows) + query_turned.shape[1:])
    offsets = jnp.arange(block_count, dtype=jnp.int32) * block_rows

    def one_block(inputs):
        query_part, offset = inputs
        scores = masked_scores(query_part, key_turned, offset, block_rows, scaling)
        row_peak = jnp.max(scores, axis=-1, keepdims=True)
        exponent = jnp.exp(scores - row_peak)
        denominator = jnp.sum(exponent, axis=-1, keepdims=True)
        attn_weights = (exponent / denominator).astype(jnp.bfloat16)
        outputs = jnp.einsum(
            "kgqs,skd->qkgd", attn_weights, value_rows, preferred_element_type=jnp.float32
        )
        return (outputs, row_peak[..., 0] + jnp.log(denominator[..., 0]))

    outputs, logsums = lax.map(one_block, (query_blocks, offsets))
    return (outputs.reshape(seq_rows, -1), logsums)


def attend_back(query_turned, key_turned, value_rows, grad_attended, logsums, scaling):
    seq_rows = query_turned.shape[0]
    block_rows = min(512, seq_rows)
    block_count = seq_rows // block_rows
    query_blocks = query_turned.reshape((block_count, block_rows) + query_turned.shape[1:])
    grad_blocks = grad_attended.reshape((block_count, block_rows) + grad_attended.shape[1:])
    offsets = jnp.arange(block_count, dtype=jnp.int32) * block_rows

    def one_block(carried, inputs):
        grad_keys, grad_values = carried
        query_part, grad_part, logsum_part, offset = inputs
        scores = masked_scores(query_part, key_turned, offset, block_rows, scaling)
        attn_weights = jnp.exp(scores - logsum_part[..., None])
        grad_weights = jnp.einsum(
            "qkgd,skd->kgqs", grad_part, value_rows, preferred_element_type=jnp.float32
        )
        inner_sum = jnp.sum(grad_weights * attn_weights, axis=-1, keepdims=True)
        grad_scores = (attn_weights * (grad_weights - inner_sum)).astype(jnp.bfloat16)
        grad_query = (
            jnp.einsum(
                "kgqs,skd->qkgd", grad_scores, key_turned, preferred_element_type=jnp.float32
            )
            * scaling
        )
        grad_keys = (
            grad_keys
            + jnp.einsum(
                "kgqs,qkgd->skd", grad_scores, query_part, preferred_element_type=jnp.float32
            )
            * scaling
        )
        grad_values = grad_values + jnp.einsum(
            "kgqs,qkgd->skd",
            attn_weights.astype(jnp.bfloat16),
            grad_part,
            preferred_element_type=jnp.float32,
        )
        return ((grad_keys, grad_values), grad_query)

    zero_keys = jnp.zeros(key_turned.shape, jnp.float32)
    (grad_keys, grad_values), grad_query = lax.scan(
        one_block, (zero_keys, zero_keys), (query_blocks, grad_blocks, logsums, offsets)
    )
    return (grad_query.reshape(seq_rows, -1), grad_keys, grad_values)


def body(
    tokens,
    query_weight,
    key_weight,
    value_weight,
    out_weight,
    gate_weight,
    up_weight,
    down_weight,
    norm_gains,
    grad_out,
):
    layers = query_weight.shape[0]
    local_rows = tokens.shape[0]
    heads_local = query_weight.shape[2] // HD
    kv_local = key_weight.shape[2] // HD
    group_size = heads_local // kv_local
    scaling = 1.0 / math.sqrt(HD)
    seq_rows = local_rows * lax.axis_size("tensor")
    cosine_table, sine_table = rope_tables(seq_rows, HD)
    arrays = (
        query_weight,
        key_weight,
        value_weight,
        out_weight,
        gate_weight,
        up_weight,
        down_weight,
        norm_gains,
    )
    residual = tokens.astype(jnp.float32)
    saved = []
    kept_weights = []
    for layer_index in range(layers):
        shards = tuple((array[layer_index] for array in arrays))
        weights = fetch_weights(shards)
        query_full, key_full, value_full, out_full, gate_full, up_full, down_full, gain_full = (
            weights
        )
        gain_values = gain_full.astype(jnp.float32)
        inverse_first, normed_first = norm_forward(residual, gain_values[0])
        rows_first = gather_rows(normed_first)
        query_rows = jnp.dot(rows_first, query_full, preferred_element_type=jnp.float32).reshape(
            seq_rows, heads_local, HD
        )
        key_rows = jnp.dot(rows_first, key_full, preferred_element_type=jnp.float32).reshape(
            seq_rows, kv_local, HD
        )
        value_rows = (
            jnp.dot(rows_first, value_full, preferred_element_type=jnp.float32)
            .astype(jnp.bfloat16)
            .reshape(seq_rows, kv_local, HD)
        )
        query_turned = (
            rotate(query_rows, cosine_table, sine_table)
            .astype(jnp.bfloat16)
            .reshape(seq_rows, kv_local, group_size, HD)
        )
        key_turned = rotate(key_rows, cosine_table, sine_table).astype(jnp.bfloat16)
        attended, logsums = attend(query_turned, key_turned, value_rows, scaling)
        attended_low = attended.astype(jnp.bfloat16)
        middle = residual + branch_sum(attended_low, out_full)
        inverse_second, normed_second = norm_forward(middle, gain_values[1])
        rows_second = gather_rows(normed_second)
        gate_rows = jnp.dot(rows_second, gate_full, preferred_element_type=jnp.float32)
        upward = jnp.dot(rows_second, up_full, preferred_element_type=jnp.float32)
        hidden = (jax.nn.silu(gate_rows) * upward).astype(jnp.bfloat16)
        new_residual = middle + branch_sum(hidden, down_full)
        saved.append(
            (
                residual,
                inverse_first,
                rows_first,
                query_turned,
                key_turned,
                value_rows,
                attended_low,
                logsums,
                middle,
                inverse_second,
                rows_second,
                gate_rows,
                upward,
                hidden,
            )
        )
        kept_weights.append(None)
        residual = new_residual
    output = residual.astype(jnp.bfloat16)
    grad_residual = grad_out.astype(jnp.float32)
    layer_results = [None] * layers
    for layer_index in range(layers - 1, -1, -1):
        (
            residual,
            inverse_first,
            rows_first,
            query_turned,
            key_turned,
            value_rows,
            attended_low,
            logsums,
            middle,
            inverse_second,
            rows_second,
            gate_rows,
            upward,
            hidden,
        ) = saved[layer_index]
        weights = fetch_again(tuple((array[layer_index] for array in arrays)))
        query_full, key_full, value_full, out_full, gate_full, up_full, down_full, gain_full = (
            weights
        )
        gain_values = gain_full.astype(jnp.float32)
        grad_rows_mlp = gather_grads(grad_residual.astype(jnp.bfloat16))
        grad_hidden = times_transpose(grad_rows_mlp, down_full)
        grad_down = contract_rows(hidden, grad_rows_mlp)
        sigma = jax.nn.sigmoid(gate_rows)
        grad_gate_rows = (grad_hidden * upward * sigma * (1.0 + gate_rows * (1.0 - sigma))).astype(
            jnp.bfloat16
        )
        grad_upward = (grad_hidden * gate_rows * sigma).astype(jnp.bfloat16)
        grad_gate = contract_rows(rows_second, grad_gate_rows)
        grad_up = contract_rows(rows_second, grad_upward)
        grad_normed_second = input_sum(((grad_gate_rows, gate_full), (grad_upward, up_full)))
        grad_norm_second, gain_part_second = norm_backward(
            middle, inverse_second, gain_values[1], grad_normed_second
        )
        grad_middle = grad_residual + grad_norm_second
        grad_rows_attn = gather_grads(grad_middle.astype(jnp.bfloat16))
        grad_attended = times_transpose(grad_rows_attn, out_full).astype(jnp.bfloat16)
        grad_out_proj = contract_rows(attended_low, grad_rows_attn)
        grad_query_turned, grad_key_turned, grad_value_rows = attend_back(
            query_turned,
            key_turned,
            value_rows,
            grad_attended.reshape(seq_rows, kv_local, group_size, HD),
            logsums,
            scaling,
        )
        grad_query_rows = (
            unrotate(grad_query_turned.reshape(seq_rows, heads_local, HD), cosine_table, sine_table)
            .reshape(seq_rows, -1)
            .astype(jnp.bfloat16)
        )
        grad_key_rows = (
            unrotate(grad_key_turned, cosine_table, sine_table)
            .reshape(seq_rows, -1)
            .astype(jnp.bfloat16)
        )
        grad_value_low = grad_value_rows.reshape(seq_rows, -1).astype(jnp.bfloat16)
        grad_query = contract_rows(rows_first, grad_query_rows)
        grad_key = contract_rows(rows_first, grad_key_rows)
        grad_value = contract_rows(rows_first, grad_value_low)
        grad_normed_first = input_sum(
            ((grad_query_rows, query_full), (grad_key_rows, key_full), (grad_value_low, value_full))
        )
        grad_norm_first, gain_part_first = norm_backward(
            residual, inverse_first, gain_values[0], grad_normed_first
        )
        grad_residual = grad_middle + grad_norm_first
        gain_sums = lax.psum(jnp.stack([gain_part_first, gain_part_second]), "tensor")
        layer_grads = (
            grad_query,
            grad_key,
            grad_value,
            grad_out_proj,
            grad_gate,
            grad_up,
            grad_down,
            gain_sums,
        )
        layer_results[layer_index] = layer_grads
    stacked = tuple(
        (
            jnp.stack([layer_results[layer_index][kind_index] for layer_index in range(layers)])
            for kind_index in range(8)
        )
    )
    reduced = (
        lax.psum_scatter(
            stacked[0].astype(jnp.bfloat16), "dp", scatter_dimension=1, tiled=True
        ).astype(jnp.float32),
        lax.psum_scatter(
            stacked[1].astype(jnp.bfloat16), "dp", scatter_dimension=1, tiled=True
        ).astype(jnp.float32),
        lax.psum_scatter(
            stacked[2].astype(jnp.bfloat16), "dp", scatter_dimension=1, tiled=True
        ).astype(jnp.float32),
        lax.psum_scatter(
            stacked[3].astype(jnp.bfloat16), "dp", scatter_dimension=2, tiled=True
        ).astype(jnp.float32),
        lax.psum_scatter(
            stacked[4].astype(jnp.bfloat16), "dp", scatter_dimension=1, tiled=True
        ).astype(jnp.float32),
        lax.psum_scatter(
            stacked[5].astype(jnp.bfloat16), "dp", scatter_dimension=1, tiled=True
        ).astype(jnp.float32),
        lax.psum_scatter(
            stacked[6].astype(jnp.bfloat16), "dp", scatter_dimension=2, tiled=True
        ).astype(jnp.float32),
        lax.psum_scatter(
            stacked[7].astype(jnp.bfloat16), "dp", scatter_dimension=2, tiled=True
        ).astype(jnp.float32),
    )
    return (
        output,
        grad_residual,
        reduced[0],
        reduced[1],
        reduced[2],
        reduced[3],
        reduced[4],
        reduced[5],
        reduced[6],
        reduced[7],
    )


def solution(mesh):
    return jax.shard_map(
        body,
        mesh=mesh,
        in_specs=(
            P(("dp", "tensor"), None),
            P(None, "dp", "tensor"),
            P(None, "dp", "tensor"),
            P(None, "dp", "tensor"),
            P(None, "tensor", "dp"),
            P(None, "dp", "tensor"),
            P(None, "dp", "tensor"),
            P(None, "tensor", "dp"),
            P(None, None, "dp"),
            P(("dp", "tensor"), None),
        ),
        out_specs=(
            P(("dp", "tensor"), None),
            P(("dp", "tensor"), None),
            P(None, "dp", "tensor"),
            P(None, "dp", "tensor"),
            P(None, "dp", "tensor"),
            P(None, "tensor", "dp"),
            P(None, "dp", "tensor"),
            P(None, "dp", "tensor"),
            P(None, "tensor", "dp"),
            P(None, None, "dp"),
        ),
        check_vma=False,
    )
```

profile of v0, /device:TPU:0, one launch (start us, length us, event | category | flops | bytes accessed | tf_op | source)
XLA Modules:
  0.0 2906.0 jit_solution(2284947225294385828)
XLA Ops:
  9.2 100.1 %all-gather = bf16[1,2,1536]{1,0,2:T(2,128)(2,1)S(1)} all-gather(bf16[1,2,48]{1,0,2:T(2,128)(2,1)S(1)} %copy.86), channel_id=2, replica_groups=mesh['dp'=32,'tensor'=4] {'dp'}, dimensions={2}, use_global_device_ids=true | all-gather | bytes 6336 | tf_op jit(solution)/shard_map/all_gather | solution.py:101
  110.3 25.1 slice_reduce_fusion.2
  140.9 97.2 %all-gather.1 = bf16[1,1536,192]{2,1,0:T(8,128)(2,1)} all-gather(bf16[1,48,192]{2,1,0:T(8,128)(2,1)S(1)} %get-tuple-element.187), channel_id=3, replica_groups=mesh['dp'=32,'tensor'=4] {'dp'}, dimensions={1}, use_global_device_ids=true | all-gather | bytes 608256 | tf_op jit(solution)/shard_map/all_gather | solution.py:96
  238.2 93.9 %all-gather.2 = bf16[1,1536,192]{2,1,0:T(8,128)(2,1)S(1)} all-gather(bf16[1,48,192]{2,1,0:T(8,128)(2,1)S(1)} %get-tuple-element.185), channel_id=4, replica_groups=mesh['dp'=32,'tensor'=4] {'dp'}, dimensions={1}, use_global_device_ids=true | all-gather | bytes 608256 | tf_op jit(solution)/shard_map/all_gather | solution.py:95
  341.7 3.6 convolution_convert_fusion.7
  346.2 18.1 reduce-scatter.15.cloned.1.call-done
  369.1 77.0 %all-gather.55.cloned.1.call-done = bf16[1,1536,1024]{2,1,0:T(8,128)(2,1)} async-done(((bf16[1,48,1024]{2,1,0:T(8,128)(2,1)}), bf16[1,1536,1024]{2,1,0:T(8,128)(2,1)}) %all-gather.55.cloned.1.call-update) | async-done | bytes 3145744 | tf_op jit(solution)/shard_map/all_gather | solution.py:98
  446.1 23.7 all-gather.37.cloned.1.call-done
  469.7 5.5 fusion.36
  475.2 76.4 %all-gather.57.cloned.1.call-done = bf16[1,1536,1024]{2,1,0:T(8,128)(2,1)} async-done(((bf16[1,48,1024]{2,1,0:T(8,128)(2,1)}), bf16[1,1536,1024]{2,1,0:T(8,128)(2,1)}) %all-gather.57.cloned.1.call-update) | async-done | bytes 3145744 | tf_op jit(solution)/shard_map/all_gather | solution.py:99
  551.6 6.5 multiply_convert_fusion.5
  558.1 71.2 %all-gather.59.cloned.1.call-done = bf16[1,1024,1536]{1,2,0:T(8,128)(2,1)} async-done(((bf16[1,1024,48]{1,2,0:T(8,128)(2,1)}), bf16[1,1024,1536]{1,2,0:T(8,128)(2,1)}) %all-gather.59.cloned.1.call-update) | async-done | bytes 3145744 | tf_op jit(solution)/shard_map/all_gather | solution.py:100
  629.3 5.2 fusion.38
  634.7 94.8 %all-gather.8 = bf16[1,2,1536]{1,0,2:T(2,128)(2,1)S(1)} all-gather(bf16[1,2,48]{1,0,2:T(2,128)(2,1)S(1)} %copy.87), channel_id=10, replica_groups=mesh['dp'=32,'tensor'=4] {'dp'}, dimensions={2}, use_global_device_ids=true | all-gather | bytes 6336 | tf_op jit(solution)/shard_map/all_gather | solution.py:101
  730.3 24.8 slice_reduce_fusion.1
  758.7 97.2 %all-gather.9 = bf16[1,1536,192]{2,1,0:T(8,128)(2,1)} all-gather(bf16[1,48,192]{2,1,0:T(8,128)(2,1)S(1)} %copy-done.73), channel_id=11, replica_groups=mesh['dp'=32,'tensor'=4] {'dp'}, dimensions={1}, use_global_device_ids=true | all-gather | bytes 608256 | tf_op jit(solution)/shard_map/all_gather | solution.py:96
  855.9 98.9 %all-gather.10 = bf16[1,1536,192]{2,1,0:T(8,128)(2,1)} all-gather(bf16[1,48,192]{2,1,0:T(8,128)(2,1)S(1)} %copy-done.72), channel_id=12, replica_groups=mesh['dp'=32,'tensor'=4] {'dp'}, dimensions={1}, use_global_device_ids=true | all-gather | bytes 608256 | tf_op jit(solution)/shard_map/all_gather | solution.py:95
  969.1 19.6 reduce-scatter.19.cloned.1.call-done
  993.7 76.7 %all-gather.67.cloned.1.call-done = bf16[1,1536,1024]{2,1,0:T(8,128)(2,1)} async-done(((bf16[1,48,1024]{2,1,0:T(8,128)(2,1)}), bf16[1,1536,1024]{2,1,0:T(8,128)(2,1)}) %all-gather.67.cloned.1.call-update) | async-done | bytes 3145744 | tf_op jit(solution)/shard_map/all_gather | solution.py:99
  1070.4 23.7 all-gather.41.cloned.1.call-done
  1094.0 5.5 fusion.21
  1099.6 76.2 %all-gather.65.cloned.1.call-done = bf16[1,1536,1024]{2,1,0:T(8,128)(2,1)} async-done(((bf16[1,48,1024]{2,1,0:T(8,128)(2,1)}), bf16[1,1536,1024]{2,1,0:T(8,128)(2,1)}) %all-gather.65.cloned.1.call-update) | async-done | bytes 3145744 | tf_op jit(solution)/shard_map/all_gather | solution.py:98
  1175.8 5.5 fusion.25
  1181.3 17.6 all-gather.43.cloned.1.call-done
  1198.9 81.2 %all-gather.69.cloned.1.call-done = bf16[1,1024,1536]{1,2,0:T(8,128)(2,1)} async-done(((bf16[1,1024,48]{1,2,0:T(8,128)(2,1)}), bf16[1,1024,1536]{1,2,0:T(8,128)(2,1)}) %all-gather.69.cloned.1.call-update) | async-done | bytes 3145744 | tf_op jit(solution)/shard_map/all_gather | solution.py:100
  1280.1 7.2 multiply_convert_fusion.2
  1293.0 20.8 reduce-scatter.23.cloned.1.call-done
  1320.2 24.3 all-gather.45.cloned.1.call-done
  1360.3 5.3 fusion.41
  1365.6 19.7 reduce-scatter.25.cloned.1.call-done
  1387.8 25.0 reduce-scatter.21.cloned.1.call-done
  1416.4 25.4 all-gather.47.cloned.1.call-done
  1441.8 6.1 multiply_convert_fusion
  1453.6 25.1 reduce-scatter.27.cloned.1.call-done
  1483.0 25.7 all-gather.49.cloned.1.call-done
  1530.1 19.4 reduce-scatter.29.cloned.1.call-done
  1551.4 10.3 all-reduce.4
  1570.0 3.7 fusion.11
  1578.8 3.7 fusion.9
  1587.9 3.7 fusion.13
  1601.1 16.4 copy.63
  1621.6 6.9 copy.62
  1630.7 4.8 copy.61
  1642.9 145.5 %reduce-scatter.37.cloned.1.call-done = bf16[48,4]{1,0:T(8,128)(2,1)} async-done(((bf16[1536,4]{1,0:T(8,128)(2,1)}), bf16[48,4]{1,0:T(8,128)(2,1)}) %reduce-scatter.37.cloned.1.call-update) | async-done | bytes 400
  1789.9 227.6 %reduce-scatter.31.cloned.1.call-done = bf16[2,48,384]{2,1,0:T(8,128)(2,1)} async-done(((bf16[2,1536,384]{2,1,0:T(8,128)(2,1)}), bf16[2,48,384]{2,1,0:T(8,128)(2,1)}) %reduce-scatter.31.cloned.1.call-update) | async-done | bytes 73744 | tf_op jit(solution)/shard_map/reduce_scatter | solution.py:393
  2019.1 234.2 %reduce-scatter.35.cloned.1.call-done = bf16[2,48,1024]{2,1,0:T(8,128)(2,1)} async-done(((bf16[2,1536,1024]{2,1,0:T(8,128)(2,1)}), bf16[2,48,1024]{2,1,0:T(8,128)(2,1)}) %reduce-scatter.35.cloned.1.call-update) | async-done | bytes 196624 | tf_op jit(solution)/shard_map/reduce_scatter | solution.py:408
  2254.9 233.7 %reduce-scatter.33.cloned.1.call-done = bf16[2,48,1024]{2,1,0:T(8,128)(2,1)} async-done(((bf16[2,1536,1024]{2,1,0:T(8,128)(2,1)}), bf16[2,48,1024]{2,1,0:T(8,128)(2,1)}) %reduce-scatter.33.cloned.1.call-update) | async-done | bytes 196624 | tf_op jit(solution)/shard_map/reduce_scatter | solution.py:405
  2490.3 402.6 %all-reduce.8.cloned.1.call-done = (bf16[2,1536,192]{2,0,1:T(2,128)(2,1)}, bf16[2,1536,192]{2,0,1:T(2,128)(2,1)}, bf16[2,384,1536]{1,0,2:T(2,128)(2,1)}, bf16[2,1024,1536]{1,0,2:T(2,128)(2,1)}) async-done(((bf16[2,1536,192]{2,0,1:T(2,128)(2,1)}, bf16[2,1536,192]{2,0,1:T(2,128)(2,1)}, bf16[2,384,1536]{1,0,2:T(2,128)(2,1)}, bf16[2,1024,1536]{1,0,2:T(2,128)(2,1)}), (bf16[2,1536,192]{2,0,1:T(2,128)(2,1)}, ...) | async-done | bytes 11010064
  (428 shorter events, 166.7 us)
Async XLA Ops:
  7.2 324.9 %all-gather.35.cloned.1.call-start = ((), (), s32[]{:S(2)}) async-start(), calls=%async_computation.12 | async-start | bytes 1966080 | tf_op jit(solution)/shard_map/all_gather | solution.py:66
  8.4 127.6 %copy-start.4 = (bf16[128,1536]{1,0:T(8,128)(2,1)S(1)}, bf16[128,1536]{1,0:T(8,128)(2,1)}, u32[]{:S(2)}) copy-start(bf16[128,1536]{1,0:T(8,128)(2,1)} %param.10) | copy-start | bytes 1179652
  8.4 128.5 %copy-start.91 = (f32[128]{0:T(128)}, f32[128]{0:T(128)S(1)}, u32[]{:S(2)}) copy-start(f32[128]{0:T(128)S(1)} %add_rsqrt_fusion.3) | copy-start | bytes 1540
  109.4 28.3 copy-start.75
  110.2 29.0 copy-start.76
  110.2 29.6 %copy-start.77 = (bf16[2,48,192]{2,1,0:T(8,128)(2,1)S(1)}, bf16[2,48,192]{2,1,0:T(8,128)(2,1)}, u32[]{:S(2)}) copy-start(bf16[2,48,192]{2,1,0:T(8,128)(2,1)} %param.13) | copy-start | bytes 110596
  136.9 197.7 %all-gather.51.cloned.1.call-start = ((), (), s32[]{:S(2)}) async-start(), calls=%async_computation.31 | async-start | bytes 1216512 | tf_op jit(solution)/shard_map/all_gather | solution.py:94
  137.7 204.0 %all-gather.53.cloned.1.call-start = ((), (), s32[]{:S(2)}) async-start(), calls=%async_computation.32 | async-start | bytes 1216512 | tf_op jit(solution)/shard_map/all_gather | solution.py:97
  138.4 225.9 %reduce-scatter.15.cloned.1.call-start = ((), (), s32[]{:S(2)}) async-start(), calls=%async_computation.13 | async-start | bytes 1966080 | tf_op jit(solution)/shard_map/reduce_scatter | solution.py:74
  140.9 819.0 %copy-start.10 = (f32[512,48]{0,1:T(8,128)}, f32[512,48]{0,1:T(8,128)S(1)}, u32[]{:S(2)}) copy-start(f32[512,48]{0,1:T(8,128)S(1)} %get-tuple-element.190) | copy-start | bytes 294916
  140.9 819.0 %copy-start.13 = (f32[512,48]{0,1:T(8,128)}, f32[512,48]{0,1:T(8,128)S(1)}, u32[]{:S(2)}) copy-start(f32[512,48]{0,1:T(8,128)S(1)} %get-tuple-element.191) | copy-start | bytes 294916
  345.3 100.7 %all-gather.55.cloned.1.call-start = ((), (), s32[]{:S(2)}) async-start(), calls=%async_computation.33 | async-start | bytes 3244032 | tf_op jit(solution)/shard_map/all_gather | solution.py:98
  346.1 123.6 %all-gather.37.cloned.1.call-start = ((), (), s32[]{:S(2)}) async-start(), calls=%async_computation.14 | async-start | bytes 1966080 | tf_op jit(solution)/shard_map/all_gather | solution.py:66
  365.5 109.7 %copy-start.87 = (f32[128]{0:T(128)}, f32[128]{0:T(128)S(1)}, u32[]{:S(2)}) copy-start(f32[128]{0:T(128)S(1)} %add_rsqrt_fusion.2) | copy-start | bytes 1540
  367.5 184.2 %all-gather.57.cloned.1.call-start = ((), (), s32[]{:S(2)}) async-start(), calls=%async_computation.34 | async-start | bytes 3244032 | tf_op jit(solution)/shard_map/all_gather | solution.py:99
  368.2 261.1 %all-gather.59.cloned.1.call-start = ((), (), s32[]{:S(2)}) async-start(), calls=%async_computation.35 | async-start | bytes 3244032 | tf_op jit(solution)/shard_map/all_gather | solution.py:100
  369.0 386.1 %reduce-scatter.17.cloned.1.call-start = ((), (), s32[]{:S(2)}) async-start(), calls=%async_computation.15 | async-start | bytes 1966080 | tf_op jit(solution)/shard_map/reduce_scatter | solution.py:74
  634.5 120.6 %copy-start.8 = (bf16[128,1536]{1,0:T(8,128)(2,1)S(1)}, bf16[128,1536]{1,0:T(8,128)(2,1)}, u32[]{:S(2)}) copy-start(bf16[128,1536]{1,0:T(8,128)(2,1)} %reduce-scatter.15.cloned.1.call-done) | copy-start | bytes 1179652
  634.5 320.2 %all-gather.39.cloned.1.call-start = ((), (), s32[]{:S(2)}) async-start(), calls=%async_computation.16 | async-start | bytes 1966080 | tf_op jit(solution)/shard_map/all_gather | solution.py:66
  755.1 100.8 %copy-start.70 = (f32[1536]{0:T(1024)}, f32[1536]{0:T(1024)S(1)}, u32[]{:S(2)}) copy-start(f32[1536]{0:T(1024)S(1)} %get-tuple-element.138) | copy-start | bytes 18436
  755.1 100.8 %copy-start.72 = (bf16[1,48,192]{2,1,0:T(8,128)(2,1)S(1)}, bf16[1,48,192]{2,1,0:T(8,128)(2,1)}, u32[]{:S(2)}) copy-start(bf16[1,48,192]{2,1,0:T(8,128)(2,1)} %get-tuple-element.184) | copy-start | bytes 55300
  756.4 200.6 %copy-start.94 = (f32[128]{0:T(128)}, f32[128]{0:T(128)S(1)}, u32[]{:S(2)}) copy-start(f32[128]{0:T(128)S(1)} %add_rsqrt_fusion.1) | copy-start | bytes 1540
  757.4 199.8 %all-gather.61.cloned.1.call-start = ((), (), s32[]{:S(2)}) async-start(), calls=%async_computation.36 | async-start | bytes 1216512 | tf_op jit(solution)/shard_map/all_gather | solution.py:94
  758.1 206.7 %all-gather.63.cloned.1.call-start = ((), (), s32[]{:S(2)}) async-start(), calls=%async_computation.37 | async-start | bytes 1216512 | tf_op jit(solution)/shard_map/all_gather | solution.py:97
  758.7 230.0 %reduce-scatter.19.cloned.1.call-start = ((), (), s32[]{:S(2)}) async-start(), calls=%async_computation.17 | async-start | bytes 1966080 | tf_op jit(solution)/shard_map/reduce_scatter | solution.py:74
  968.4 102.0 %all-gather.67.cloned.1.call-start = ((), (), s32[]{:S(2)}) async-start(), calls=%async_computation.39 | async-start | bytes 3244032 | tf_op jit(solution)/shard_map/all_gather | solution.py:99
  969.0 125.0 %all-gather.41.cloned.1.call-start = ((), (), s32[]{:S(2)}) async-start(), calls=%async_computation.18 | async-start | bytes 1966080 | tf_op jit(solution)/shard_map/all_gather | solution.py:66
  989.8 109.8 %copy-start.90 = (f32[128]{0:T(128)}, f32[128]{0:T(128)S(1)}, u32[]{:S(2)}) copy-start(f32[128]{0:T(128)S(1)} %add_rsqrt_fusion) | copy-start | bytes 1540
  991.7 184.1 %all-gather.65.cloned.1.call-start = ((), (), s32[]{:S(2)}) async-start(), calls=%async_computation.38 | async-start | bytes 3244032 | tf_op jit(solution)/shard_map/all_gather | solution.py:98
  992.3 206.6 %all-gather.43.cloned.1.call-start = ((), (), s32[]{:S(2)}) async-start(), calls=%async_computation.20 | async-start | bytes 1966080 | tf_op jit(solution)/shard_map/all_gather | solution.py:70
  992.9 287.2 %all-gather.69.cloned.1.call-start = ((), (), s32[]{:S(2)}) async-start(), calls=%async_computation.40 | async-start | bytes 3244032 | tf_op jit(solution)/shard_map/all_gather | solution.py:100
  993.5 320.4 %reduce-scatter.23.cloned.1.call-start = ((), (), s32[]{:S(2)}) async-start(), calls=%async_computation.21 | async-start | bytes 1966080 | tf_op jit(solution)/shard_map/reduce_scatter | solution.py:87
  1293.0 51.6 %all-gather.45.cloned.1.call-start = ((), (), s32[]{:S(2)}) async-start(), calls=%async_computation.22 | async-start | bytes 1966080 | tf_op jit(solution)/shard_map/all_gather | solution.py:70
  1318.6 66.8 %reduce-scatter.25.cloned.1.call-start = ((), (), s32[]{:S(2)}) async-start(), calls=%async_computation.23 | async-start | bytes 1966080 | tf_op jit(solution)/shard_map/reduce_scatter | solution.py:87
  1360.2 52.5 %reduce-scatter.21.cloned.1.call-start = ((), (), s32[]{:S(2)}) async-start(), calls=%async_computation.19 | async-start | bytes 1966080 | tf_op jit(solution)/shard_map/reduce_scatter | solution.py:74
  1365.6 76.2 %all-gather.47.cloned.1.call-start = ((), (), s32[]{:S(2)}) async-start(), calls=%async_computation.24 | async-start | bytes 1966080 | tf_op jit(solution)/shard_map/all_gather | solution.py:70
  1415.9 62.8 %reduce-scatter.27.cloned.1.call-start = ((), (), s32[]{:S(2)}) async-start(), calls=%async_computation.25 | async-start | bytes 1966080 | tf_op jit(solution)/shard_map/reduce_scatter | solution.py:87
  1450.5 28.2 copy-start.88
  1453.5 29.5 %copy-start.79 = (f32[2,2,512]{2,1,0:T(2,128)S(1)}, f32[2,2,512]{2,1,0:T(2,128)}, u32[]{:S(2)}) copy-start(f32[2,2,512]{2,1,0:T(2,128)} %copy-done.78) | copy-start | bytes 24580
  1453.5 29.5 %copy-start.81 = (f32[2,2,512]{2,1,0:T(2,128)S(1)}, f32[2,2,512]{2,1,0:T(2,128)}, u32[]{:S(2)}) copy-start(f32[2,2,512]{2,1,0:T(2,128)} %copy-done.80) | copy-start | bytes 24580
  1453.6 55.1 %all-gather.49.cloned.1.call-start = ((), (), s32[]{:S(2)}) async-start(), calls=%async_computation.26 | async-start | bytes 1966080 | tf_op jit(solution)/shard_map/all_gather | solution.py:70
  1480.7 30.6 %copy-start.95 = (f32[128]{0:T(128)}, f32[128]{0:T(128)S(1)}, u32[]{:S(2)}) copy-start(f32[128]{0:T(128)S(1)} %broadcast_multiply_fusion.1) | copy-start | bytes 1540
  1482.8 66.7 %reduce-scatter.29.cloned.1.call-start = ((), (), s32[]{:S(2)}) async-start(), calls=%async_computation.27 | async-start | bytes 1966080 | tf_op jit(solution)/shard_map/reduce_scatter | solution.py:87
  1524.4 264.1 %reduce-scatter.37.cloned.1.call-start = ((), (), s32[]{:S(2)}) async-start(), calls=%async_computation.41 | async-start | bytes 405504
  1566.3 451.2 %reduce-scatter.31.cloned.1.call-start = ((), (), s32[]{:S(2)}) async-start(), calls=%async_computation.28 | async-start | bytes 2433024 | tf_op jit(solution)/shard_map/reduce_scatter | solution.py:393
  1569.7 683.5 %reduce-scatter.35.cloned.1.call-start = ((), (), s32[]{:S(2)}) async-start(), calls=%async_computation.30 | async-start | bytes 6488064 | tf_op jit(solution)/shard_map/reduce_scatter | solution.py:408
  1578.7 909.9 %reduce-scatter.33.cloned.1.call-start = ((), (), s32[]{:S(2)}) async-start(), calls=%async_computation.29 | async-start | bytes 6488064 | tf_op jit(solution)/shard_map/reduce_scatter | solution.py:405
  1587.6 1305.4 %all-reduce.8.cloned.1.call-start = ((), (), s32[]{:S(2)}) async-start(), calls=%async_computation.42 | async-start | bytes 23592960
  (98 other events, 382.6 us)
Sparse Core Ops, SparseCore 0:
  137.0 20.6 all-gather.34
  161.4 67.9 all-gather.50
  233.0 65.4 all-gather.52
  345.5 18.8 reduce-scatter.14
  367.7 78.3 all-gather.54
  448.2 21.5 all-gather.36
  473.3 78.3 all-gather.56
  555.2 74.0 all-gather.58
  634.6 22.0 reduce-scatter.16
  757.5 22.0 all-gather.38
  783.2 68.6 all-gather.60
  854.8 65.1 all-gather.62
  968.5 20.0 reduce-scatter.18
  992.0 78.3 all-gather.66
  1072.5 21.5 all-gather.40
  1097.4 78.3 all-gather.64
  1177.3 21.5 all-gather.42
  1201.7 78.3 all-gather.68
  1293.1 20.7 reduce-scatter.22
  1318.7 25.7 all-gather.44
  1360.3 24.9 reduce-scatter.24
  1387.8 24.9 reduce-scatter.20
  1416.0 25.7 all-gather.46
  1453.7 24.9 reduce-scatter.26
  1482.9 25.7 all-gather.48
  1524.5 24.9 reduce-scatter.28
  1566.5 221.9 reduce-scatter.36
  1794.1 223.3 reduce-scatter.30
  2023.5 229.7 reduce-scatter.34
  2259.0 229.5 reduce-scatter.32
  2491.6 401.2 all-reduce.7
where the time goes:
time: 2920 us; the launch traced here: 2910 us
  waiting for transfers between devices  1990 us (68%)
  blocking collectives  592 us (20%)
  matrix products  131 us (4%)
  local copies, waits for them, and re-layouts  108 us (4%)
  other arithmetic  60.4 us (2%)
    unnamed x33, waiting for transfers between devices  552 us
    reduce_scatter x1, waiting for transfers between devices, body(): lax.psum_scatter(stacked[5].astype(jnp.bfloat16), 'dp', scatter_dimension...  234 us
    reduce_scatter x1, waiting for transfers between devices, body(): lax.psum_scatter(stacked[4].astype(jnp.bfloat16), 'dp', scatter_dimension...  234 us
    reduce_scatter x1, waiting for transfers between devices, body(): lax.psum_scatter(stacked[0].astype(jnp.bfloat16), 'dp', scatter_dimension...  228 us
    all_gather x2, blocking collectives, fetch_weights(): lax.all_gather(shards[7], 'dp', axis=1, tiled=True)  195 us
    all_gather x2, blocking collectives, fetch_weights(): lax.all_gather(shards[2], 'dp', axis=0, tiled=True)  194 us
    all_gather x2, blocking collectives, fetch_weights(): lax.all_gather(shards[1], 'dp', axis=0, tiled=True)  193 us
    all_gather x2, waiting for transfers between devices, fetch_weights(): lax.all_gather(shards[4], 'dp', axis=0, tiled=True)  153 us
  transfers between devices with their start and end apart: 31, of which 24 were waited for; matrix products, arithmetic and copies ran while one was open for 6% of the time, Pallas kernels for 0%

commit v1 on v0

--- a/solution.py
+++ b/solution.py
@@ -1,11 +1,533 @@
+import functools
 import math
 
 import jax
 import jax.numpy as jnp
 from jax import lax
+from jax.experimental import pallas as pl
+from jax.experimental.pallas import tpu as pltpu
 from jax.sharding import PartitionSpec as P
 
 HD = 96
+MESH_IDS = pl.DeviceIdType.MESH
+SIDE = 4
+
+
+COLS = (384, 192, 192, 384, 1024, 1024, 1024)
+WIDTH = 4224
+HALVES = (((0, 1024), (1024, 2048)), ((2048, 3072), (3072, 4224)))
+
+
+def here():
+    dp = lax.axis_index("dp")
+    tensor = lax.axis_index("tensor")
+    return dp // 16, (dp // 4) % 4, dp % 4, tensor
+
+
+def device(z_hi, x, y, tensor):
+    return (z_hi * 16 + x * 4 + y, tensor)
+
+
+def shift(place, step):
+    return lax.rem(place + step + 2 * SIDE, SIDE)
+
+
+def greet(targets):
+    barrier = pltpu.get_barrier_semaphore()
+    for target in targets:
+        pl.semaphore_signal(barrier, inc=1, device_id=target, device_id_type=MESH_IDS)
+    pl.semaphore_wait(barrier, len(targets))
+
+
+class Wire:
+    def __init__(self, send_sems, recv_sems):
+        self.send_sems, self.recv_sems = send_sems, recv_sems
+        self.count = 0
+        self.sent = []
+
+    def slot(self):
+        self.count += 1
+        return self.count - 1
+
+    def send(self, slot, source, target_ref, target):
+        copy = pltpu.make_async_remote_copy(
+            src_ref=source,
+            dst_ref=target_ref,
+            send_sem=self.send_sems.at[slot],
+            recv_sem=self.recv_sems.at[slot],
+            device_id=target,
+            device_id_type=MESH_IDS,
+        )
+        copy.start()
+        self.sent.append(copy)
+
+    def arrive(self, slot, landed, target):
+        pltpu.make_async_remote_copy(
+            src_ref=landed,
+            dst_ref=landed,
+            send_sem=self.send_sems.at[slot],
+            recv_sem=self.recv_sems.at[slot],
+            device_id=target,
+            device_id_type=MESH_IDS,
+        ).wait_recv()
+
+    def drain(self):
+        for copy in self.sent:
+            copy.wait_send()
+        self.sent = []
+
+
+class Place:
+    def __init__(self):
+        self.z_hi, self.x, self.y, self.tensor = here()
+
+    def beside(self, axis, step):
+        if axis == "x":
+            return device(self.z_hi, shift(self.x, step), self.y, self.tensor)
+        return device(self.z_hi, self.x, shift(self.y, step), self.tensor)
+
+    def across(self):
+        return device(1 - self.z_hi, self.x, self.y, self.tensor)
+
+    def greeted(self):
+        return [
+            self.beside("x", 1),
+            self.beside("x", -1),
+            self.beside("y", 1),
+            self.beside("y", -1),
+            self.across(),
+        ]
+
+
+def gather_job(wire, at, full, layer, z_data, own):
+    parts = []
+    for first, second, (left, right) in (("y", "x", HALVES[0]), ("x", "y", HALVES[1])):
+
+        def block(first_step, second_step, cols, first=first):
+            steps = {first: first_step}
+            steps["x" if first == "y" else "y"] = second_step
+            return full.at[
+                layer,
+                z_data,
+                shift(at.x, steps["x"]),
+                shift(at.y, steps["y"]),
+                :,
+                pl.ds(cols[0], cols[1] - cols[0]),
+            ]
+
+        def source(first_step, second_step, cols, block=block):
+            if own is not None and first_step == 0 and second_step == 0:
+                return own.at[layer, :, pl.ds(cols[0], cols[1] - cols[0])]
+            return block(first_step, second_step, cols)
+
+        parts.append(
+            dict(
+                first=first,
+                second=second,
+                left=left,
+                right=right,
+                whole=(left[0], right[1]),
+                block=block,
+                source=source,
+                one={s: wire.slot() for s in (1, -1)},
+                two={s: wire.slot() for s in (1, -1)},
+                side={(f, s): wire.slot() for f in (0, -1, 1, 2) for s in (1, -1)},
+                far={(f, s): wire.slot() for f in (0, -1, 1, 2) for s in (1, -1)},
+            )
+        )
+
+    def one_start(part, step):
+        wire.send(
+            part["one"][step],
+            part["source"](0, 0, part["whole"]),
+            part["block"](0, 0, part["whole"]),
+            at.beside(part["first"], step),
+        )
+
+    def side_start(part, first_step):
+        for step in (1, -1):
+            wire.send(
+                part["side"][first_step, step],
+                part["source"](first_step, 0, part["whole"]),
+                part["block"](first_step, 0, part["whole"]),
+                at.beside(part["second"], step),
+            )
+
+    def half(part, step):
+        return part["left"] if step == 1 else part["right"]
+
+    def one_done(part, step):
+        target = at.beside(part["first"], step)
+        wire.arrive(part["one"][step], part["block"](-step, 0, part["whole"]), target)
+        piece = part["block"](-step, 0, half(part, step))
+        wire.send(part["two"][step], piece, piece, target)
+
+    def two_done(part):
+        for step in (1, -1):
+            piece = part["block"](2, 0, half(part, step))
+            wire.arrive(part["two"][step], piece, at.beside(part["first"], step))
+
+    def side_done(part, first_step):
+        for step in (1, -1):
+            target = at.beside(part["second"], step)
+            wire.arrive(
+                part["side"][first_step, step],
+                part["block"](first_step, -step, part["whole"]),
+                target,
+            )
+            piece = part["block"](first_step, -step, half(part, step))
+            wire.send(part["far"][first_step, step], piece, piece, target)
+
+    def far_done(part, first_step):
+        for step in (1, -1):
+            piece = part["block"](first_step, 2, half(part, step))
+            wire.arrive(part["far"][first_step, step], piece, at.beside(part["second"], step))
+
+    for part in parts:
+        for step in (1, -1):
+            one_start(part, step)
+    for part in parts:
+        side_start(part, 0)
+    yield
+    for step in (1, -1):
+        for part in parts:
+            one_done(part, step)
+    for first_step in (-1, 1):
+        for part in parts:
+            side_start(part, first_step)
+    yield
+    for part in parts:
+        two_done(part)
+    for part in parts:
+        side_start(part, 2)
+    for part in parts:
+        side_done(part, 0)
+    yield
+    for first_step in (-1, 1):
+        for part in parts:
+            side_done(part, first_step)
+    yield
+    for part in parts:
+        side_done(part, 2)
+    yield
+    for first_step in (0, -1, 1, 2):
+        for part in parts:
+            far_done(part, first_step)
+    yield
+
+
+def gather_kernel(shard, full, send_sems, recv_sems, own_sem):
+    at = Place()
+    greet(at.greeted())
+    wire = Wire(send_sems, recv_sems)
+    layers = shard.shape[0]
+    own_copies = [
+        pltpu.make_async_copy(
+            shard.at[layer], full.at[layer, at.z_hi, at.x, at.y], own_sem.at[layer]
+        )
+        for layer in range(layers)
+    ]
+    for copy in own_copies:
+        copy.start()
+    across = [wire.slot() for _ in range(layers)]
+    jobs = []
+    for layer in range(layers):
+        jobs.append((layer, gather_job(wire, at, full, layer, at.z_hi, shard)))
+        jobs.append((layer, gather_job(wire, at, full, layer, 1 - at.z_hi, None)))
+    for layer in range(layers):
+        wire.send(
+            across[layer], shard.at[layer], full.at[layer, at.z_hi, at.x, at.y], at.across()
+        )
+
+    def advance(index):
+        if index < len(jobs):
+            next(jobs[index][1])
+
+    def begin(index):
+        if index < len(jobs):
+            layer = jobs[index][0]
+            if index % 2:
+                wire.arrive(
+                    across[layer], full.at[layer, 1 - at.z_hi, at.x, at.y], at.across()
+                )
+            advance(index)
+
+    begin(0)
+    advance(0)
+    for index in range(len(jobs)):
+        advance(index)
+        begin(index + 1)
+        advance(index)
+        advance(index)
+        advance(index + 1)
+        advance(index)
+    for copy in own_copies:
+        copy.wait()
+    wire.drain()
+
+
+def gather_weights(shard):
+    layers = shard.shape[0]
+    slots = layers * 81
+    return pl.pallas_call(
+        gather_kernel,
+        out_shape=jax.ShapeDtypeStruct((layers, 2, SIDE, SIDE, 48, WIDTH), jnp.bfloat16),
+        in_specs=[pl.BlockSpec(memory_space=pl.ANY)],
+        out_specs=pl.BlockSpec(memory_space=pl.ANY),
+        scratch_shapes=[
+            pltpu.SemaphoreType.DMA((slots,)),
+            pltpu.SemaphoreType.DMA((slots,)),
+            pltpu.SemaphoreType.DMA((layers,)),
+        ],
+        compiler_params=pltpu.CompilerParams(collective_id=0, has_side_effects=True),
+        name="gather_weights",
+    )(shard)
+
+
+def add_into(target, terms, rows_lead):
+    def step(index, carry):
+        lead, start = index // 3, pl.multiple_of((index % 3) * 16, 16)
+        window = (lead, pl.ds(start, 16)) if rows_lead else (pl.ds(start, 16),)
+        total = None
+        for term in terms:
+            value = term[window].astype(jnp.float32)
+            total = value if total is None else total + value
+        target[window] = total.astype(target.dtype)
+        return carry
+
+    lax.fori_loop(0, 3 * (SIDE if rows_lead else 1), step, 0)
+
+
+def scatter_job(wire, at, grads, layer, z_data, job, bufs, finish):
+    one, two_up, two_down, small_one, small_up, small_down = bufs
+
+    def cut(cols):
+        return pl.ds(cols[0], cols[1] - cols[0])
+
+    parts = []
+    for first, second, (left, right) in (("y", "x", HALVES[0]), ("x", "y", HALVES[1])):
+
+        def region(step, cols, second=second):
+            if second == "x":
+                return grads.at[layer, z_data, shift(at.x, step), :, :, cut(cols)]
+            return grads.at[layer, z_data, :, shift(at.y, step), :, cut(cols)]
+
+        def mine(step, cols, first=first):
+            place = at.y if first == "y" else at.x
+            return two_up.at[job, shift(place, step), :, cut(cols)]
+
+        parts.append(
+            dict(
+                first=first,
+                second=second,
+                left=left,
+                right=right,
+                whole=(left[0], right[1]),
+                region=region,
+                mine=mine,
+                far={s: wire.slot() for s in (1, -1)},
+                raw={s: wire.slot() for s in (1, -1)},
+                sum={s: wire.slot() for s in (1, -1)},
+                far2={s: wire.slot() for s in (1, -1)},
+                raw2={s: wire.slot() for s in (1, -1)},
+                sum2={s: wire.slot() for s in (1, -1)},
+            )
+        )
+
+    def half(part, step):
+        return part["left"] if step == 1 else part["right"]
+
+    def other(part, step):
+        return part["right"] if step == 1 else part["left"]
+
+    def landing(step):
+        return two_up if step == 1 else two_down
+
+    def small_landing(step):
+        return small_up if step == 1 else small_down
+
+    for part in parts:
+        for step in (1, -1):
+            cols = half(part, step)
+            wire.send(
+                part["far"][step],
+                part["region"](2, cols),
+                one.at[job, :, :, cut(cols)],
+                at.beside(part["second"], step),
+            )
+    for part in parts:
+        for step in (1, -1):
+            cols = other(part, step)
+            wire.send(
+                part["raw"][step],
+                part["region"](step, cols),
+                landing(step).at[job, :, :, cut(cols)],
+                at.beside(part["second"], step),
+            )
+    yield
+    for step in (1, -1):
+        for part in parts:
+            cols = half(part, step)
+            target = at.beside(part["second"], step)
+            piece = one.at[job, :, :, cut(cols)]
+            wire.arrive(part["far"][step], piece, target)
+            add_into(piece, (piece, part["region"](step, cols)), True)
+            wire.send(part["sum"][step], piece, landing(step).at[job, :, :, cut(cols)], target)
+    yield
+    for part in parts:
+        for step in (1, -1):
+            target = at.beside(part["second"], step)
+            cols = other(part, step)
+            wire.arrive(part["raw"][step], landing(step).at[job, :, :, cut(cols)], target)
+            cols = half(part, step)
+            wire.arrive(part["sum"][step], landing(step).at[job, :, :, cut(cols)], target)
+        cols = part["whole"]
+        piece = two_up.at[job, :, :, cut(cols)]
+        add_into(
+            piece,
+            (part["region"](0, cols), piece, two_down.at[job, :, :, cut(cols)]),
+            True,
+        )
+        for step in (1, -1):
+            cols = half(part, step)
+            target = at.beside(part["first"], step)
+            wire.send(
+                part["far2"][step], part["mine"](2, cols), small_one.at[job, :, cut(cols)], target
+            )
+            cols = other(part, step)
+            wire.send(
+                part["raw2"][step],
+                part["mine"](step, cols),
+                small_landing(step).at[job, :, cut(cols)],
+                target,
+            )
+    yield
+    for step in (1, -1):
+        for part in parts:
+            cols = half(part, step)
+            target = at.beside(part["first"], step)
+            piece = small_one.at[job, :, cut(cols)]
+            wire.arrive(part["far2"][step], piece, target)
+            add_into(piece, (piece, part["mine"](step, cols)), False)
+            wire.send(
+                part["sum2"][step], piece, small_landing(step).at[job, :, cut(cols)], target
+            )
+    yield
+    for part in parts:
+        for step in (1, -1):
+            target = at.beside(part["first"], step)
+            cols = other(part, step)
+            wire.arrive(part["raw2"][step], small_landing(step).at[job, :, cut(cols)], target)
+            cols = half(part, step)
+            wire.arrive(part["sum2"][step], small_landing(step).at[job, :, cut(cols)], target)
+        cols = part["whole"]
+        finish(
+            cut(cols),
+            (
+                part["mine"](0, cols),
+                small_up.at[job, :, cut(cols)],
+                small_down.at[job, :, cut(cols)],
+            ),
+        )
+    yield
+
+
+def scatter_kernel(
+    grads,
+    out,
+    one,
+    two_up,
+    two_down,
+    small_one,
+    small_up,
+    small_down,
+    leaving,
+    landed,
+    send_sems,
+    recv_sems,
+):
+    at = Place()
+    greet(at.greeted())
+    wire = Wire(send_sems, recv_sems)
+    layers = grads.shape[0]
+    bufs = (one, two_up, two_down, small_one, small_up, small_down)
+    jobs = []
+    for layer in range(layers):
+        across = [wire.slot() for _ in range(2)]
+        places = (pl.ds(0, 2048), pl.ds(2048, WIDTH - 2048))
+        turn = iter(range(2))
+
+        def finish_other(cols, terms, layer=layer, across=across, turn=turn):
+            piece = leaving.at[layer, :, cols]
+            add_into(piece, terms, False)
+            wire.send(
+                across[next(turn)], piece, landed.at[layer, :, cols], at.across()
+            )
+
+        turn_own = iter(range(2))
+
+        def finish_own(cols, terms, layer=layer, across=across, turn=turn_own):
+            piece = landed.at[layer, :, cols]
+            wire.arrive(across[next(turn)], piece, at.across())
+            add_into(out.at[layer, :, cols], terms + (piece,), False)
+
+        jobs.append(
+            scatter_job(
+                wire, at, grads, layer, 1 - at.z_hi, 2 * layer, bufs, finish_other
+            )
+        )
+        jobs.append(
+            scatter_job(wire, at, grads, layer, at.z_hi, 2 * layer + 1, bufs, finish_own)
+        )
+
+    def advance(index):
+        if index < len(jobs):
+            next(jobs[index])
+
+    advance(0)
+    advance(0)
+    for index in range(len(jobs)):
+        advance(index + 1)
+        advance(index)
+        advance(index)
+        advance(index + 1)
+        advance(index)
+    wire.drain()
+
+
+def scatter_grads(grads):
+    layers = grads.shape[0]
+    slots = layers * 50
+    jobs = 2 * layers
+    return pl.pallas_call(
+        scatter_kernel,
+        out_shape=jax.ShapeDtypeStruct((layers, 48, WIDTH), jnp.float32),
+        in_specs=[pl.BlockSpec(memory_space=pltpu.VMEM)],
+        out_specs=pl.BlockSpec(memory_space=pltpu.VMEM),
+        scratch_shapes=[
+            pltpu.VMEM((jobs, SIDE, 48, WIDTH), jnp.bfloat16),
+            pltpu.VMEM((jobs, SIDE, 48, WIDTH), jnp.bfloat16),
+            pltpu.VMEM((jobs, SIDE, 48, WIDTH), jnp.bfloat16),
+            pltpu.VMEM((jobs, 48, WIDTH), jnp.bfloat16),
+            pltpu.VMEM((jobs, 48, WIDTH), jnp.bfloat16),
+            pltpu.VMEM((jobs, 48, WIDTH), jnp.bfloat16),
+            pltpu.VMEM((layers, 48, WIDTH), jnp.bfloat16),
+            pltpu.VMEM((layers, 48, WIDTH), jnp.bfloat16),
+            pltpu.SemaphoreType.DMA((slots,)),
+            pltpu.SemaphoreType.DMA((slots,)),
+        ],
+        compiler_params=pltpu.CompilerParams(
+            collective_id=1, has_side_effects=True, vmem_limit_bytes=60 * 2**20
+        ),
+        name="scatter_grads",
+    )(grads)
+
+
+def pack_rows(arrays):
+    query, key, value, out, gate, up, down = arrays
+    turned_out = jnp.swapaxes(out, 1, 2)
+    turned_down = jnp.swapaxes(down, 1, 2)
+    return jnp.concatenate([query, key, value, turned_out, gate, up, turned_down], axis=2)
 
 
 norm_eps = 1e-05
@@ -87,32 +609,6 @@
     return lax.psum_scatter(
         summed.astype(jnp.bfloat16), "tensor", scatter_dimension=0, tiled=True
     ).astype(jnp.float32)
-
-
-def fetch_weights(shards):
-    return (
-        lax.all_gather(shards[0], "dp", axis=0, tiled=True),
-        lax.all_gather(shards[1], "dp", axis=0, tiled=True),
-        lax.all_gather(shards[2], "dp", axis=0, tiled=True),
-        lax.all_gather(shards[3], "dp", axis=1, tiled=True),
-        lax.all_gather(shards[4], "dp", axis=0, tiled=True),
-        lax.all_gather(shards[5], "dp", axis=0, tiled=True),
-        lax.all_gather(shards[6], "dp", axis=1, tiled=True),
-        lax.all_gather(shards[7], "dp", axis=1, tiled=True),
-    )
-
-
-def fetch_again(shards):
-    return (
-        lax.all_gather(shards[0], "dp", axis=0, tiled=True),
-        lax.all_gather(shards[1], "dp", axis=0, tiled=True),
-        lax.all_gather(shards[2], "dp", axis=0, tiled=True),
-        lax.all_gather(shards[3], "dp", axis=1, tiled=True),
-        lax.all_gather(shards[4], "dp", axis=0, tiled=True),
-        lax.all_gather(shards[5], "dp", axis=0, tiled=True),
-        lax.all_gather(shards[6], "dp", axis=1, tiled=True),
-        lax.all_gather(shards[7], "dp", axis=1, tiled=True),
-    )
 
 
 def norm_forward(rows_in, gain):
@@ -231,22 +727,25 @@
     scaling = 1.0 / math.sqrt(HD)
     seq_rows = local_rows * lax.axis_size("tensor")
     cosine_table, sine_table = rope_tables(seq_rows, HD)
-    arrays = (
-        query_weight,
-        key_weight,
-        value_weight,
-        out_weight,
-        gate_weight,
-        up_weight,
-        down_weight,
-        norm_gains,
-    )
+    packed = pack_rows(
+        (query_weight, key_weight, value_weight, out_weight, gate_weight, up_weight, down_weight)
+    )
+    gathered = gather_weights(packed).reshape(layers, -1, WIDTH)
+    all_gains = lax.all_gather(norm_gains, "dp", axis=2, tiled=True)
+
+    def unpack(layer_index):
+        pieces, start = [], 0
+        for width in COLS:
+            pieces.append(gathered[layer_index, :, start : start + width])
+            start += width
+        query, key, value, out, gate, up, down = pieces
+        return (query, key, value, out.T, gate, up, down.T, all_gains[layer_index])
+
     residual = tokens.astype(jnp.float32)
     saved = []
     kept_weights = []
     for layer_index in range(layers):
-        shards = tuple((array[layer_index] for array in arrays))
-        weights = fetch_weights(shards)
+        weights = unpack(layer_index)
         query_full, key_full, value_full, out_full, gate_full, up_full, down_full, gain_full = (
             weights
         )
@@ -319,14 +818,14 @@
             upward,
             hidden,
         ) = saved[layer_index]
-        weights = fetch_again(tuple((array[layer_index] for array in arrays)))
+        weights = unpack(layer_index)
         query_full, key_full, value_full, out_full, gate_full, up_full, down_full, gain_full = (
             weights
         )
         gain_values = gain_full.astype(jnp.float32)
         grad_rows_mlp = gather_grads(grad_residual.astype(jnp.bfloat16))
         grad_hidden = times_transpose(grad_rows_mlp, down_full)
-        grad_down = contract_rows(hidden, grad_rows_mlp)
+        grad_down = contract_rows(grad_rows_mlp, hidden)
         sigma = jax.nn.sigmoid(gate_rows)
         grad_gate_rows = (grad_hidden * upward * sigma * (1.0 + gate_rows * (1.0 - sigma))).astype(
             jnp.bfloat16
@@ -341,7 +840,7 @@
         grad_middle = grad_residual + grad_norm_second
         grad_rows_attn = gather_grads(grad_middle.astype(jnp.bfloat16))
         grad_attended = times_transpose(grad_rows_attn, out_full).astype(jnp.bfloat16)
-        grad_out_proj = contract_rows(attended_low, grad_rows_attn)
+        grad_out_proj = contract_rows(grad_rows_attn, attended_low)
         grad_query_turned, grad_key_turned, grad_value_rows = attend_back(
             query_turned,
             key_turned,
@@ -383,49 +882,35 @@
             gain_sums,
         )
         layer_results[layer_index] = layer_grads
-    stacked = tuple(
-        (
-            jnp.stack([layer_results[layer_index][kind_index] for layer_index in range(layers)])
-            for kind_index in range(8)
-        )
-    )
-    reduced = (
-        lax.psum_scatter(
-            stacked[0].astype(jnp.bfloat16), "dp", scatter_dimension=1, tiled=True
-        ).astype(jnp.float32),
-        lax.psum_scatter(
-            stacked[1].astype(jnp.bfloat16), "dp", scatter_dimension=1, tiled=True
-        ).astype(jnp.float32),
-        lax.psum_scatter(
-            stacked[2].astype(jnp.bfloat16), "dp", scatter_dimension=1, tiled=True
-        ).astype(jnp.float32),
-        lax.psum_scatter(
-            stacked[3].astype(jnp.bfloat16), "dp", scatter_dimension=2, tiled=True
-        ).astype(jnp.float32),
-        lax.psum_scatter(
-            stacked[4].astype(jnp.bfloat16), "dp", scatter_dimension=1, tiled=True
-        ).astype(jnp.float32),
-        lax.psum_scatter(
-            stacked[5].astype(jnp.bfloat16), "dp", scatter_dimension=1, tiled=True
-        ).astype(jnp.float32),
-        lax.psum_scatter(
-            stacked[6].astype(jnp.bfloat16), "dp", scatter_dimension=2, tiled=True
-        ).astype(jnp.float32),
-        lax.psum_scatter(
-            stacked[7].astype(jnp.bfloat16), "dp", scatter_dimension=2, tiled=True
-        ).astype(jnp.float32),
-    )
+    grads = jnp.stack(
+        [
+            jnp.concatenate([part.astype(jnp.bfloat16) for part in layer_results[layer_index][:7]], axis=1)
+            for layer_index in range(layers)
+        ]
+    ).reshape(layers, 2, SIDE, SIDE, 48, WIDTH)
+    summed = scatter_grads(grads)
+    gains_summed = lax.psum_scatter(
+        jnp.stack([layer_results[layer_index][7] for layer_index in range(layers)]),
+        "dp",
+        scatter_dimension=2,
+        tiled=True,
+    )
+    pieces, start = [], 0
+    for width in COLS:
+        pieces.append(summed[:, :, start : start + width])
+        start += width
+    query, key, value, out, gate, up, down = pieces
     return (
         output,
         grad_residual,
-        reduced[0],
-        reduced[1],
-        reduced[2],
-        reduced[3],
-        reduced[4],
-        reduced[5],
-        reduced[6],
-        reduced[7],
+        query,
+        key,
+        value,
+        jnp.swapaxes(out, 1, 2),
+        gate,
+        up,
+        jnp.swapaxes(down, 1, 2),
+        gains_summed,
     )
 
 

time: 2920 us -> 1250 us (0.43)
  waiting for transfers between devices: 1990 us -> 507 us
  blocking collectives: 592 us -> 110 us
  Pallas kernels: 0 us -> 285 us
    reduce_scatter x3 -> x0, waiting for transfers between devices: 695 us -> none  [the longest x1 234 us: body(): lax.psum_scatter(stacked[5].astype(jnp.bfloat16), 'dp', scatter_dimension...]
    all_gather x6 -> x1, blocking collectives: 582 us -> 100 us  [body(): all_gains = lax.all_gather(norm_gains, 'dp', axis=2, tiled=True)]
    all_gather x10 -> x0, waiting for transfers between devices: 459 us -> none  [the longest x2 153 us: fetch_weights(): lax.all_gather(shards[4], 'dp', axis=0, tiled=True)]
    unnamed x33 -> x18, waiting for transfers between devices: 552 us -> 219 us
    pallas_call x0 -> x2, Pallas kernels: none -> 285 us  [the longest x1 157 us: scatter_grads(): pl.pallas_call(scatter_kernel, out_shape=jax.ShapeDtypeStruct((layers, 48...]
    concatenate x0 -> x3, local copies, waits for them, and re-layouts: none -> 35.5 us  [the longest x2 34.4 us: body(): jnp.concatenate([part.astype(jnp.bfloat16) for part in layer_results[laye...]
    another operation x4 -> x0, local copies, waits for them, and re-layouts: 31 us -> none  [body(): jnp.stack([layer_results[layer_index][kind_index] for layer_index in rang...]
  transfers between devices with their start and end apart: 31 -> 17, of which waited for: 24 -> 14; matrix products, arithmetic and copies ran while one was open for 6% -> 13% of each run, Pallas kernels for 0% -> 23%
where the time goes in v1:
time: 1250 us; the launch traced here: 1240 us
  waiting for transfers between devices  507 us (41%)
  Pallas kernels  285 us (23%)
  matrix products  155 us (12%)
  local copies, waits for them, and re-layouts  113 us (9%)
  blocking collectives  110 us (9%)
  other arithmetic  52.8 us (4%)
  between operations  15.5 us (1%)
    unnamed x18, waiting for transfers between devices  219 us
    pallas_call x1, Pallas kernels, scatter_grads(): pl.pallas_call(scatter_kernel, out_shape=jax.ShapeDtypeStruct((layers, 48...  157 us
    pallas_call x1, Pallas kernels, gather_weights(): pl.pallas_call(gather_kernel, out_shape=jax.ShapeDtypeStruct((layers, 2,...  127 us
    all_gather x1, blocking collectives, body(): all_gains = lax.all_gather(norm_gains, 'dp', axis=2, tiled=True)  100 us
    all_gather x4, waiting for transfers between devices, gather_grads(): return lax.all_gather(gradient, 'tensor', axis=0, tiled=True)  75.4 us
    reduce_scatter x4, waiting for transfers between devices, branch_sum(): lax.psum_scatter(jnp.dot(left_rows, weight, preferred_element_type=jnp.fl...  71.6 us
    all_gather x4, waiting for transfers between devices, gather_rows(): return lax.all_gather(normed, 'tensor', axis=0, tiled=True)  70.8 us
    reduce_scatter x4, waiting for transfers between devices, input_sum(): lax.psum_scatter(summed.astype(jnp.bfloat16), 'tensor', scatter_dimension...  69.9 us
  transfers between devices with their start and end apart: 17, of which 14 were waited for; matrix products, arithmetic and copies ran while one was open for 13% of the time, Pallas kernels for 23%

profile of v1, /device:TPU:0, one launch (start us, length us, event | category | flops | bytes accessed | tf_op | source)
XLA Modules:
  0.0 1241.3 jit_solution(12443682963359801640)
XLA Ops:
  8.1 100.1 %all_gather.27 = bf16[2,2,1536]{1,0,2:T(2,128)(2,1)S(1)} all-gather(bf16[2,2,48]{1,0,2:T(2,128)(2,1)S(1)} %copy.51), channel_id=1, replica_groups=mesh['dp'=32,'tensor'=4] {'dp'}, dimensions={2}, use_global_device_ids=true | all-gather | bytes 12672 | tf_op jit(solution)/shard_map/all_gather | solution.py:734
  109.4 25.1 %slice_reduce_fusion.2 = (f32[1536]{0:T(1024)S(1)}, f32[1536]{0:T(1024)S(1)}) fusion(f32[1,2,1536]{1,0,2:T(1,128)S(1)} %get-tuple-element.143), kind=kLoop, calls=%fused_computation.179 | loop fusion | bytes 24576 | tf_op jit(solution)/shard_map/slice | solution.py:775
  137.0 127.3 %gather_weights.1 = bf16[2,2,4,4,48,4224]{5,4,3,2,1,0:T(8,128)(2,1)} custom-call(bf16[2,48,4224]{2,1,0:T(8,128)(2,1)} %concatenate.48.shard), custom_call_target="tpu_custom_call" | custom-call | tf_op jit(solution)/shard_map/gather_weights/pallas_call | solution.py:272
  283.7 3.6 convolution_convert_fusion.9
  287.4 22.1 %reduce-scatter.12.cloned.1.call-done = bf16[128,1536]{1,0:T(8,128)(2,1)} async-done(((bf16[512,1536]{1,0:T(8,128)(2,1)}), bf16[128,1536]{1,0:T(8,128)(2,1)}) %reduce-scatter.12.cloned.1.call-update) | async-done | bytes 393232 | tf_op jit(solution)/shard_map/reduce_scatter | solution.py:596
  312.8 25.7 %all-gather.11.cloned.1.call-done = bf16[512,1536]{1,0:T(8,128)(2,1)} async-done(((bf16[128,1536]{1,0:T(8,128)(2,1)}), bf16[512,1536]{1,0:T(8,128)(2,1)}) %all-gather.11.cloned.1.call-update) | async-done | bytes 1572880 | tf_op jit(solution)/shard_map/all_gather | solution.py:588
  338.5 4.3 fusion.26
  342.8 5.9 multiply_convert_fusion.3
  349.7 4.9 convolution_convert_fusion.8
  354.7 24.8 %slice_reduce_fusion.1 = (f32[1536]{0:T(1024)S(1)}, f32[1536]{0:T(1024)S(1)}) fusion(f32[1,2,1536]{1,0,2:T(1,128)S(1)} %get-tuple-element.144), kind=kLoop, calls=%fused_computation.177 | loop fusion | bytes 24576 | tf_op jit(solution)/shard_map/slice | solution.py:753
  385.3 22.6 %all-gather.13.cloned.1.call-done = bf16[512,1536]{1,0:T(8,128)(2,1)} async-done(((bf16[128,1536]{1,0:T(8,128)(2,1)}), bf16[512,1536]{1,0:T(8,128)(2,1)}) %all-gather.13.cloned.1.call-update) | async-done | bytes 1572880 | tf_op jit(solution)/shard_map/all_gather | solution.py:588
  417.1 3.6 convolution_convert_fusion.7
  421.5 24.3 %reduce-scatter.16.cloned.1.call-done = bf16[128,1536]{1,0:T(8,128)(2,1)} async-done(((bf16[512,1536]{1,0:T(8,128)(2,1)}), bf16[128,1536]{1,0:T(8,128)(2,1)}) %reduce-scatter.16.cloned.1.call-update) | async-done | bytes 393232 | tf_op jit(solution)/shard_map/reduce_scatter | solution.py:596
  449.2 24.1 %all-gather.17.cloned.1.call-done = bf16[512,1536]{1,0:T(8,128)(2,1)} async-done(((bf16[128,1536]{1,0:T(8,128)(2,1)}), bf16[512,1536]{1,0:T(8,128)(2,1)}) %all-gather.17.cloned.1.call-update) | async-done | bytes 1572880 | tf_op jit(solution)/shard_map/all_gather | solution.py:592
  473.3 5.5 fusion.32
  478.8 22.5 %all-gather.15.cloned.1.call-done = bf16[512,1536]{1,0:T(8,128)(2,1)} async-done(((bf16[128,1536]{1,0:T(8,128)(2,1)}), bf16[512,1536]{1,0:T(8,128)(2,1)}) %all-gather.15.cloned.1.call-update) | async-done | bytes 1572880 | tf_op jit(solution)/shard_map/all_gather | solution.py:588
  501.4 4.3 fusion.31
  505.7 5.5 fusion.45
  511.2 4.5 fusion.29
  515.7 4.9 fusion.17
  520.7 25.1 %reduce-scatter.20.cloned.1.call-done = bf16[128,1536]{1,0:T(8,128)(2,1)} async-done(((bf16[512,1536]{1,0:T(8,128)(2,1)}), bf16[128,1536]{1,0:T(8,128)(2,1)}) %reduce-scatter.20.cloned.1.call-update) | async-done | bytes 393232 | tf_op jit(solution)/shard_map/reduce_scatter | solution.py:609
  550.1 25.6 %all-gather.19.cloned.1.call-done = bf16[512,1536]{1,0:T(8,128)(2,1)} async-done(((bf16[128,1536]{1,0:T(8,128)(2,1)}), bf16[512,1536]{1,0:T(8,128)(2,1)}) %all-gather.19.cloned.1.call-update) | async-done | bytes 1572880 | tf_op jit(solution)/shard_map/all_gather | solution.py:592
  578.3 3.3 fusion.3
  590.1 3.3 fusion.19
  593.5 5.2 convolution_convert_fusion.6
  598.8 19.8 %reduce-scatter.22.cloned.1.call-done = bf16[128,1536]{1,0:T(8,128)(2,1)} async-done(((bf16[512,1536]{1,0:T(8,128)(2,1)}), bf16[128,1536]{1,0:T(8,128)(2,1)}) %reduce-scatter.22.cloned.1.call-update) | async-done | bytes 393232 | tf_op jit(solution)/shard_map/reduce_scatter | solution.py:609
  621.0 24.8 %reduce-scatter.18.cloned.1.call-done = bf16[128,1536]{1,0:T(8,128)(2,1)} async-done(((bf16[512,1536]{1,0:T(8,128)(2,1)}), bf16[128,1536]{1,0:T(8,128)(2,1)}) %reduce-scatter.18.cloned.1.call-update) | async-done | bytes 393232 | tf_op jit(solution)/shard_map/reduce_scatter | solution.py:596
  648.9 25.6 %all-gather.21.cloned.1.call-done = bf16[512,1536]{1,0:T(8,128)(2,1)} async-done(((bf16[128,1536]{1,0:T(8,128)(2,1)}), bf16[512,1536]{1,0:T(8,128)(2,1)}) %all-gather.21.cloned.1.call-update) | async-done | bytes 1572880 | tf_op jit(solution)/shard_map/all_gather | solution.py:592
  674.5 5.9 multiply_convert_fusion
  680.4 4.5 fusion.25
  685.0 4.9 fusion.18
  690.0 25.0 %reduce-scatter.24.cloned.1.call-done = bf16[128,1536]{1,0:T(8,128)(2,1)} async-done(((bf16[512,1536]{1,0:T(8,128)(2,1)}), bf16[128,1536]{1,0:T(8,128)(2,1)}) %reduce-scatter.24.cloned.1.call-update) | async-done | bytes 393232 | tf_op jit(solution)/shard_map/reduce_scatter | solution.py:609
  719.6 3.3 fusion.23
  728.9 3.6 fusion.7
  732.5 3.5 fusion.6
  736.0 3.5 fusion.14
  739.5 18.0 %copy.66 = bf16[1536,4224]{1,0:T(8,128)(2,1)} copy(bf16[1536,4224]{0,1:T(8,128)(2,1)} %fusion.14) | data formatting | bytes 25952256 | tf_op jit(solution)/shard_map/concatenate | solution.py:887
  760.2 3.3 fusion
  771.8 3.3 fusion.20
  775.4 3.3 fusion.21
  784.8 3.5 fusion.10
  788.3 3.6 fusion.9
  791.9 3.6 fusion.8
  795.6 16.5 %copy.65 = bf16[1536,4224]{1,0:T(8,128)(2,1)} copy(bf16[1536,4224]{0,1:T(8,128)(2,1)} %fusion.8) | data formatting | bytes 25952256 | tf_op jit(solution)/shard_map/concatenate | solution.py:887
  812.0 21.1 %pad_maximum_fusion.grads = bf16[2,2,4,4,48,4224]{5,4,3,2,1,0:T(8,128)(2,1)} fusion(bf16[1,2,4,4,48,4224]{5,4,3,2,1,0:T(8,128)(2,1)} %bitcast.288, bf16[1,2,4,4,48,4224]{5,4,3,2,1,0:T(8,128)(2,1)} %bitcast.289), kind=kLoop, calls=%fused_computation | loop fusion | flops 12976128 | bytes 51904512 | tf_op jit(solution)/shard_map/stack | solution.py:885
  833.1 157.4 %scatter_grads.1 = f32[2,48,4224]{2,1,0:T(8,128)} custom-call(bf16[2,2,4,4,48,4224]{5,4,3,2,1,0:T(8,128)(2,1)} %pad_maximum_fusion.grads), custom_call_target="tpu_custom_call" | custom-call | tf_op jit(solution)/shard_map/scatter_grads/pallas_call | solution.py:502
  997.7 10.3 all-reduce
  1014.6 218.4 %reduce-scatter.28.cloned.1.call-done = f32[48,4]{1,0:T(8,128)} async-done(((f32[1536,4]{1,0:T(8,128)}), f32[48,4]{1,0:T(8,128)}) %reduce-scatter.28.cloned.1.call-update) | async-done | bytes 784
  (317 shorter events, 110.9 us)
Async XLA Ops:
  7.2 127.3 %copy-start.4 = (bf16[128,1536]{1,0:T(8,128)(2,1)S(1)}, bf16[128,1536]{1,0:T(8,128)(2,1)}, u32[]{:S(2)}) copy-start(bf16[128,1536]{1,0:T(8,128)(2,1)} %param.10) | copy-start | bytes 1179652
  7.2 267.2 %all-gather.9.cloned.1.call-start = ((), (), s32[]{:S(2)}) async-start(), calls=%async_computation.9 | async-start | bytes 1966080 | tf_op jit(solution)/shard_map/all_gather | solution.py:588
  108.2 27.7 %copy-start.35 = (bf16[2,48,1024]{2,1,0:T(8,128)(2,1)S(1)}, bf16[2,48,1024]{2,1,0:T(8,128)(2,1)}, u32[]{:S(2)}) copy-start(bf16[2,48,1024]{2,1,0:T(8,128)(2,1)} %param.15) | copy-start | bytes 589828
  108.2 27.7 %copy-start.36 = (bf16[2,48,1024]{2,1,0:T(8,128)(2,1)S(1)}, bf16[2,48,1024]{2,1,0:T(8,128)(2,1)}, u32[]{:S(2)}) copy-start(bf16[2,48,1024]{2,1,0:T(8,128)(2,1)} %param.16) | copy-start | bytes 589828
  108.2 27.7 %copy-start.37 = (bf16[2,1024,48]{1,2,0:T(8,128)(2,1)S(1)}, bf16[2,1024,48]{1,2,0:T(8,128)(2,1)}, u32[]{:S(2)}) copy-start(bf16[2,1024,48]{1,2,0:T(8,128)(2,1)} %param.17) | copy-start | bytes 589828
  108.2 27.7 %copy-start.46 = (bf16[2,48,384]{2,1,0:T(8,128)(2,1)S(1)}, bf16[2,48,384]{2,1,0:T(8,128)(2,1)}, u32[]{:S(2)}) copy-start(bf16[2,48,384]{2,1,0:T(8,128)(2,1)} %param.11) | copy-start | bytes 221188
  108.2 27.7 %copy-start.47 = (bf16[2,384,48]{1,2,0:T(8,128)(2,1)S(1)}, bf16[2,384,48]{1,2,0:T(8,128)(2,1)}, u32[]{:S(2)}) copy-start(bf16[2,384,48]{1,2,0:T(8,128)(2,1)} %param.14) | copy-start | bytes 221188
  108.2 27.7 %copy-start.48 = (bf16[2,48,192]{2,1,0:T(8,128)(2,1)S(1)}, bf16[2,48,192]{2,1,0:T(8,128)(2,1)}, u32[]{:S(2)}) copy-start(bf16[2,48,192]{2,1,0:T(8,128)(2,1)} %param.12) | copy-start | bytes 110596
  108.2 27.7 %copy-start.49 = (bf16[2,48,192]{2,1,0:T(8,128)(2,1)S(1)}, bf16[2,48,192]{2,1,0:T(8,128)(2,1)}, u32[]{:S(2)}) copy-start(bf16[2,48,192]{2,1,0:T(8,128)(2,1)} %param.13) | copy-start | bytes 110596
  134.5 129.8 %copy-start.40 = (f32[1536]{0:T(1024)}, f32[1536]{0:T(1024)S(1)}, u32[]{:S(2)}) copy-start(f32[1536]{0:T(1024)S(1)} %get-tuple-element.102) | copy-start | bytes 18436
  134.7 129.6 %copy-start.60 = (f32[128]{0:T(128)}, f32[128]{0:T(128)S(1)}, u32[]{:S(2)}) copy-start(f32[128]{0:T(128)S(1)} %add_rsqrt_fusion.3) | copy-start | bytes 1540
  135.6 173.8 %reduce-scatter.12.cloned.1.call-start = ((), (), s32[]{:S(2)}) async-start(), calls=%async_computation.10 | async-start | bytes 1966080 | tf_op jit(solution)/shard_map/reduce_scatter | solution.py:596
  283.7 28.9 %copy-start.75 = (bf16[2,96,2,512]{3,1,2,0:T(8,128)(2,1)}, bf16[2,96,2,512]{3,1,2,0:T(8,128)(2,1)S(1)}, u32[]{:S(2)}) copy-start(bf16[2,96,2,512]{3,1,2,0:T(8,128)(2,1)S(1)} %fusion.59) | copy-start | bytes 1179652
  287.3 51.2 %all-gather.11.cloned.1.call-start = ((), (), s32[]{:S(2)}) async-start(), calls=%async_computation.11 | async-start | bytes 1966080 | tf_op jit(solution)/shard_map/all_gather | solution.py:588
  310.6 32.1 %copy-start.56 = (f32[128]{0:T(128)}, f32[128]{0:T(128)S(1)}, u32[]{:S(2)}) copy-start(f32[128]{0:T(128)S(1)} %add_rsqrt_fusion.2) | copy-start | bytes 1540
  312.6 67.2 %reduce-scatter.14.cloned.1.call-start = ((), (), s32[]{:S(2)}) async-start(), calls=%async_computation.12 | async-start | bytes 1966080 | tf_op jit(solution)/shard_map/reduce_scatter | solution.py:596
  342.8 5.9 copy-start.79
  354.6 25.2 %copy-start.5 = (bf16[128,1536]{1,0:T(8,128)(2,1)S(1)}, bf16[128,1536]{1,0:T(8,128)(2,1)}, u32[]{:S(2)}) copy-start(bf16[128,1536]{1,0:T(8,128)(2,1)} %reduce-scatter.12.cloned.1.call-done) | copy-start | bytes 1179652
  354.6 53.3 %all-gather.13.cloned.1.call-start = ((), (), s32[]{:S(2)}) async-start(), calls=%async_computation.13 | async-start | bytes 1966080 | tf_op jit(solution)/shard_map/all_gather | solution.py:588
  381.1 26.8 %copy-start.62 = (f32[128]{0:T(128)}, f32[128]{0:T(128)S(1)}, u32[]{:S(2)}) copy-start(f32[128]{0:T(128)S(1)} %add_rsqrt_fusion.1) | copy-start | bytes 1540
  382.0 63.9 %reduce-scatter.16.cloned.1.call-start = ((), (), s32[]{:S(2)}) async-start(), calls=%async_computation.14 | async-start | bytes 1966080 | tf_op jit(solution)/shard_map/reduce_scatter | solution.py:596
  417.1 29.9 %copy-start.77 = (bf16[2,96,2,512]{3,1,2,0:T(8,128)(2,1)}, bf16[2,96,2,512]{3,1,2,0:T(8,128)(2,1)S(1)}, u32[]{:S(2)}) copy-start(bf16[2,96,2,512]{3,1,2,0:T(8,128)(2,1)S(1)} %fusion.58) | copy-start | bytes 1179652
  420.7 52.6 %all-gather.17.cloned.1.call-start = ((), (), s32[]{:S(2)}) async-start(), calls=%async_computation.17 | async-start | bytes 1966080 | tf_op jit(solution)/shard_map/all_gather | solution.py:592
  421.5 79.9 %all-gather.15.cloned.1.call-start = ((), (), s32[]{:S(2)}) async-start(), calls=%async_computation.15 | async-start | bytes 1966080 | tf_op jit(solution)/shard_map/all_gather | solution.py:588
  447.0 100.7 %copy-start.59 = (f32[128]{0:T(128)}, f32[128]{0:T(128)S(1)}, u32[]{:S(2)}) copy-start(f32[128]{0:T(128)S(1)} %add_rsqrt_fusion) | copy-start | bytes 1540
  449.0 96.8 %reduce-scatter.20.cloned.1.call-start = ((), (), s32[]{:S(2)}) async-start(), calls=%async_computation.18 | async-start | bytes 1966080 | tf_op jit(solution)/shard_map/reduce_scatter | solution.py:609
  515.7 30.1 %copy-start.6 = (bf16[128,1536]{1,0:T(8,128)(2,1)S(1)}, bf16[128,1536]{1,0:T(8,128)(2,1)}, u32[]{:S(2)}) copy-start(bf16[128,1536]{1,0:T(8,128)(2,1)} %reduce-scatter.16.cloned.1.call-done) | copy-start | bytes 1179652
  520.6 27.1 %copy-start.12 = (bf16[128,1536]{1,0:T(8,128)(2,1)S(1)}, bf16[128,1536]{1,0:T(8,128)(2,1)}, u32[]{:S(2)}) copy-start(bf16[128,1536]{1,0:T(8,128)(2,1)} %param.19) | copy-start | bytes 1179652
  520.6 55.1 %all-gather.19.cloned.1.call-start = ((), (), s32[]{:S(2)}) async-start(), calls=%async_computation.19 | async-start | bytes 1966080 | tf_op jit(solution)/shard_map/all_gather | solution.py:592
  549.8 68.7 %reduce-scatter.22.cloned.1.call-start = ((), (), s32[]{:S(2)}) async-start(), calls=%async_computation.20 | async-start | bytes 1966080 | tf_op jit(solution)/shard_map/reduce_scatter | solution.py:609
  550.1 31.5 %copy-start.44 = (f32[2,2,512]{2,1,0:T(2,128)}, f32[2,2,512]{2,1,0:T(2,128)S(1)}, u32[]{:S(2)}) copy-start(f32[2,2,512]{2,1,0:T(2,128)S(1)} %log_add_fusion.1) | copy-start | bytes 24580
  593.4 52.4 %reduce-scatter.18.cloned.1.call-start = ((), (), s32[]{:S(2)}) async-start(), calls=%async_computation.16 | async-start | bytes 1966080 | tf_op jit(solution)/shard_map/reduce_scatter | solution.py:596
  593.5 25.1 %copy-start.43 = (f32[1536]{0:T(1024)S(1)}, f32[1536]{0:T(1024)}, u32[]{:S(2)}) copy-start(f32[1536]{0:T(1024)} %copy-done.42) | copy-start | bytes 18436
  593.5 25.1 %copy-start.63 = (f32[128]{0:T(128)S(1)}, f32[128]{0:T(128)}, u32[]{:S(2)}) copy-start(f32[128]{0:T(128)} %copy-done.62) | copy-start | bytes 1540
  598.7 75.8 %all-gather.21.cloned.1.call-start = ((), (), s32[]{:S(2)}) async-start(), calls=%async_computation.21 | async-start | bytes 1966080 | tf_op jit(solution)/shard_map/all_gather | solution.py:592
  648.6 66.5 %reduce-scatter.24.cloned.1.call-start = ((), (), s32[]{:S(2)}) async-start(), calls=%async_computation.22 | async-start | bytes 1966080 | tf_op jit(solution)/shard_map/reduce_scatter | solution.py:609
  685.0 30.1 %copy-start.57 = (f32[128]{0:T(128)S(1)}, f32[128]{0:T(128)}, u32[]{:S(2)}) copy-start(f32[128]{0:T(128)} %copy-done.56) | copy-start | bytes 1540
  689.9 29.7 %copy-start.16 = (bf16[512,4,96]{0,2,1:T(8,128)(2,1)S(1)}, bf16[512,4,96]{0,2,1:T(8,128)(2,1)}, u32[]{:S(2)}) copy-start(bf16[512,4,96]{0,2,1:T(8,128)(2,1)} %copy-done.15) | copy-start | bytes 1179652
  689.9 67.7 %all-gather.23.cloned.1.call-start = ((), (), s32[]{:S(2)}) async-start(), calls=%async_computation.23 | async-start | bytes 1966080 | tf_op jit(solution)/shard_map/all_gather | solution.py:592
  719.1 277.2 %reduce-scatter.26.cloned.1.call-start = ((), (), s32[]{:S(2)}) async-start(), calls=%async_computation.24 | async-start | bytes 1966080 | tf_op jit(solution)/shard_map/reduce_scatter | solution.py:609
  719.6 6.2 copy-start.10
  739.5 18.0 %copy-start.55 = (f32[1536]{0:T(1024)S(1)}, f32[1536]{0:T(1024)}, u32[]{:S(2)}) copy-start(f32[1536]{0:T(1024)} %get-tuple-element.86) | copy-start | bytes 18436
  775.2 457.8 %reduce-scatter.28.cloned.1.call-start = ((), (), s32[]{:S(2)}) async-start(), calls=%async_computation.25 | async-start | bytes 811008
  775.4 6.2 copy-start.8
  996.2 17.0 %copy-start.11 = (bf16[128,1536]{1,0:T(8,128)(2,1)S(1)}, bf16[128,1536]{1,0:T(8,128)(2,1)}, u32[]{:S(2)}) copy-start(bf16[128,1536]{1,0:T(8,128)(2,1)} %reduce-scatter.24.cloned.1.call-done) | copy-start | bytes 1179652
  996.2 17.0 %copy-start.58 = (f32[128]{0:T(128)S(1)}, f32[128]{0:T(128)}, u32[]{:S(2)}) copy-start(f32[128]{0:T(128)} %copy-done.56) | copy-start | bytes 1540
  996.2 17.0 %copy-start.65 = (f32[128]{0:T(128)S(1)}, f32[128]{0:T(128)}, u32[]{:S(2)}) copy-start(f32[128]{0:T(128)} %copy-done.64) | copy-start | bytes 1540
  996.2 16.9 %copy-start.17 = (bf16[128,1536]{1,0:T(8,128)(2,1)S(1)}, bf16[128,1536]{1,0:T(8,128)(2,1)}, u32[]{:S(2)}) copy-start(bf16[128,1536]{1,0:T(8,128)(2,1)} %reduce-scatter.26.cloned.1.call-done) | copy-start | bytes 1179652
  (61 other events, 183.3 us)
Sparse Core Ops, SparseCore 0:
  135.8 25.7 all-gather.8
  287.4 21.9 reduce-scatter.11
  312.7 25.7 all-gather.10
  354.8 24.9 reduce-scatter.13
  382.1 25.7 all-gather.12
  420.8 24.9 reduce-scatter.15
  447.5 25.7 all-gather.16
  475.5 25.7 all-gather.14
  520.7 24.9 reduce-scatter.19
  550.0 25.7 all-gather.18
  593.6 24.9 reduce-scatter.21
  620.8 24.9 reduce-scatter.17
  648.7 25.7 all-gather.20
  690.0 24.9 reduce-scatter.23
  719.2 25.7 all-gather.22
  775.3 24.9 reduce-scatter.25
  1013.3 219.6 reduce-scatter.27

commit v2 on v1

v2 whole, which is shorter than its diff:
```python
import math

import jax
import jax.numpy as jnp
from jax import lax
from jax.experimental import pallas as pl
from jax.experimental.pallas import tpu as pltpu
from jax.sharding import PartitionSpec as P

HD = 96
MESH_IDS = pl.DeviceIdType.MESH
SIDE = 4
MODEL = 1536
SEQ_ROWS = 512
OWN = 128
QKV = (0, 768)
OUT = (768, 1152)
GATE = (1152, 2176)
UP = (2176, 3200)
DOWN = (3200, 4224)
COLS = (384, 192, 192, 384, 1024, 1024, 1024)
WIDTH = 4224
ATTN_PARTS = (((0, 256), (256, 512)), ((512, 768), (768, 1152)))
MLP_PARTS = (((1152, 1920), (1920, 2688)), ((2688, 3456), (3456, 4224)))

norm_eps = 1e-05
rope_base = 100000.0
SCALING = 1.0 / math.sqrt(HD)


def cut(cols):
    return pl.ds(cols[0], cols[1] - cols[0])


def shift(place, step):
    return lax.rem(place + step + 2 * SIDE, SIDE)


class Place:
    def __init__(self):
        dp = lax.axis_index("dp")
        tensor = lax.axis_index("tensor")
        self.z_hi, self.x, self.y = dp // 16, (dp // 4) % 4, dp % 4
        self.z_lo, self.core = tensor // 2, tensor % 2
        self.dp, self.tensor = dp, tensor

    def device(self, z_hi, x, y, tensor):
        return (z_hi * 16 + x * 4 + y, tensor)

    def beside(self, axis, step):
        if axis == "x":
            return self.device(self.z_hi, shift(self.x, step), self.y, self.tensor)
        return self.device(self.z_hi, self.x, shift(self.y, step), self.tensor)

    def across(self):
        return self.device(1 - self.z_hi, self.x, self.y, self.tensor)

    def twin(self):
        return (self.dp, self.z_lo * 2 + 1 - self.core)

    def above(self):
        return (self.dp, (1 - self.z_lo) * 2 + self.core)

    def greet(self):
        targets = [self.beside(axis, step) for axis in ("x", "y") for step in (1, 2, 3)]
        targets += [self.across(), self.twin(), self.above()]
        barrier = pltpu.get_barrier_semaphore()
        for target in targets:
            pl.semaphore_signal(barrier, inc=1, device_id=target, device_id_type=MESH_IDS)
        pl.semaphore_wait(barrier, len(targets))


class Wire:
    def __init__(self, send_sems, recv_sems):
        self.send_sems, self.recv_sems = send_sems, recv_sems
        self.count = 0
        self.sent = []

    def slot(self):
        self.count += 1
        return self.count - 1

    def send(self, slot, source, target_ref, target):
        copy = pltpu.make_async_remote_copy(
            src_ref=source,
            dst_ref=target_ref,
            send_sem=self.send_sems.at[slot],
            recv_sem=self.recv_sems.at[slot],
            device_id=target,
            device_id_type=MESH_IDS,
        )
        copy.start()
        self.sent.append(copy)
        return copy

    def arrive(self, slot, landed, target):
        pltpu.make_async_remote_copy(
            src_ref=landed,
            dst_ref=landed,
            send_sem=self.send_sems.at[slot],
            recv_sem=self.recv_sems.at[slot],
            device_id=target,
            device_id_type=MESH_IDS,
        ).wait_recv()

    def release(self, copy):
        copy.wait_send()
        self.sent = [other for other in self.sent if other is not copy]

    def drain(self):
        for copy in self.sent:
            copy.wait_send()
        self.sent = []


class Local:
    def __init__(self, sems):
        self.sems, self.count, self.open = sems, 0, []

    def start(self, source, target):
        copy = pltpu.make_async_copy(source, target, self.sems.at[self.count])
        self.count += 1
        copy.start()
        self.open.append(copy)
        return copy

    def wait(self, copy):
        copy.wait()
        self.open = [other for other in self.open if other is not copy]

    def drain(self):
        for copy in self.open:
            copy.wait()
        self.open = []


def sum_small(wire, at, value_ref, landing, whole_group):
    rounds = []
    if whole_group:
        rounds += [[at.twin()], [at.above()]]
    rounds += [[at.across()]]
    rounds += [[at.beside(axis, step) for step in (1, 2, 3)] for axis in ("y", "x")]
    place = 0
    for targets in rounds:
        slots = [wire.slot() for _ in targets]
        copies = []
        for index, target in enumerate(targets):
            copies.append(wire.send(slots[index], value_ref, landing.at[place + index], target))
        yield
        total = value_ref[...]
        for index, target in enumerate(targets):
            wire.arrive(slots[index], landing.at[place + index], target)
            total = total + landing[place + index]
        for copy in copies:
            wire.release(copy)
        value_ref[...] = total
        place += len(targets)
    yield


class Spread:
    pieces = 2

    def __init__(self, wire, at, rows_ref):
        self.wire, self.at, self.rows_ref = wire, at, rows_ref
        self.near = wire.slot()
        self.over = [wire.slot() for _ in range(self.pieces)]
        self.passed = [wire.slot() for _ in range(self.pieces)]
        self.size = OWN // self.pieces

    def rows(self, tensor, piece=None):
        start = pl.multiple_of(tensor * OWN, OWN)
        if piece is None:
            return self.rows_ref.at[pl.ds(start, OWN)]
        return self.rows_ref.at[
            pl.ds(pl.multiple_of(start + piece * self.size, self.size), self.size)
        ]

    def start(self):
        at, wire = self.at, self.wire
        own = at.tensor
        for piece in range(self.pieces):
            wire.send(self.over[piece], self.rows(own, piece), self.rows(own, piece), at.above())
        wire.send(self.near, self.rows(own), self.rows(own), at.twin())

    def near_done(self):
        at = self.at
        self.wire.arrive(self.near, self.rows(at.z_lo * 2 + 1 - at.core), at.twin())

    def pass_on(self):
        at, wire = self.at, self.wire
        there = (1 - at.z_lo) * 2 + at.core
        for piece in range(self.pieces):
            block = self.rows(there, piece)
            wire.arrive(self.over[piece], block, at.above())
            wire.send(self.passed[piece], block, block, at.twin())

    def far_done(self):
        at = self.at
        there = (1 - at.z_lo) * 2 + 1 - at.core
        for piece in range(self.pieces):
            self.wire.arrive(self.passed[piece], self.rows(there, piece), at.twin())


class Collect:
    pieces = 2

    def __init__(self, wire, at, part, help_ref, near_ref, over_ref):
        self.wire, self.at, self.part = wire, at, part
        self.help_ref, self.near_ref, self.over_ref = help_ref, near_ref, over_ref
        self.help = wire.slot()
        self.near = wire.slot()
        self.over = [wire.slot() for _ in range(self.pieces)]
        self.copies = []
        self.size = OWN // self.pieces

    def rows(self, z_lo, core):
        return pl.ds(pl.multiple_of((z_lo * 2 + core) * OWN, OWN), OWN)

    def other_ready(self):
        at = self.at
        block = self.part.at[self.rows(1 - at.z_lo, 1 - at.core)]
        self.copies.append(self.wire.send(self.help, block, self.help_ref, at.twin()))

    def own_ready(self):
        at = self.at
        block = self.part.at[self.rows(at.z_lo, 1 - at.core)]
        self.copies.append(self.wire.send(self.near, block, self.near_ref, at.twin()))

    def send_over(self):
        at = self.at
        self.wire.arrive(self.help, self.help_ref, at.twin())
        for piece in range(self.pieces):
            window = pl.ds(piece * self.size, self.size)
            start = ((1 - at.z_lo) * 2 + at.core) * OWN + piece * self.size
            rows = pl.ds(pl.multiple_of(start, self.size), self.size)
            total = self.part[rows, :].astype(jnp.float32) + self.help_ref[window, :].astype(
                jnp.float32
            )
            self.part[rows, :] = total.astype(jnp.bfloat16)
            self.copies.append(
                self.wire.send(
                    self.over[piece],
                    self.part.at[rows],
                    self.over_ref.at[window],
                    at.above(),
                )
            )

    def result(self):
        at = self.at
        self.wire.arrive(self.near, self.near_ref, at.twin())
        total = self.part[self.rows(at.z_lo, at.core), :].astype(jnp.float32) + self.near_ref[
            ...
        ].astype(jnp.float32)
        for piece in range(self.pieces):
            window = pl.ds(piece * self.size, self.size)
            self.wire.arrive(self.over[piece], self.over_ref.at[window], at.above())
        total = total + self.over_ref[...].astype(jnp.float32)
        for copy in self.copies:
            self.wire.release(copy)
        self.copies = []
        return total


def nn(left, right):
    return jnp.dot(left, right, preferred_element_type=jnp.float32)


def nt(left, right):
    return lax.dot_general(
        left, right, (((1,), (1,)), ((), ())), preferred_element_type=jnp.float32
    )


def tn(left, right):
    return lax.dot_general(
        left, right, (((0,), (0,)), ((), ())), preferred_element_type=jnp.float32
    )


def rope_tables(heads):
    half = HD // 2
    position = jnp.arange(SEQ_ROWS, dtype=jnp.float32)[:, None]
    exponent = 2.0 * jnp.arange(half, dtype=jnp.float32) / HD
    angles = position * (rope_base ** (-exponent))[None, :]
    cosine, sine = jnp.cos(angles), jnp.sin(angles)
    wide_cosine = jnp.concatenate([cosine, cosine], axis=1)
    wide_sine = jnp.concatenate([-sine, sine], axis=1)
    return jnp.tile(wide_cosine, (1, heads)), jnp.tile(wide_sine, (1, heads))


def swap_halves(values):
    width = values.shape[1]
    lane = lax.broadcasted_iota(jnp.int32, values.shape, 1)
    first = lax.rem(lane, HD) < HD // 2
    return jnp.where(
        first, pltpu.roll(values, width - HD // 2, 1), pltpu.roll(values, HD // 2, 1)
    )


def head_of(values, start):
    width = values.shape[1]
    moved = values if start == 0 else pltpu.roll(values, width - start, 1)
    moved = moved[:, :128]
    lane = lax.broadcasted_iota(jnp.int32, moved.shape, 1)
    return jnp.where(lane < HD, moved, 0.0)


def side_by_side(heads):
    tiles = []
    for tile in range(len(heads) * HD // 128):
        total = None
        lane = lax.broadcasted_iota(jnp.int32, heads[0].shape, 1)
        for index, head in enumerate(heads):
            start = index * HD - tile * 128
            if start <= -HD or start >= 128:
                continue
            moved = pltpu.roll(head, start % 128, 1) if start else head
            if start > 0 or start < 0:
                keep = (lane >= start) if start > 0 else (lane < start + HD)
                moved = jnp.where(keep, moved, 0.0)
            total = moved if total is None else total + moved
        tiles.append(total)
    return jnp.concatenate(tiles, axis=1)


def chip_rows(z_lo):
    return pl.ds(pl.multiple_of(z_lo * 256, 256), 256)


def weight(w_ref, layer, cols):
    value = w_ref[layer, :, :, cols]
    return value.reshape(MODEL, value.shape[-1])


def gather_job(wire, at, full, layer, group):
    parts = []
    for (first, second), (left, right) in zip((("y", "x"), ("x", "y")), group):

        def block(first_step, second_step, cols, first=first):
            x_step, y_step = (
                (first_step, second_step) if first == "x" else (second_step, first_step)
            )
            row = shift(at.x, x_step) * 192 + shift(at.y, y_step) * 48
            return full.at[layer, :, pl.ds(pl.multiple_of(row, 48), 48), cut(cols)]

        parts.append(
            dict(
                first=first,
                second=second,
                left=left,
                right=right,
                whole=(left[0], right[1]),
                block=block,
                one={s: wire.slot() for s in (1, -1)},
                two={s: wire.slot() for s in (1, -1)},
                side={(f, s): wire.slot() for f in (0, -1, 1, 2) for s in (1, -1)},
                far={(f, s): wire.slot() for f in (0, -1, 1, 2) for s in (1, -1)},
            )
        )

    def half(part, step):
        return part["left"] if step == 1 else part["right"]

    def one_start(part, step):
        piece = part["block"](0, 0, part["whole"])
        wire.send(part["one"][step], piece, piece, at.beside(part["first"], step))

    def side_start(part, first_step):
        for step in (1, -1):
            piece = part["block"](first_step, 0, part["whole"])
            wire.send(
                part["side"][first_step, step], piece, piece, at.beside(part["second"], step)
            )

    def one_done(part, step):
        target = at.beside(part["first"], step)
        wire.arrive(part["one"][step], part["block"](-step, 0, part["whole"]), target)
        piece = part["block"](-step, 0, half(part, step))
        wire.send(part["two"][step], piece, piece, target)

    def two_done(part):
        for step in (1, -1):
            piece = part["block"](2, 0, half(part, step))
            wire.arrive(part["two"][step], piece, at.beside(part["first"], step))

    def side_done(part, first_step):
        for step in (1, -1):
            target = at.beside(part["second"], step)
            landed = part["block"](first_step, -step, part["whole"])
            wire.arrive(part["side"][first_step, step], landed, target)
            piece = part["block"](first_step, -step, half(part, step))
            wire.send(part["far"][first_step, step], piece, piece, target)

    def far_done(part, first_step):
        for step in (1, -1):
            piece = part["block"](first_step, 2, half(part, step))
            wire.arrive(part["far"][first_step, step], piece, at.beside(part["second"], step))

    for part in parts:
        for step in (1, -1):
            one_start(part, step)
    for part in parts:
        side_start(part, 0)
    yield
    for step in (1, -1):
        for part in parts:
            one_done(part, step)
    for first_step in (-1, 1):
        for part in parts:
            side_start(part, first_step)
    yield
    for part in parts:
        two_done(part)
    for part in parts:
        side_start(part, 2)
    for part in parts:
        side_done(part, 0)
    yield
    for first_step in (-1, 1):
        for part in parts:
            side_done(part, first_step)
    yield
    for part in parts:
        side_done(part, 2)
    yield
    for first_step in (0, -1, 1, 2):
        for part in parts:
            far_done(part, first_step)
    yield


class Gather:
    def __init__(self, wire, local, at, shard, full, kept):
        self.wire, self.local, self.at, self.shard = wire, local, at, shard
        self.full, self.kept = full, kept
        self.groups = [
            (layer, group) for layer in range(2) for group in (ATTN_PARTS, MLP_PARTS)
        ]
        self.jobs = [gather_job(wire, at, full, *pair) for pair in self.groups]
        self.slots = [wire.slot() for _ in self.groups]
        self.own = []
        order = [(0, 0), (0, 1)]
        for index in range(len(self.jobs)):
            order += [(index, 2), (index + 1, 0), (index, 3), (index, 4), (index + 1, 1)]
            order += [(index, 5)]
        self.order = [pair for pair in order if pair[0] < len(self.jobs)]
        self.done = 0

    def columns(self, index):
        group = self.groups[index][1]
        return cut((group[0][0][0], group[1][1][1]))

    def mine(self, z_hi):
        row = self.at.x * 192 + self.at.y * 48
        return (z_hi, pl.ds(pl.multiple_of(row, 48), 48))

    def begin(self):
        at = self.at
        z_own, rows = self.mine(at.z_hi)
        for index, (layer, _) in enumerate(self.groups):
            cols = self.columns(index)
            source = self.shard.at[layer, :, cols]
            target = self.full.at[layer, z_own, rows, cols]
            self.wire.send(self.slots[index], source, target, at.across())
            self.own.append(self.local.start(source, target))

    def step(self, count=1):
        for _ in range(count):
            if self.done == len(self.order):
                return
            index, stage = self.order[self.done]
            self.done += 1
            layer = self.groups[index][0]
            cols = self.columns(index)
            if stage == 0:
                self.local.wait(self.own[index])
                z_other, rows = self.mine(1 - self.at.z_hi)
                landed = self.full.at[layer, z_other, rows, cols]
                self.wire.arrive(self.slots[index], landed, self.at.across())
            next(self.jobs[index])
            if stage == 5:
                self.local.start(
                    self.full.at[layer, :, :, cols], self.kept.at[layer, :, :, cols]
                )

    def until(self, index):
        while (index, 5) in self.order[self.done :]:
            self.step()


def normed(rows_in, gain):
    inverse = lax.rsqrt(jnp.mean(rows_in * rows_in, axis=-1, keepdims=True) + norm_eps)
    return (rows_in * inverse * gain).astype(jnp.bfloat16)


def project_heads(layer, rows, n1, w, cosine, sine, q_ref, k_ref, v_ref):
    left = n1[layer, rows, :]
    cosine_rows, sine_rows = cosine[rows, :], sine[rows, :]
    query = nn(left, weight(w, layer, pl.ds(0, 384)))
    turned = query * cosine_rows + swap_halves(query) * sine_rows
    for head in range(4):
        q_ref[layer, head, rows, :] = head_of(turned, head * HD).astype(jnp.bfloat16)
    both = nn(left, weight(w, layer, pl.ds(384, 384)))
    turned = both * cosine_rows + swap_halves(both) * sine_rows
    for head in range(2):
        k_ref[layer, head, rows, :] = head_of(turned, head * HD).astype(jnp.bfloat16)
        v_ref[layer, head, rows, :] = head_of(both, 192 + head * HD).astype(jnp.bfloat16)


def attend(layer, q_ref, k_ref, v_ref, p_ref, o_ref):
    for block in range(4):
        rows = pl.ds(block * 128, 128)
        keys = (block + 1) * 128
        outputs = []
        for head in range(2):
            pair = jnp.concatenate(
                [q_ref[layer, 2 * head, rows, :], q_ref[layer, 2 * head + 1, rows, :]], axis=0
            )
            scores = nt(pair, k_ref[layer, head, pl.ds(0, keys), :]) * SCALING
            row = lax.broadcasted_iota(jnp.int32, (256, keys), 0) % 128 + block * 128
            key = lax.broadcasted_iota(jnp.int32, (256, keys), 1)
            scores = jnp.where(row >= key, scores, -1e30)
            peak = jnp.max(scores, axis=-1, keepdims=True)
            exponent = jnp.exp(scores - peak)
            inverse = 1.0 / jnp.sum(exponent, axis=-1, keepdims=True)
            shares = (exponent * inverse).astype(jnp.bfloat16)
            p_ref[layer, 2 * head, rows, pl.ds(0, keys)] = shares[:128]
            p_ref[layer, 2 * head + 1, rows, pl.ds(0, keys)] = shares[128:]
            out = nn(shares, v_ref[layer, head, pl.ds(0, keys), :])
            outputs += [out[:128], out[128:]]
        o_ref[layer, rows, :] = side_by_side(outputs).astype(jnp.bfloat16)


def out_partial(layer, rows, o_ref, w, part):
    left = o_ref[layer, rows, :]
    for half in range(2):
        for tile in range(3):
            right = w[layer, half, pl.ds(tile * 256, 256), cut(OUT)]
            part[rows, pl.ds(half * 768 + tile * 256, 256)] = nt(left, right).astype(jnp.bfloat16)


def hidden_rows(layer, rows, n2, w, g_ref, u_ref, a_ref):
    left = n2[layer, rows, :]

    def tile(index, carry):
        start = pl.multiple_of(index * 256, 256)
        gate = nn(left, weight(w, layer, pl.ds(GATE[0] + start, 256)))
        up = nn(left, weight(w, layer, pl.ds(UP[0] + start, 256)))
        hidden = gate * up / (1.0 + jnp.exp(-gate))
        g_ref[layer, rows, pl.ds(start, 256)] = gate.astype(g_ref.dtype)
        u_ref[layer, rows, pl.ds(start, 256)] = up.astype(u_ref.dtype)
        a_ref[layer, rows, pl.ds(start, 256)] = hidden.astype(jnp.bfloat16)
        return carry

    lax.fori_loop(0, 4, tile, 0)


def down_partial(layer, rows, a_ref, w, part):
    left = a_ref[layer, rows, :]
    for half in range(2):

        def tile(index, carry, half=half):
            start = pl.multiple_of(index * 256, 256)
            right = w[layer, half, pl.ds(start, 256), cut(DOWN)]
            part[rows, pl.ds(pl.multiple_of(half * 768 + start, 256), 256)] = nt(
                left, right
            ).astype(jnp.bfloat16)
            return carry

        lax.fori_loop(0, 3, tile, 0)


def forward_kernel(
    shard,
    gains_placed,
    tokens,
    cosine,
    sine,
    w_kept,
    gains,
    output,
    n1_kept,
    n2_kept,
    q_kept,
    k_kept,
    v_kept,
    p_kept,
    o_kept,
    g_kept,
    u_kept,
    a_kept,
    x_kept,
    h_kept,
    w,
    n1,
    n2,
    q_ref,
    k_ref,
    v_ref,
    p_ref,
    o_ref,
    g_ref,
    u_ref,
    a_ref,
    x_ref,
    h_ref,
    part,
    help_ref,
    near_ref,
    over_ref,
    gains_landing,
    send_sems,
    recv_sems,
    local_sems,
):
    at = Place()
    at.greet()
    wire = Wire(send_sems, recv_sems)
    local = Local(local_sems)
    gather = Gather(wire, local, at, shard, w, w_kept)
    gather.begin()
    gather.step()
    gains[...] = gains_placed[...]
    rounds = sum_small(wire, at, gains, gains_landing, False)
    for _ in rounds:
        gather.step()
    x_ref[0] = tokens[...].astype(jnp.float32)
    own = pl.ds(pl.multiple_of(at.tensor * OWN, OWN), OWN)
    here, there = chip_rows(at.z_lo), chip_rows(1 - at.z_lo)
    turn = 0

    def collector():
        nonlocal turn
        turn += 1
        slot = turn % 2
        return Collect(
            wire, at, part, help_ref.at[slot], near_ref.at[slot], over_ref.at[slot]
        )

    for layer in range(2):
        n1[layer, own, :] = normed(x_ref[layer], gains[pl.ds(2 * layer, 1), :])
        spread = Spread(wire, at, n1.at[layer])
        spread.start()
        gather.until(2 * layer)
        heads = (n1, w, cosine, sine, q_ref, k_ref, v_ref)
        spread.near_done()
        project_heads(layer, here, *heads)
        gather.step()
        spread.pass_on()
        spread.far_done()
        project_heads(layer, there, *heads)
        for source, target in ((n1, n1_kept), (q_ref, q_kept), (k_ref, k_kept), (v_ref, v_kept)):
            local.start(source.at[layer], target.at[layer])
        gather.step()
        attend(layer, q_ref, k_ref, v_ref, p_ref, o_ref)
        for source, target in ((p_ref, p_kept), (o_ref, o_kept)):
            local.start(source.at[layer], target.at[layer])
        collect = collector()
        out_partial(layer, there, o_ref, w, part)
        collect.other_ready()
        out_partial(layer, here, o_ref, w, part)
        collect.own_ready()
        collect.send_over()
        gather.step()
        h_ref[layer] = x_ref[layer] + collect.result()
        n2[layer, own, :] = normed(h_ref[layer], gains[pl.ds(2 * layer + 1, 1), :])
        spread = Spread(wire, at, n2.at[layer])
        spread.start()
        gather.until(2 * layer + 1)
        spread.near_done()
        hidden_rows(layer, here, n2, w, g_ref, u_ref, a_ref)
        gather.step()
        spread.pass_on()
        spread.far_done()
        hidden_rows(layer, there, n2, w, g_ref, u_ref, a_ref)
        for source, target in (
            (n2, n2_kept),
            (h_ref, h_kept),
            (g_ref, g_kept),
            (u_ref, u_kept),
            (a_ref, a_kept),
        ):
            local.start(source.at[layer], target.at[layer])
        collect = collector()
        down_partial(layer, there, a_ref, w, part)
        collect.other_ready()
        down_partial(layer, here, a_ref, w, part)
        collect.own_ready()
        collect.send_over()
        gather.step()
        total = h_ref[layer] + collect.result()
        if layer == 0:
            x_ref[1] = total
            local.start(x_ref.at[1], x_kept)
        else:
            output[...] = total.astype(jnp.bfloat16)
    local.drain()
    wire.drain()


KEEP = jnp.bfloat16


def run_forward(shard, gains_placed, tokens, cosine, sine):
    def kept(*shape, kind=jnp.bfloat16):
        return jax.ShapeDtypeStruct(shape, kind)

    def held(*shape, kind=jnp.bfloat16):
        return pltpu.VMEM(shape, kind)

    vmem = pl.BlockSpec(memory_space=pltpu.VMEM)
    hbm = pl.BlockSpec(memory_space=pl.ANY)
    float32 = jnp.float32
    wires = 4 * 41 + 7 + 8 * 5 + 4
    return pl.pallas_call(
        forward_kernel,
        out_shape=(
            kept(2, 2, 768, WIDTH),
            kept(8, MODEL, kind=float32),
            kept(OWN, MODEL),
            kept(2, SEQ_ROWS, MODEL),
            kept(2, SEQ_ROWS, MODEL),
            kept(2, 4, SEQ_ROWS, 128),
            kept(2, 2, SEQ_ROWS, 128),
            kept(2, 2, SEQ_ROWS, 128),
            kept(2, 4, SEQ_ROWS, SEQ_ROWS),
            kept(2, SEQ_ROWS, 384),
            kept(2, SEQ_ROWS, 1024, kind=KEEP),
            kept(2, SEQ_ROWS, 1024, kind=KEEP),
            kept(2, SEQ_ROWS, 1024),
            kept(OWN, MODEL, kind=float32),
            kept(2, OWN, MODEL, kind=float32),
        ),
        in_specs=[vmem] * 5,
        out_specs=(hbm, vmem, vmem) + (hbm,) * 12,
        scratch_shapes=[
            held(2, 2, 768, WIDTH),
            held(2, SEQ_ROWS, MODEL),
            held(2, SEQ_ROWS, MODEL),
            held(2, 4, SEQ_ROWS, 128),
            held(2, 2, SEQ_ROWS, 128),
            held(2, 2, SEQ_ROWS, 128),
            held(2, 4, SEQ_ROWS, SEQ_ROWS),
            held(2, SEQ_ROWS, 384),
            held(2, SEQ_ROWS, 1024, kind=KEEP),
            held(2, SEQ_ROWS, 1024, kind=KEEP),
            held(2, SEQ_ROWS, 1024),
            held(2, OWN, MODEL, kind=float32),
            held(2, OWN, MODEL, kind=float32),
            held(SEQ_ROWS, MODEL),
            held(2, OWN, MODEL),
            held(2, OWN, MODEL),
            held(2, OWN, MODEL),
            held(7, 8, MODEL, kind=float32),
            pltpu.SemaphoreType.DMA((wires,)),
            pltpu.SemaphoreType.DMA((wires,)),
            pltpu.SemaphoreType.DMA((40,)),
        ],
        compiler_params=pltpu.CompilerParams(
            collective_id=0, has_side_effects=True, vmem_limit_bytes=62 * 2**20
        ),
        name="forward",
    )(shard, gains_placed, tokens, cosine, sine)


HALVES = (((0, 1024), (1024, 2048)), ((2048, 3072), (3072, 4224)))


def add_into(target, terms, rows_lead):
    def step(index, carry):
        lead, start = index // 3, pl.multiple_of((index % 3) * 16, 16)
        window = (lead, pl.ds(start, 16)) if rows_lead else (pl.ds(start, 16),)
        total = None
        for term in terms:
            value = term[window].astype(jnp.float32)
            total = value if total is None else total + value
        target[window] = total.astype(target.dtype)
        return carry

    lax.fori_loop(0, 3 * (SIDE if rows_lead else 1), step, 0)


def scatter_job(wire, at, grads, layer, z_data, job, bufs, finish):
    one, two_up, two_down, small_one, small_up, small_down = bufs

    def cut(cols):
        return pl.ds(cols[0], cols[1] - cols[0])

    parts = []
    for first, second, (left, right) in (("y", "x", HALVES[0]), ("x", "y", HALVES[1])):

        def region(step, cols, second=second):
            if second == "x":
                return grads.at[layer, z_data, shift(at.x, step), :, :, cut(cols)]
            return grads.at[layer, z_data, :, shift(at.y, step), :, cut(cols)]

        def mine(step, cols, first=first):
            place = at.y if first == "y" else at.x
            return two_up.at[job, shift(place, step), :, cut(cols)]

        parts.append(
            dict(
                first=first,
                second=second,
                left=left,
                right=right,
                whole=(left[0], right[1]),
                region=region,
                mine=mine,
                far={s: wire.slot() for s in (1, -1)},
                raw={s: wire.slot() for s in (1, -1)},
                sum={s: wire.slot() for s in (1, -1)},
                far2={s: wire.slot() for s in (1, -1)},
                raw2={s: wire.slot() for s in (1, -1)},
                sum2={s: wire.slot() for s in (1, -1)},
            )
        )

    def half(part, step):
        return part["left"] if step == 1 else part["right"]

    def other(part, step):
        return part["right"] if step == 1 else part["left"]

    def landing(step):
        return two_up if step == 1 else two_down

    def small_landing(step):
        return small_up if step == 1 else small_down

    for part in parts:
        for step in (1, -1):
            cols = half(part, step)
            wire.send(
                part["far"][step],
                part["region"](2, cols),
                one.at[job, :, :, cut(cols)],
                at.beside(part["second"], step),
            )
    for part in parts:
        for step in (1, -1):
            cols = other(part, step)
            wire.send(
                part["raw"][step],
                part["region"](step, cols),
                landing(step).at[job, :, :, cut(cols)],
                at.beside(part["second"], step),
            )
    yield
    for step in (1, -1):
        for part in parts:
            cols = half(part, step)
            target = at.beside(part["second"], step)
            piece = one.at[job, :, :, cut(cols)]
            wire.arrive(part["far"][step], piece, target)
            add_into(piece, (piece, part["region"](step, cols)), True)
            wire.send(part["sum"][step], piece, landing(step).at[job, :, :, cut(cols)], target)
    yield
    for part in parts:
        for step in (1, -1):
            target = at.beside(part["second"], step)
            cols = other(part, step)
            wire.arrive(part["raw"][step], landing(step).at[job, :, :, cut(cols)], target)
            cols = half(part, step)
            wire.arrive(part["sum"][step], landing(step).at[job, :, :, cut(cols)], target)
        cols = part["whole"]
        piece = two_up.at[job, :, :, cut(cols)]
        add_into(
            piece,
            (part["region"](0, cols), piece, two_down.at[job, :, :, cut(cols)]),
            True,
        )
        for step in (1, -1):
            cols = half(part, step)
            target = at.beside(part["first"], step)
            wire.send(
                part["far2"][step], part["mine"](2, cols), small_one.at[job, :, cut(cols)], target
            )
            cols = other(part, step)
            wire.send(
                part["raw2"][step],
                part["mine"](step, cols),
                small_landing(step).at[job, :, cut(cols)],
                target,
            )
    yield
    for step in (1, -1):
        for part in parts:
            cols = half(part, step)
            target = at.beside(part["first"], step)
            piece = small_one.at[job, :, cut(cols)]
            wire.arrive(part["far2"][step], piece, target)
            add_into(piece, (piece, part["mine"](step, cols)), False)
            wire.send(
                part["sum2"][step], piece, small_landing(step).at[job, :, cut(cols)], target
            )
    yield
    for part in parts:
        for step in (1, -1):
            target = at.beside(part["first"], step)
            cols = other(part, step)
            wire.arrive(part["raw2"][step], small_landing(step).at[job, :, cut(cols)], target)
            cols = half(part, step)
            wire.arrive(part["sum2"][step], small_landing(step).at[job, :, cut(cols)], target)
        cols = part["whole"]
        finish(
            cut(cols),
            (
                part["mine"](0, cols),
                small_up.at[job, :, cut(cols)],
                small_down.at[job, :, cut(cols)],
            ),
        )
    yield


def scatter_kernel(
    grads,
    out,
    one,
    two_up,
    two_down,
    small_one,
    small_up,
    small_down,
    leaving,
    landed,
    send_sems,
    recv_sems,
):
    at = Place()
    at.greet()
    wire = Wire(send_sems, recv_sems)
    layers = grads.shape[0]
    bufs = (one, two_up, two_down, small_one, small_up, small_down)
    jobs = []
    for layer in range(layers):
        across = [wire.slot() for _ in range(2)]
        places = (pl.ds(0, 2048), pl.ds(2048, WIDTH - 2048))
        turn = iter(range(2))

        def finish_other(cols, terms, layer=layer, across=across, turn=turn):
            piece = leaving.at[layer, :, cols]
            add_into(piece, terms, False)
            wire.send(
                across[next(turn)], piece, landed.at[layer, :, cols], at.across()
            )

        turn_own = iter(range(2))

        def finish_own(cols, terms, layer=layer, across=across, turn=turn_own):
            piece = landed.at[layer, :, cols]
            wire.arrive(across[next(turn)], piece, at.across())
            add_into(out.at[layer, :, cols], terms + (piece,), False)

        jobs.append(
            scatter_job(
                wire, at, grads, layer, 1 - at.z_hi, 2 * layer, bufs, finish_other
            )
        )
        jobs.append(
            scatter_job(wire, at, grads, layer, at.z_hi, 2 * layer + 1, bufs, finish_own)
        )

    def advance(index):
        if index < len(jobs):
            next(jobs[index])

    advance(0)
    advance(0)
    for index in range(len(jobs)):
        advance(index + 1)
        advance(index)
        advance(index)
        advance(index + 1)
        advance(index)
    wire.drain()


def scatter_grads(grads):
    layers = grads.shape[0]
    slots = layers * 50
    jobs = 2 * layers
    return pl.pallas_call(
        scatter_kernel,
        out_shape=jax.ShapeDtypeStruct((layers, 48, WIDTH), jnp.float32),
        in_specs=[pl.BlockSpec(memory_space=pltpu.VMEM)],
        out_specs=pl.BlockSpec(memory_space=pltpu.VMEM),
        scratch_shapes=[
            pltpu.VMEM((jobs, SIDE, 48, WIDTH), jnp.bfloat16),
            pltpu.VMEM((jobs, SIDE, 48, WIDTH), jnp.bfloat16),
            pltpu.VMEM((jobs, SIDE, 48, WIDTH), jnp.bfloat16),
            pltpu.VMEM((jobs, 48, WIDTH), jnp.bfloat16),
            pltpu.VMEM((jobs, 48, WIDTH), jnp.bfloat16),
            pltpu.VMEM((jobs, 48, WIDTH), jnp.bfloat16),
            pltpu.VMEM((layers, 48, WIDTH), jnp.bfloat16),
            pltpu.VMEM((layers, 48, WIDTH), jnp.bfloat16),
            pltpu.SemaphoreType.DMA((slots,)),
            pltpu.SemaphoreType.DMA((slots,)),
        ],
        compiler_params=pltpu.CompilerParams(
            collective_id=1, has_side_effects=True, vmem_limit_bytes=60 * 2**20
        ),
        name="scatter_grads",
    )(grads)


def pack_rows(arrays):
    query, key, value, out, gate, up, down = arrays
    turned_out = jnp.swapaxes(out, 1, 2)
    turned_down = jnp.swapaxes(down, 1, 2)
    return jnp.concatenate([query, key, value, turned_out, gate, up, turned_down], axis=2)


def norm_backward(rows_in, gain, grad_normed):
    inverse = lax.rsqrt(jnp.mean(rows_in * rows_in, axis=-1, keepdims=True) + norm_eps)
    scaled = rows_in * inverse
    grad_gain = jnp.sum(grad_normed * scaled, axis=0)
    grad_scaled = grad_normed * gain
    grad_input = inverse * (
        grad_scaled - scaled * jnp.mean(grad_scaled * scaled, axis=-1, keepdims=True)
    )
    return (grad_input, grad_gain)


def body(
    tokens,
    query_weight,
    key_weight,
    value_weight,
    out_weight,
    gate_weight,
    up_weight,
    down_weight,
    norm_gains,
    grad_out,
):
    layers = 2
    packed = pack_rows(
        (query_weight, key_weight, value_weight, out_weight, gate_weight, up_weight, down_weight)
    )
    dp = lax.axis_index("dp")
    gains_placed = lax.dynamic_update_slice(
        jnp.zeros((8, MODEL), jnp.float32),
        norm_gains.reshape(4, -1).astype(jnp.float32),
        (0, dp * 48),
    )
    cosine, sine = rope_tables(4)
    (
        w_kept, gains, output, n1, n2, q, k, v, p, o, g, u, a, x_second, h,
    ) = run_forward(packed, gains_placed, tokens, cosine, sine)
    w_kept = w_kept.reshape(2, MODEL, WIDTH)
    grad_residual = grad_out.astype(jnp.float32)
    layer_results = [None] * layers
    tri = jnp.tril(jnp.ones((512, 512), bool))
    def gat(r):
        return lax.all_gather(r.astype(jnp.bfloat16), "tensor", axis=0, tiled=True)
    def rs(r):
        return lax.psum_scatter(r.astype(jnp.bfloat16), "tensor", scatter_dimension=0, tiled=True).astype(jnp.float32)
    f32 = jnp.float32
    def unrot(vals):
        c, s = cosine[:, : vals.shape[1]], sine[:, : vals.shape[1]]
        v4 = vals.reshape(512, -1, 2, 48)
        sw = v4[:, :, ::-1].reshape(vals.shape)
        return vals * c - sw * s
    for l in (1, 0):
        W = w_kept[l]
        residual = tokens.astype(f32) if l == 0 else x_second
        dm = gat(grad_residual)
        da = nn(dm, W[:, 3200:4224])
        gd = tn(dm, a[l])
        G, U = g[l].astype(f32), u[l].astype(f32)
        sg = jax.nn.sigmoid(G)
        dg = (da * U * sg * (1 + G * (1 - sg))).astype(jnp.bfloat16)
        du = (da * G * sg).astype(jnp.bfloat16)
        gg, gu = tn(n2[l], dg), tn(n2[l], du)
        dn2 = rs(nt(dg, W[:, 1152:2176]) + nt(du, W[:, 2176:3200]))
        gn, gain2 = norm_backward(h[l], gains[2 * l + 1], dn2)
        gmid = grad_residual + gn
        dhb = gat(gmid)
        do = nn(dhb, W[:, 768:1152]).astype(jnp.bfloat16)
        go = tn(dhb, o[l])
        dqs, dks, dvs = [], [], []
        for kv in range(2):
            dk = dv = 0
            for hh in (2 * kv, 2 * kv + 1):
                P_ = jnp.where(tri, p[l, hh], 0).astype(f32)
                doh = do[:, hh * 96 : hh * 96 + 96]
                dP = nt(doh, v[l, kv, :, :96])
                dS = (P_ * (dP - jnp.sum(dP * P_, -1, keepdims=True))).astype(jnp.bfloat16)
                dqs.append(nn(dS, k[l, kv, :, :96]) * SCALING)
                dk = dk + tn(dS, q[l, hh, :, :96]) * SCALING
                dv = dv + tn(P_.astype(jnp.bfloat16), doh)
            dks.append(dk)
            dvs.append(dv)
        dq = unrot(jnp.concatenate(dqs, 1)).astype(jnp.bfloat16)
        dk = unrot(jnp.concatenate(dks, 1)).astype(jnp.bfloat16)
        dv = jnp.concatenate(dvs, 1).astype(jnp.bfloat16)
        dqkv = jnp.concatenate([dq, dk, dv], 1)
        gqkv = tn(n1[l], dqkv)
        dn1 = rs(nt(dqkv, W[:, :768]))
        gn, gain1 = norm_backward(residual, gains[2 * l], dn1)
        grad_residual = gmid + gn
        layer_results[l] = (gqkv, go, gg, gu, gd, jnp.stack([gain1, gain2]))
    grads = jnp.stack(
        [jnp.concatenate([t.astype(jnp.bfloat16) for t in r[:5]], axis=1) for r in layer_results]
    ).reshape(layers, 2, SIDE, SIDE, 48, WIDTH)
    summed = scatter_grads(grads)
    gains_summed = lax.psum_scatter(
        lax.psum(jnp.stack([r[5] for r in layer_results]), "tensor"), "dp", scatter_dimension=2, tiled=True
    )
    pieces, start = [], 0
    for width in COLS:
        pieces.append(summed[:, :, start : start + width])
        start += width
    query, key, value, out, gate, up, down = pieces
    return (
        output,
        grad_residual,
        query,
        key,
        value,
        jnp.swapaxes(out, 1, 2),
        gate,
        up,
        jnp.swapaxes(down, 1, 2),
        gains_summed,
    )


def solution(mesh):
    return jax.shard_map(
        body,
        mesh=mesh,
        in_specs=(
            P(("dp", "tensor"), None),
            P(None, "dp", "tensor"),
            P(None, "dp", "tensor"),
            P(None, "dp", "tensor"),
            P(None, "tensor", "dp"),
            P(None, "dp", "tensor"),
            P(None, "dp", "tensor"),
            P(None, "tensor", "dp"),
            P(None, None, "dp"),
            P(("dp", "tensor"), None),
        ),
        out_specs=(
            P(("dp", "tensor"), None),
            P(("dp", "tensor"), None),
            P(None, "dp", "tensor"),
            P(None, "dp", "tensor"),
            P(None, "dp", "tensor"),
            P(None, "tensor", "dp"),
            P(None, "dp", "tensor"),
            P(None, "dp", "tensor"),
            P(None, "tensor", "dp"),
            P(None, None, "dp"),
        ),
        check_vma=False,
    )
```

time: 1250 us -> 975 us (0.78)
  waiting for transfers between devices: 507 us -> 338 us
  blocking collectives: 110 us -> 6.21 us
  Pallas kernels: 285 us -> 358 us
  matrix products: 155 us -> 108 us
  local copies, waits for them, and re-layouts: 113 us -> 82.4 us
    all_gather x1 -> x0, blocking collectives: 100 us -> none  [body(): all_gains = lax.all_gather(norm_gains, 'dp', axis=2, tiled=True)]
    all_gather x8 -> x4, waiting for transfers between devices: 146 us -> 51.7 us  [gat(): return lax.all_gather(r.astype(jnp.bfloat16), 'tensor', axis=0, tiled=True)]
    reduce_scatter x8 -> x4, waiting for transfers between devices: 141 us -> 67.8 us  [rs(): lax.psum_scatter(r.astype(jnp.bfloat16), 'tensor', scatter_dimension=0, t...]
    pallas_call x1, Pallas kernels: 127 us -> 201 us  [run_forward(): pl.pallas_call(forward_kernel, out_shape=(kept(2, 2, 768, WIDTH), kept(8,...]
    dot_general x54 -> x52, matrix products: 155 us -> 108 us  [the longest x26 57.4 us: tn(): lax.dot_general(left, right, (((0,), (0,)), ((), ())), preferred_element_...]
    slice x2, local copies, waits for them, and re-layouts: 49.9 us -> 18.3 us  [the longest x1 17.7 us: body(): W = w_kept[l]]
    unnamed x18 -> x10, waiting for transfers between devices: 219 us -> 218 us
  transfers between devices with their start and end apart: 17 -> 9, of which waited for: 14 -> 6; matrix products, arithmetic and copies ran while one was open for 13% -> 13% of each run, Pallas kernels for 23% -> 37%
where the time goes in v2:
time: 975 us; the launch traced here: 964 us
  Pallas kernels  358 us (37%)
  waiting for transfers between devices  338 us (35%)
  matrix products  108 us (11%)
  local copies, waits for them, and re-layouts  82.4 us (8%)
  other arithmetic  54.7 us (6%)
  between operations  15.5 us (2%)
    unnamed x10, waiting for transfers between devices  218 us
    pallas_call x1, Pallas kernels, run_forward(): pl.pallas_call(forward_kernel, out_shape=(kept(2, 2, 768, WIDTH), kept(8,...  201 us
    pallas_call x1, Pallas kernels, scatter_grads(): pl.pallas_call(scatter_kernel, out_shape=jax.ShapeDtypeStruct((layers, 48...  157 us
    reduce_scatter x4, waiting for transfers between devices, rs(): lax.psum_scatter(r.astype(jnp.bfloat16), 'tensor', scatter_dimension=0, t...  67.8 us
    dot_general x26, matrix products, tn(): lax.dot_general(left, right, (((0,), (0,)), ((), ())), preferred_element_...  57.4 us
    all_gather x4, waiting for transfers between devices, gat(): return lax.all_gather(r.astype(jnp.bfloat16), 'tensor', axis=0, tiled=True)  51.7 us
    concatenate x2, local copies, waits for them, and re-layouts, body(): jnp.concatenate([t.astype(jnp.bfloat16) for t in r[:5]], axis=1)  33.7 us
    dot_general x14, matrix products, nt(): lax.dot_general(left, right, (((1,), (1,)), ((), ())), preferred_element_...  32.7 us
  transfers between devices with their start and end apart: 9, of which 6 were waited for; matrix products, arithmetic and copies ran while one was open for 13% of the time, Pallas kernels for 37%

profile of v2, /device:TPU:0, one launch (start us, length us, event | category | flops | bytes accessed | tf_op | source)
XLA Modules:
  0.0 964.5 jit_solution(12395863110394033525)
XLA Ops:
  12.7 200.9 %forward.1 = (bf16[2,2,768,4224]{3,2,1,0:T(8,128)(2,1)}, f32[8,1536]{1,0:T(8,128)}, bf16[128,1536]{1,0:T(8,128)(2,1)}, bf16[2,512,1536]{2,1,0:T(8,128)(2,1)}, bf...) custom-call(bf16[2,48,4224]{2,1,0:T(8,128)(2,1)} %concatenate.40.sha, ...), custom_call_target="tpu_custom_call" | custom-call | tf_op jit(solution)/shard_map/forward/pallas_call | solution.py:717
  213.6 17.7 %fusion.248 = (bf16[1,2,768,4224]{3,2,1,0:T(8,128)(2,1)}, bf16[1,2,768,4224]{3,2,1,0:T(8,128)(2,1)}) fusion(bf16[2,2,768,4224]{3,2,1,0:T(8,128)(2,1)} %get-tuple-element.27), kind=kLoop, calls=%fused_computation.337 | loop fusion | bytes 51904512 | tf_op jit(solution)/shard_map/slice | solution.py:1069
  231.3 5.3 fusion.34
  236.6 4.9 fusion.15
  241.5 5.0 fusion.19
  248.1 21.6 %reduce-scatter.8.cloned.1.call-done = bf16[128,1536]{1,0:T(8,128)(2,1)} async-done(((bf16[512,1536]{1,0:T(8,128)(2,1)}), bf16[128,1536]{1,0:T(8,128)(2,1)}) %reduce-scatter.8.cloned.1.call-update) | async-done | bytes 393232 | tf_op jit(solution)/shard_map/reduce_scatter | solution.py:1061
  269.7 2.0 fusion.117
  272.8 25.8 %all-gather.7.cloned.1.call-done = bf16[512,1536]{1,0:T(8,128)(2,1)} async-done(((bf16[128,1536]{1,0:T(8,128)(2,1)}), bf16[512,1536]{1,0:T(8,128)(2,1)}) %all-gather.7.cloned.1.call-update) | async-done | bytes 1572880 | tf_op jit(solution)/shard_map/all_gather | solution.py:1059
  298.7 2.7 convolution_convert_fusion.13
  304.6 1.9 fusion.171
  311.6 2.4 fusion.127
  324.1 4.3 convolution_convert_fusion.9
  330.4 23.2 %reduce-scatter.10.cloned.1.call-done = bf16[128,1536]{1,0:T(8,128)(2,1)} async-done(((bf16[512,1536]{1,0:T(8,128)(2,1)}), bf16[128,1536]{1,0:T(8,128)(2,1)}) %reduce-scatter.10.cloned.1.call-update) | async-done | bytes 393232 | tf_op jit(solution)/shard_map/reduce_scatter | solution.py:1061
  353.6 2.1 fusion.118
  355.7 2.8 fusion.246
  358.6 25.9 %all-gather.9.cloned.1.call-done = bf16[512,1536]{1,0:T(8,128)(2,1)} async-done(((bf16[128,1536]{1,0:T(8,128)(2,1)}), bf16[512,1536]{1,0:T(8,128)(2,1)}) %all-gather.9.cloned.1.call-update) | async-done | bytes 1572880 | tf_op jit(solution)/shard_map/all_gather | solution.py:1059
  384.5 5.3 fusion.42
  389.8 4.9 fusion.10
  394.8 5.1 fusion.22
  401.9 23.1 %reduce-scatter.12.cloned.1.call-done = bf16[128,1536]{1,0:T(8,128)(2,1)} async-done(((bf16[512,1536]{1,0:T(8,128)(2,1)}), bf16[128,1536]{1,0:T(8,128)(2,1)}) %reduce-scatter.12.cloned.1.call-update) | async-done | bytes 393232 | tf_op jit(solution)/shard_map/reduce_scatter | solution.py:1061
  425.0 1.9 fusion.119
  427.5 2.2 fusion.241
  430.0 4.6 fusion.5
  437.2 3.5 fusion.1
  440.8 3.6 fusion
  444.4 3.6 fusion.8
  448.0 16.8 %copy.104 = bf16[1536,4224]{1,0:T(8,128)(2,1)} copy(bf16[1536,4224]{0,1:T(8,128)(2,1)} %fusion.8) | data formatting | bytes 25952256 | tf_op jit(solution)/shard_map/concatenate | solution.py:1108
  467.4 2.7 convolution_convert_fusion.12
  474.1 1.9 fusion.153
  476.3 1.9 fusion.150
  481.6 2.1 rev.14
  483.8 2.6 fusion.124
  495.5 4.3 convolution_convert_fusion.8
  499.9 4.4 fusion.6
  504.7 3.4 fusion.25
  508.1 3.5 fusion.4
  511.6 3.6 fusion.3
  515.3 3.6 fusion.2
  518.9 16.9 %copy.103 = bf16[1536,4224]{1,0:T(8,128)(2,1)} copy(bf16[1536,4224]{0,1:T(8,128)(2,1)} %fusion.2) | data formatting | bytes 25952256 | tf_op jit(solution)/shard_map/concatenate | solution.py:1108
  535.8 21.1 %pad_maximum_fusion.grads = bf16[2,2,4,4,48,4224]{5,4,3,2,1,0:T(8,128)(2,1)} fusion(bf16[1,2,4,4,48,4224]{5,4,3,2,1,0:T(8,128)(2,1)} %bitcast.294, bf16[1,2,4,4,48,4224]{5,4,3,2,1,0:T(8,128)(2,1)} %bitcast.295), kind=kLoop, calls=%fused_computation | loop fusion | flops 12976128 | bytes 51904512 | tf_op jit(solution)/shard_map/stack | solution.py:1107
  556.9 157.4 %scatter_grads.1 = f32[2,48,4224]{2,1,0:T(8,128)} custom-call(bf16[2,2,4,4,48,4224]{5,4,3,2,1,0:T(8,128)(2,1)} %pad_maximum_fusion.grads), custom_call_target="tpu_custom_call" | custom-call | tf_op jit(solution)/shard_map/scatter_grads/pallas_call | solution.py:986
  717.7 2.3 slice_bitcast_fusion
  720.0 1.9 fusion.122
  722.5 2.9 copy.114
  725.4 3.0 reshape.148
  729.1 1.9 fusion.107
  731.1 217.5 %reduce-scatter.16.cloned.1.call-done = f32[48,4]{1,0:T(8,128)} async-done(((f32[1536,4]{1,0:T(8,128)}), f32[48,4]{1,0:T(8,128)}) %reduce-scatter.16.cloned.1.call-update) | async-done | bytes 784
  949.5 6.2 psum.8
  (286 shorter events, 60.7 us)
Async XLA Ops:
  7.2 224.1 %all-gather.5.cloned.1.call-start = ((), (), s32[]{:S(2)}) async-start(), calls=%async_computation.5 | async-start | bytes 1966080 | tf_op jit(solution)/shard_map/all_gather | solution.py:1059
  7.9 261.8 %reduce-scatter.8.cloned.1.call-start = ((), (), s32[]{:S(2)}) async-start(), calls=%async_computation.6 | async-start | bytes 1966080 | tf_op jit(solution)/shard_map/reduce_scatter | solution.py:1061
  9.9 203.6 %copy-start.3 = (f32[512,4,96]{0,2,1:T(8,128)}, f32[512,4,96]{0,2,1:T(8,128)S(1)}, u32[]{:S(2)}) copy-start(f32[512,4,96]{0,2,1:T(8,128)S(1)} %tile.20) | copy-start | bytes 2359300
  236.6 4.9 copy-start.86
  236.6 4.9 copy-start.90
  236.6 4.9 copy-start.73
  241.5 5.1 copy-start.62
  246.6 25.2 %copy-start.16 = (bf16[128,1536]{1,0:T(8,128)(2,1)S(1)}, bf16[128,1536]{1,0:T(8,128)(2,1)}, u32[]{:S(2)}) copy-start(bf16[128,1536]{1,0:T(8,128)(2,1)} %param.19) | copy-start | bytes 1179652
  246.6 52.1 %all-gather.7.cloned.1.call-start = ((), (), s32[]{:S(2)}) async-start(), calls=%async_computation.7 | async-start | bytes 1966080 | tf_op jit(solution)/shard_map/all_gather | solution.py:1059
  248.1 24.6 %copy-start.64 = (f32[128]{0:T(128)}, f32[128]{0:T(128)S(1)}, u32[]{:S(2)}) copy-start(f32[128]{0:T(128)S(1)} %add_rsqrt_fusion.3) | copy-start | bytes 1540
  272.8 28.6 %copy-start.36 = (bf16[2,2,512,128]{3,2,1,0:T(8,128)(2,1)S(1)}, bf16[2,2,512,128]{3,2,1,0:T(8,128)(2,1)}, u32[]{:S(2)}) copy-start(bf16[2,2,512,128]{3,2,1,0:T(8,128)(2,1)} %get-tuple-element.33) | copy-start | bytes 1572868
  272.8 80.8 %reduce-scatter.10.cloned.1.call-start = ((), (), s32[]{:S(2)}) async-start(), calls=%async_computation.8 | async-start | bytes 1966080 | tf_op jit(solution)/shard_map/reduce_scatter | solution.py:1061
  301.4 7.9 copy-start.46
  303.5 6.7 copy-start.13
  303.5 7.0 copy-start.11
  304.3 6.5 copy-start.29
  304.6 6.2 copy-start.30
  314.0 5.3 copy-start.2
  314.0 5.3 copy-start.4
  319.3 4.8 copy-start.42
  328.5 56.0 %all-gather.9.cloned.1.call-start = ((), (), s32[]{:S(2)}) async-start(), calls=%async_computation.9 | async-start | bytes 1966080 | tf_op jit(solution)/shard_map/all_gather | solution.py:1059
  358.6 66.4 %reduce-scatter.12.cloned.1.call-start = ((), (), s32[]{:S(2)}) async-start(), calls=%async_computation.10 | async-start | bytes 1966080 | tf_op jit(solution)/shard_map/reduce_scatter | solution.py:1061
  389.8 5.0 copy-start.88
  389.8 5.0 copy-start.92
  389.8 5.0 copy-start.74
  394.8 5.2 copy-start.6
  394.8 5.9 copy-start.59
  399.9 67.5 %all-gather.11.cloned.1.call-start = ((), (), s32[]{:S(2)}) async-start(), calls=%async_computation.11 | async-start | bytes 1966080 | tf_op jit(solution)/shard_map/all_gather | solution.py:1059
  401.9 32.7 %copy-start.63 = (f32[128]{0:T(128)}, f32[128]{0:T(128)S(1)}, u32[]{:S(2)}) copy-start(f32[128]{0:T(128)S(1)} %add_rsqrt_fusion.1) | copy-start | bytes 1540
  429.7 290.2 %reduce-scatter.14.cloned.1.call-start = ((), (), s32[]{:S(2)}) async-start(), calls=%async_computation.12 | async-start | bytes 1966080 | tf_op jit(solution)/shard_map/reduce_scatter | solution.py:1061
  430.0 4.7 copy-start.79
  430.0 4.6 copy-start.80
  448.0 16.8 %copy-start.60 = (f32[1536]{0:T(1024)S(1)}, f32[1536]{0:T(1024)}, u32[]{:S(2)}) copy-start(f32[1536]{0:T(1024)} %get-tuple-element.53) | copy-start | bytes 18436
  467.4 4.8 copy-start.15
  470.1 9.0 copy-start.45
  473.3 6.7 copy-start.9
  473.3 7.1 copy-start.7
  474.1 6.6 copy-start.27
  476.3 4.4 copy-start.28
  499.9 4.8 copy-start.81
  504.3 444.2 %reduce-scatter.16.cloned.1.call-start = ((), (), s32[]{:S(2)}) async-start(), calls=%async_computation.13 | async-start | bytes 811008
  714.2 5.7 copy-start.53
  714.2 5.7 copy-start.65
  714.3 7.6 copy-start.61
  714.3 7.6 copy-start.58
  722.5 6.6 copy-start.5
  722.5 6.6 copy-start.18
  722.5 6.6 copy-start.35
  (55 other events, 138.3 us)
Sparse Core Ops, SparseCore 0:
  9.7 40.4 all-gather.4
  246.7 22.9 reduce-scatter.7
  272.9 25.7 all-gather.6
  328.6 24.9 reduce-scatter.9
  358.7 25.7 all-gather.8
  400.0 24.9 reduce-scatter.11
  429.8 25.7 all-gather.10
  504.4 24.9 reduce-scatter.13
  728.6 219.9 reduce-scatter.15

commit v3 on v2

--- a/solution.py
+++ b/solution.py
@@ -167,6 +167,7 @@
         self.over = [wire.slot() for _ in range(self.pieces)]
         self.passed = [wire.slot() for _ in range(self.pieces)]
         self.size = OWN // self.pieces
+        self.copies = []
 
     def rows(self, tensor, piece=None):
         start = pl.multiple_of(tensor * OWN, OWN)
@@ -180,8 +181,9 @@
         at, wire = self.at, self.wire
         own = at.tensor
         for piece in range(self.pieces):
-            wire.send(self.over[piece], self.rows(own, piece), self.rows(own, piece), at.above())
-        wire.send(self.near, self.rows(own), self.rows(own), at.twin())
+            block = self.rows(own, piece)
+            self.copies.append(wire.send(self.over[piece], block, block, at.above()))
+        self.copies.append(wire.send(self.near, self.rows(own), self.rows(own), at.twin()))
 
     def near_done(self):
         at = self.at
@@ -193,13 +195,15 @@
         for piece in range(self.pieces):
             block = self.rows(there, piece)
             wire.arrive(self.over[piece], block, at.above())
-            wire.send(self.passed[piece], block, block, at.twin())
+            self.copies.append(wire.send(self.passed[piece], block, block, at.twin()))
 
     def far_done(self):
         at = self.at
         there = (1 - at.z_lo) * 2 + 1 - at.core
         for piece in range(self.pieces):
             self.wire.arrive(self.passed[piece], self.rows(there, piece), at.twin())
+        for copy in self.copies:
+            self.wire.release(copy)
 
 
 class Collect:
@@ -332,6 +336,15 @@
 def weight(w_ref, layer, cols):
     value = w_ref[layer, :, :, cols]
     return value.reshape(MODEL, value.shape[-1])
+
+
+def turn_rows(source, target):
+    def tile(index, carry):
+        start = pl.multiple_of(index * 256, 256)
+        target[pl.ds(start, 256), :] = source[:, pl.ds(start, 256)].T
+        return carry
+
+    lax.fori_loop(0, MODEL // 256, tile, 0)
 
 
 def gather_job(wire, at, full, layer, group):
@@ -606,6 +619,8 @@
     a_ref,
     x_ref,
     h_ref,
+    n1_turned,
+    n2_turned,
     part,
     help_ref,
     near_ref,
@@ -639,6 +654,7 @@
             wire, at, part, help_ref.at[slot], near_ref.at[slot], over_ref.at[slot]
         )
 
+    turning = [None, None]
     for layer in range(2):
         n1[layer, own, :] = normed(x_ref[layer], gains[pl.ds(2 * layer, 1), :])
         spread = Spread(wire, at, n1.at[layer])
@@ -651,7 +667,7 @@
         spread.pass_on()
         spread.far_done()
         project_heads(layer, there, *heads)
-        for source, target in ((n1, n1_kept), (q_ref, q_kept), (k_ref, k_kept), (v_ref, v_kept)):
+        for source, target in ((q_ref, q_kept), (k_ref, k_kept), (v_ref, v_kept)):
             local.start(source.at[layer], target.at[layer])
         gather.step()
         attend(layer, q_ref, k_ref, v_ref, p_ref, o_ref)
@@ -663,6 +679,10 @@
         out_partial(layer, here, o_ref, w, part)
         collect.own_ready()
         collect.send_over()
+        if layer == 1:
+            local.wait(turning[0])
+        turn_rows(n1.at[layer], n1_turned)
+        turning[0] = local.start(n1_turned, n1_kept.at[layer])
         gather.step()
         h_ref[layer] = x_ref[layer] + collect.result()
         n2[layer, own, :] = normed(h_ref[layer], gains[pl.ds(2 * layer + 1, 1), :])
@@ -676,7 +696,6 @@
         spread.far_done()
         hidden_rows(layer, there, n2, w, g_ref, u_ref, a_ref)
         for source, target in (
-            (n2, n2_kept),
             (h_ref, h_kept),
             (g_ref, g_kept),
             (u_ref, u_kept),
@@ -689,6 +708,10 @@
         down_partial(layer, here, a_ref, w, part)
         collect.own_ready()
         collect.send_over()
+        if layer == 1:
+            local.wait(turning[1])
+        turn_rows(n2.at[layer], n2_turned)
+        turning[1] = local.start(n2_turned, n2_kept.at[layer])
         gather.step()
         total = h_ref[layer] + collect.result()
         if layer == 0:
@@ -720,8 +743,8 @@
             kept(2, 2, 768, WIDTH),
             kept(8, MODEL, kind=float32),
             kept(OWN, MODEL),
-            kept(2, SEQ_ROWS, MODEL),
-            kept(2, SEQ_ROWS, MODEL),
+            kept(2, MODEL, SEQ_ROWS),
+            kept(2, MODEL, SEQ_ROWS),
             kept(2, 4, SEQ_ROWS, 128),
             kept(2, 2, SEQ_ROWS, 128),
             kept(2, 2, SEQ_ROWS, 128),
@@ -749,6 +772,8 @@
             held(2, SEQ_ROWS, 1024),
             held(2, OWN, MODEL, kind=float32),
             held(2, OWN, MODEL, kind=float32),
+            held(MODEL, SEQ_ROWS),
+            held(MODEL, SEQ_ROWS),
             held(SEQ_ROWS, MODEL),
             held(2, OWN, MODEL),
             held(2, OWN, MODEL),
@@ -765,40 +790,47 @@
     )(shard, gains_placed, tokens, cosine, sine)
 
 
-HALVES = (((0, 1024), (1024, 2048)), ((2048, 3072), (3072, 4224)))
-
-
-def add_into(target, terms, rows_lead):
+JOBS = (
+    (((3200, 3456), (3456, 3712)), ((3712, 3968), (3968, 4224))),
+    (((1152, 1408), (1408, 1664)), ((1664, 1920), (1920, 2176))),
+    (((2176, 2432), (2432, 2688)), ((2688, 2944), (2944, 3200))),
+    (((0, 256), (256, 512)), ((512, 768), (768, 1152))),
+)
+JOB_WIDTH = 1152
+SETS = 2
+
+
+def add_rows(target, terms):
+    lead = target.shape[:-2]
+
     def step(index, carry):
-        lead, start = index // 3, pl.multiple_of((index % 3) * 16, 16)
-        window = (lead, pl.ds(start, 16)) if rows_lead else (pl.ds(start, 16),)
+        window = ()
+        if lead:
+            window = (index // lead[1], index % lead[1])
         total = None
         for term in terms:
-            value = term[window].astype(jnp.float32)
+            value = term[window + (slice(None), slice(None))].astype(jnp.float32)
             total = value if total is None else total + value
-        target[window] = total.astype(target.dtype)
+        target[window + (slice(None), slice(None))] = total.astype(target.dtype)
         return carry
 
-    lax.fori_loop(0, 3 * (SIDE if rows_lead else 1), step, 0)
-
-
-def scatter_job(wire, at, grads, layer, z_data, job, bufs, finish):
-    one, two_up, two_down, small_one, small_up, small_down = bufs
-
-    def cut(cols):
-        return pl.ds(cols[0], cols[1] - cols[0])
-
+    lax.fori_loop(0, math.prod(lead), step, 0)
+
+
+def scatter_job(wire, local, at, grads, layer, group, bufs, finish):
+    one, two_up, two_down, small_one, small_up, small_down, near_side, near_own = bufs
+    base = group[0][0][0]
     parts = []
-    for first, second, (left, right) in (("y", "x", HALVES[0]), ("x", "y", HALVES[1])):
+    for (first, second), (left, right) in zip((("y", "x"), ("x", "y")), group):
 
         def region(step, cols, second=second):
             if second == "x":
-                return grads.at[layer, z_data, shift(at.x, step), :, :, cut(cols)]
-            return grads.at[layer, z_data, :, shift(at.y, step), :, cut(cols)]
+                return grads.at[layer, :, shift(at.x, step), :, :, cut(cols)]
+            return grads.at[layer, :, :, shift(at.y, step), :, cut(cols)]
 
         def mine(step, cols, first=first):
             place = at.y if first == "y" else at.x
-            return two_up.at[job, shift(place, step), :, cut(cols)]
+            return two_up.at[:, shift(place, step), :, inside(cols)]
 
         parts.append(
             dict(
@@ -809,202 +841,562 @@
                 whole=(left[0], right[1]),
                 region=region,
                 mine=mine,
-                far={s: wire.slot() for s in (1, -1)},
-                raw={s: wire.slot() for s in (1, -1)},
-                sum={s: wire.slot() for s in (1, -1)},
-                far2={s: wire.slot() for s in (1, -1)},
-                raw2={s: wire.slot() for s in (1, -1)},
-                sum2={s: wire.slot() for s in (1, -1)},
+                **{
+                    name: {s: wire.slot() for s in (1, -1)}
+                    for name in ("far", "raw", "sum", "far2", "raw2", "sum2")
+                },
             )
         )
 
+    def inside(cols):
+        return pl.ds(cols[0] - base, cols[1] - cols[0])
+
     def half(part, step):
         return part["left"] if step == 1 else part["right"]
 
     def other(part, step):
         return part["right"] if step == 1 else part["left"]
 
-    def landing(step):
-        return two_up if step == 1 else two_down
-
-    def small_landing(step):
-        return small_up if step == 1 else small_down
-
+    def big(ref, cols):
+        return ref.at[:, :, :, inside(cols)]
+
+    def small(ref, cols):
+        return ref.at[:, :, inside(cols)]
+
+    copies = []
+    near = {}
     for part in parts:
         for step in (1, -1):
             cols = half(part, step)
-            wire.send(
-                part["far"][step],
-                part["region"](2, cols),
-                one.at[job, :, :, cut(cols)],
-                at.beside(part["second"], step),
+            target = at.beside(part["second"], step)
+            copies.append(
+                wire.send(part["far"][step], part["region"](2, cols), big(one, cols), target)
             )
-    for part in parts:
+    for number, part in enumerate(parts):
         for step in (1, -1):
             cols = other(part, step)
-            wire.send(
-                part["raw"][step],
-                part["region"](step, cols),
-                landing(step).at[job, :, :, cut(cols)],
-                at.beside(part["second"], step),
+            landing = two_up if step == 1 else two_down
+            target = at.beside(part["second"], step)
+            copies.append(
+                wire.send(part["raw"][step], part["region"](step, cols), big(landing, cols), target)
             )
+            cols = half(part, step)
+            near[number, step] = local.start(part["region"](step, cols), big(near_side, cols))
+        cols = part["whole"]
+        near[number, 0] = local.start(part["region"](0, cols), big(near_own, cols))
     yield
     for step in (1, -1):
-        for part in parts:
+        for number, part in enumerate(parts):
             cols = half(part, step)
             target = at.beside(part["second"], step)
-            piece = one.at[job, :, :, cut(cols)]
+            piece = big(one, cols)
+            local.wait(near[number, step])
             wire.arrive(part["far"][step], piece, target)
-            add_into(piece, (piece, part["region"](step, cols)), True)
-            wire.send(part["sum"][step], piece, landing(step).at[job, :, :, cut(cols)], target)
+            add_rows(piece, (piece, big(near_side, cols)))
+            landing = two_up if step == 1 else two_down
+            copies.append(wire.send(part["sum"][step], piece, big(landing, cols), target))
     yield
-    for part in parts:
+    for number, part in enumerate(parts):
+        local.wait(near[number, 0])
         for step in (1, -1):
             target = at.beside(part["second"], step)
-            cols = other(part, step)
-            wire.arrive(part["raw"][step], landing(step).at[job, :, :, cut(cols)], target)
+            landing = two_up if step == 1 else two_down
+            for name, cols in (("raw", other(part, step)), ("sum", half(part, step))):
+                wire.arrive(part[name][step], big(landing, cols), target)
+        cols = part["whole"]
+        add_rows(big(two_up, cols), (big(near_own, cols), big(two_up, cols), big(two_down, cols)))
+        for step in (1, -1):
+            target = at.beside(part["first"], step)
             cols = half(part, step)
-            wire.arrive(part["sum"][step], landing(step).at[job, :, :, cut(cols)], target)
-        cols = part["whole"]
-        piece = two_up.at[job, :, :, cut(cols)]
-        add_into(
-            piece,
-            (part["region"](0, cols), piece, two_down.at[job, :, :, cut(cols)]),
-            True,
-        )
-        for step in (1, -1):
-            cols = half(part, step)
-            target = at.beside(part["first"], step)
-            wire.send(
-                part["far2"][step], part["mine"](2, cols), small_one.at[job, :, cut(cols)], target
+            copies.append(
+                wire.send(part["far2"][step], part["mine"](2, cols), small(small_one, cols), target)
             )
             cols = other(part, step)
-            wire.send(
-                part["raw2"][step],
-                part["mine"](step, cols),
-                small_landing(step).at[job, :, cut(cols)],
-                target,
+            landing = small_up if step == 1 else small_down
+            copies.append(
+                wire.send(part["raw2"][step], part["mine"](step, cols), small(landing, cols), target)
             )
     yield
     for step in (1, -1):
         for part in parts:
             cols = half(part, step)
             target = at.beside(part["first"], step)
-            piece = small_one.at[job, :, cut(cols)]
+            piece = small(small_one, cols)
             wire.arrive(part["far2"][step], piece, target)
-            add_into(piece, (piece, part["mine"](step, cols)), False)
-            wire.send(
-                part["sum2"][step], piece, small_landing(step).at[job, :, cut(cols)], target
-            )
+            own = part["mine"](step, cols)
+            for z_hi in range(2):
+                add_rows(piece.at[z_hi], (piece.at[z_hi], own.at[z_hi]))
+            landing = small_up if step == 1 else small_down
+            copies.append(wire.send(part["sum2"][step], piece, small(landing, cols), target))
     yield
     for part in parts:
         for step in (1, -1):
             target = at.beside(part["first"], step)
-            cols = other(part, step)
-            wire.arrive(part["raw2"][step], small_landing(step).at[job, :, cut(cols)], target)
-            cols = half(part, step)
-            wire.arrive(part["sum2"][step], small_landing(step).at[job, :, cut(cols)], target)
+            landing = small_up if step == 1 else small_down
+            for name, cols in (("raw2", other(part, step)), ("sum2", half(part, step))):
+                wire.arrive(part[name][step], small(landing, cols), target)
         cols = part["whole"]
         finish(
-            cut(cols),
-            (
-                part["mine"](0, cols),
-                small_up.at[job, :, cut(cols)],
-                small_down.at[job, :, cut(cols)],
-            ),
+            cols,
+            [
+                [
+                    ref.at[z_hi]
+                    for ref in (part["mine"](0, cols), small(small_up, cols), small(small_down, cols))
+                ]
+                for z_hi in (1 - at.z_hi, at.z_hi)
+            ],
         )
+    for copy in copies:
+        wire.release(copy)
     yield
 
 
-def scatter_kernel(
+class Scatter:
+    def __init__(self, wire, local, at, grads, summed, sets, leaving, landed, credits):
+        self.wire, self.local, self.at, self.grads = wire, local, at, grads
+        self.summed, self.leaving, self.landed, self.credits = summed, leaving, landed, credits
+        self.groups = [(layer, group) for layer in (1, 0) for group in JOBS]
+        self.last = []
+        self.jobs = []
+        for index, (layer, group) in enumerate(self.groups):
+            bufs = tuple(ref.at[index % SETS] for ref in sets)
+            self.jobs.append(
+                scatter_job(
+                    wire, local, at, grads, layer, group, bufs, self.finisher(index, layer, group)
+                )
+            )
+        order = [(0, 0), (0, 1)]
+        count = len(self.jobs)
+        for index in range(count):
+            order += [(index + 1, 0), (index, 2), (index, 3), (index + 1, 1), (index, 4)]
+            order += [(index - 1, 5)]
+        order += [(count - 1, 5)]
+        self.order = [pair for pair in order if 0 <= pair[0] < count]
+        self.done = 0
+        self.ready = 0
+
+    def finisher(self, index, layer, group):
+        wire, at = self.wire, self.at
+        base = group[0][0][0]
+
+        def finish(cols, terms):
+            theirs, own = terms
+            window = pl.ds(cols[0] - base, cols[1] - cols[0])
+            piece = self.leaving.at[index, :, window]
+            add_rows(piece, theirs)
+            slot = wire.slot()
+            landing = self.landed.at[index, :, window]
+            wire.send(slot, piece, landing, at.across())
+            target = self.summed.at[layer, :, cut(cols)]
+            add_rows(target, own)
+            self.last.append((index, slot, landing, target))
+
+        return finish
+
+    def step(self, count=1):
+        at = self.at
+        for _ in range(count):
+            if self.done == len(self.order):
+                return
+            index, stage = self.order[self.done]
+            if index >= self.ready:
+                return
+            self.done += 1
+            ways = [(axis, step) for axis in ("x", "y") for step in (1, -1)]
+            if stage == 5:
+                for job, slot, landing, target in self.last:
+                    if job == index:
+                        self.wire.arrive(slot, landing, at.across())
+                        add_rows(target, (target, landing))
+                continue
+            if stage == 0 and index >= SETS:
+                for number in range(4):
+                    pl.semaphore_wait(self.credits.at[number], 1)
+            next(self.jobs[index])
+            if stage == 4 and index + SETS < len(self.jobs):
+                for number, (axis, step) in enumerate(ways):
+                    pl.semaphore_signal(
+                        self.credits.at[number],
+                        inc=1,
+                        device_id=at.beside(axis, step),
+                        device_id_type=MESH_IDS,
+                    )
+
+
+def norm_backward(rows_in, gain, grad_normed):
+    inverse = lax.rsqrt(jnp.mean(rows_in * rows_in, axis=-1, keepdims=True) + norm_eps)
+    scaled = rows_in * inverse
+    grad_gain = jnp.sum(grad_normed * scaled, axis=0, keepdims=True)
+    grad_scaled = grad_normed * gain
+    grad_input = inverse * (
+        grad_scaled - scaled * jnp.mean(grad_scaled * scaled, axis=-1, keepdims=True)
+    )
+    return grad_input, grad_gain
+
+
+def hidden_back(rows, dm, w, g_ref, u_ref, dgu):
+    left = dm[rows, :]
+
+    def tile(index, carry):
+        start = pl.multiple_of(index * 256, 256)
+        grad = nn(left, weight(w, 0, pl.ds(DOWN[0] + start, 256)))
+        gate = g_ref[rows, pl.ds(start, 256)].astype(jnp.float32)
+        up = u_ref[rows, pl.ds(start, 256)].astype(jnp.float32)
+        sigma = 1.0 / (1.0 + jnp.exp(-gate))
+        dgu[rows, pl.ds(start, 256)] = (
+            grad * up * sigma * (1.0 + gate * (1.0 - sigma))
+        ).astype(jnp.bfloat16)
+        dgu[rows, pl.ds(1024 + start, 256)] = (grad * gate * sigma).astype(jnp.bfloat16)
+        return carry
+
+    lax.fori_loop(0, 4, tile, 0)
+
+
+def rows_partial(rows, left_ref, w, cols, part):
+    left = left_ref[rows, :]
+    for half in range(2):
+
+        def tile(index, carry, half=half):
+            start = pl.multiple_of(index * 256, 256)
+            right = w[0, half, pl.ds(start, 256), cut(cols)]
+            part[rows, pl.ds(pl.multiple_of(half * 768 + start, 256), 256)] = nt(
+                left, right
+            ).astype(jnp.bfloat16)
+            return carry
+
+        lax.fori_loop(0, 3, tile, 0)
+
+
+def attend_back(q_ref, k_ref, v_ref, p_ref, do_ref, dk_ref, dv_ref, cosine, sine, dqkv):
+    dk_ref[...] = jnp.zeros_like(dk_ref)
+    dv_ref[...] = jnp.zeros_like(dv_ref)
+    for block in range(4):
+        rows = pl.ds(block * 128, 128)
+        keys = pl.ds(0, (block + 1) * 128)
+        queries = []
+        for head in range(2):
+            both = (2 * head, 2 * head + 1)
+            shares = jnp.concatenate([p_ref[h, rows, keys] for h in both], axis=0)
+            pair = jnp.concatenate([q_ref[h, rows, :] for h in both], axis=0)
+            grad = jnp.concatenate([do_ref[h, rows, :] for h in both], axis=0)
+            wide = shares.astype(jnp.float32)
+            grad_shares = nt(grad, v_ref[head, keys, :])
+            inner = jnp.sum(grad_shares * wide, axis=-1, keepdims=True)
+            grad_scores = (wide * (grad_shares - inner)).astype(jnp.bfloat16)
+            grad_pair = nn(grad_scores, k_ref[head, keys, :]) * SCALING
+            queries += [grad_pair[:128], grad_pair[128:]]
+            dk_ref[head, :, keys] += nn(pair.T, grad_scores)
+            dv_ref[head, :, keys] += nn(grad.T, shares)
+        grad_rows = side_by_side(queries)
+        turned = grad_rows * cosine[rows, :] - swap_halves(grad_rows) * sine[rows, :]
+        dqkv[rows, pl.ds(0, 384)] = turned.astype(jnp.bfloat16)
+    both = side_by_side(
+        [dk_ref[0].T * SCALING, dk_ref[1].T * SCALING, dv_ref[0].T, dv_ref[1].T]
+    )
+    turned = both * cosine[...] - swap_halves(both) * sine[...]
+    lane = lax.broadcasted_iota(jnp.int32, both.shape, 1)
+    dqkv[:, pl.ds(384, 384)] = jnp.where(lane < 192, turned, both).astype(jnp.bfloat16)
+
+
+def backward_kernel(
+    gains,
+    grad_out,
+    tokens,
+    cosine,
+    sine,
+    x_second,
+    h_ref,
+    w_kept,
+    n1_kept,
+    n2_kept,
+    q_kept,
+    k_kept,
+    v_kept,
+    p_kept,
+    o_kept,
+    g_kept,
+    u_kept,
+    a_kept,
+    input_grad,
+    summed,
+    gains_grad,
     grads,
-    out,
+    w,
+    n1_turned,
+    n2_turned,
+    q_ref,
+    k_ref,
+    v_ref,
+    p_ref,
+    o_ref,
+    g_ref,
+    u_ref,
+    a_ref,
+    dm,
+    turned,
+    dgu,
+    do_ref,
+    dk_ref,
+    dv_ref,
+    dqkv,
+    dx,
+    part,
+    help_ref,
+    near_ref,
+    over_ref,
+    staged,
     one,
     two_up,
     two_down,
     small_one,
     small_up,
     small_down,
+    near_side,
+    near_own,
     leaving,
     landed,
+    gains_landing,
     send_sems,
     recv_sems,
+    local_sems,
+    credits,
 ):
     at = Place()
     at.greet()
     wire = Wire(send_sems, recv_sems)
-    layers = grads.shape[0]
-    bufs = (one, two_up, two_down, small_one, small_up, small_down)
-    jobs = []
-    for layer in range(layers):
-        across = [wire.slot() for _ in range(2)]
-        places = (pl.ds(0, 2048), pl.ds(2048, WIDTH - 2048))
-        turn = iter(range(2))
-
-        def finish_other(cols, terms, layer=layer, across=across, turn=turn):
-            piece = leaving.at[layer, :, cols]
-            add_into(piece, terms, False)
-            wire.send(
-                across[next(turn)], piece, landed.at[layer, :, cols], at.across()
+    local = Local(local_sems)
+    sets = (one, two_up, two_down, small_one, small_up, small_down, near_side, near_own)
+    scatter = Scatter(wire, local, at, grads, summed, sets, leaving, landed, credits)
+    own = pl.ds(pl.multiple_of(at.tensor * OWN, OWN), OWN)
+    here, there = chip_rows(at.z_lo), chip_rows(1 - at.z_lo)
+    turn = 0
+
+    def collector():
+        nonlocal turn
+        turn += 1
+        slot = turn % 2
+        return Collect(
+            wire, at, part, help_ref.at[slot], near_ref.at[slot], over_ref.at[slot]
+        )
+
+    loads = {}
+
+    def load(layer, names):
+        pairs = dict(
+            n1=(n1_kept, n1_turned),
+            n2=(n2_kept, n2_turned),
+            q=(q_kept, q_ref),
+            k=(k_kept, k_ref),
+            v=(v_kept, v_ref),
+            p=(p_kept, p_ref),
+            o=(o_kept, o_ref),
+            g=(g_kept, g_ref),
+            u=(u_kept, u_ref),
+            a=(a_kept, a_ref),
+        )
+        columns = dict(down=DOWN, gu=(GATE[0], UP[1]), out=OUT, qkv=QKV)
+        for name in names:
+            if name in columns:
+                cols = cut(columns[name])
+                loads[name] = local.start(w_kept.at[layer, :, :, cols], w.at[0, :, :, cols])
+            else:
+                kept, held = pairs[name]
+                loads[name] = local.start(kept.at[layer], held)
+
+    def ready(*names):
+        for name in names:
+            local.wait(loads.pop(name))
+
+    mlp_names = ("down", "g", "u", "gu", "a", "n2")
+    attn_names = ("out", "v", "p", "k", "q", "qkv", "o", "n1")
+    load(1, mlp_names)
+    load(1, attn_names)
+    staging = [None, None]
+    tiles = 0
+
+    def keep_grads(layer, left, right_ref, start, width, column):
+        nonlocal tiles
+        for tile in range(0, width, 256):
+            size = min(256, width - tile)
+            slot = tiles % 2
+            tiles += 1
+            if staging[slot] is not None:
+                local.wait(staging[slot])
+            product = nn(left[...], right_ref[:, pl.ds(start + tile, size)])
+            staged[slot, :, :, :, :, pl.ds(0, size)] = product.astype(jnp.bfloat16).reshape(
+                2, SIDE, SIDE, 48, size
             )
-
-        turn_own = iter(range(2))
-
-        def finish_own(cols, terms, layer=layer, across=across, turn=turn_own):
-            piece = landed.at[layer, :, cols]
-            wire.arrive(across[next(turn)], piece, at.across())
-            add_into(out.at[layer, :, cols], terms + (piece,), False)
-
-        jobs.append(
-            scatter_job(
-                wire, at, grads, layer, 1 - at.z_hi, 2 * layer, bufs, finish_other
+            staging[slot] = local.start(
+                staged.at[slot, :, :, :, :, pl.ds(0, size)],
+                grads.at[layer, :, :, :, :, pl.ds(column + tile, size)],
             )
+
+    def grads_kept():
+        for slot in range(2):
+            if staging[slot] is not None:
+                local.wait(staging[slot])
+                staging[slot] = None
+        scatter.ready += 1
+
+    gains_grad[...] = jnp.zeros_like(gains_grad)
+    dx[0] = grad_out[...].astype(jnp.float32)
+    for layer in (1, 0):
+        dm[0, own, :] = dx[0].astype(jnp.bfloat16)
+        spread = Spread(wire, at, dm.at[0])
+        spread.start()
+        spread.near_done()
+        ready("down", "g", "u")
+        hidden_back(here, dm.at[0], w, g_ref, u_ref, dgu)
+        if layer == 0:
+            scatter.step()
+        spread.pass_on()
+        spread.far_done()
+        hidden_back(there, dm.at[0], w, g_ref, u_ref, dgu)
+        collect = collector()
+        ready("gu")
+        rows_partial(there, dgu, w, (GATE[0], UP[1]), part)
+        collect.other_ready()
+        rows_partial(here, dgu, w, (GATE[0], UP[1]), part)
+        collect.own_ready()
+        collect.send_over()
+        if layer == 0:
+            scatter.step(2)
+        turn_rows(dm.at[0], turned)
+        ready("a")
+        keep_grads(layer, turned, a_ref, 0, 1024, DOWN[0])
+        grads_kept()
+        scatter.step()
+        if layer == 1:
+            total = collect.result()
+        ready("n2")
+        keep_grads(layer, n2_turned, dgu, 0, 1024, GATE[0])
+        grads_kept()
+        if layer == 0:
+            total = collect.result()
+        normed_grad, gain_row = norm_backward(
+            h_ref[layer], gains[pl.ds(2 * layer + 1, 1), :], total
         )
-        jobs.append(
-            scatter_job(wire, at, grads, layer, at.z_hi, 2 * layer + 1, bufs, finish_own)
+        gains_grad[pl.ds(2 * layer + 1, 1), :] = gain_row
+        dx[1] = dx[0] + normed_grad
+        dm[1, own, :] = dx[1].astype(jnp.bfloat16)
+        spread = Spread(wire, at, dm.at[1])
+        spread.start()
+        scatter.step(2)
+        keep_grads(layer, n2_turned, dgu, 1024, 1024, UP[0])
+        grads_kept()
+        if layer == 1:
+            load(0, mlp_names)
+        ready("out")
+        spread.near_done()
+
+        def heads_back(rows):
+            grad = nn(dm[1, rows, :], weight(w, 0, cut(OUT)))
+            for head in range(4):
+                do_ref[head, rows, :] = head_of(grad, head * HD).astype(jnp.bfloat16)
+
+        heads_back(here)
+        spread.pass_on()
+        spread.far_done()
+        heads_back(there)
+        ready("v", "p", "k", "q")
+        attend_back(
+            q_ref, k_ref, v_ref, p_ref, do_ref, dk_ref, dv_ref, cosine, sine, dqkv
         )
-
-    def advance(index):
-        if index < len(jobs):
-            next(jobs[index])
-
-    advance(0)
-    advance(0)
-    for index in range(len(jobs)):
-        advance(index + 1)
-        advance(index)
-        advance(index)
-        advance(index + 1)
-        advance(index)
+        scatter.step()
+        collect = collector()
+        ready("qkv")
+        rows_partial(there, dqkv, w, QKV, part)
+        collect.other_ready()
+        rows_partial(here, dqkv, w, QKV, part)
+        collect.own_ready()
+        collect.send_over()
+        turn_rows(dm.at[1], turned)
+        ready("o", "n1")
+        keep_grads(layer, turned, o_ref, 0, 384, OUT[0])
+        keep_grads(layer, n1_turned, dqkv, 0, 768, QKV[0])
+        grads_kept()
+        if layer == 1:
+            load(0, attn_names)
+        scatter.step(2)
+        total = collect.result()
+        rows_in = tokens[...].astype(jnp.float32) if layer == 0 else x_second[...]
+        normed_grad, gain_row = norm_backward(rows_in, gains[pl.ds(2 * layer, 1), :], total)
+        gains_grad[pl.ds(2 * layer, 1), :] = gain_row
+        dx[0] = dx[1] + normed_grad
+    input_grad[...] = dx[0]
+    rounds = sum_small(wire, at, gains_grad, gains_landing, True)
+    for _ in rounds:
+        scatter.step()
+    while scatter.done < len(scatter.order):
+        scatter.step()
+    local.drain()
     wire.drain()
 
 
-def scatter_grads(grads):
-    layers = grads.shape[0]
-    slots = layers * 50
-    jobs = 2 * layers
+def run_backward(gains, grad_out, tokens, cosine, sine, x_second, h, kept):
+    def held(*shape, kind=jnp.bfloat16):
+        return pltpu.VMEM(shape, kind)
+
+    vmem = pl.BlockSpec(memory_space=pltpu.VMEM)
+    hbm = pl.BlockSpec(memory_space=pl.ANY)
+    float32 = jnp.float32
+    wires = 8 * 26 + 9 + 8 * 5 + 4
     return pl.pallas_call(
-        scatter_kernel,
-        out_shape=jax.ShapeDtypeStruct((layers, 48, WIDTH), jnp.float32),
-        in_specs=[pl.BlockSpec(memory_space=pltpu.VMEM)],
-        out_specs=pl.BlockSpec(memory_space=pltpu.VMEM),
+        backward_kernel,
+        out_shape=(
+            jax.ShapeDtypeStruct((OWN, MODEL), float32),
+            jax.ShapeDtypeStruct((2, 48, WIDTH), float32),
+            jax.ShapeDtypeStruct((8, MODEL), float32),
+            jax.ShapeDtypeStruct((2, 2, SIDE, SIDE, 48, WIDTH), jnp.bfloat16),
+        ),
+        in_specs=[vmem] * 7 + [hbm] * len(kept),
+        out_specs=(vmem, vmem, vmem, hbm),
         scratch_shapes=[
-            pltpu.VMEM((jobs, SIDE, 48, WIDTH), jnp.bfloat16),
-            pltpu.VMEM((jobs, SIDE, 48, WIDTH), jnp.bfloat16),
-            pltpu.VMEM((jobs, SIDE, 48, WIDTH), jnp.bfloat16),
-            pltpu.VMEM((jobs, 48, WIDTH), jnp.bfloat16),
-            pltpu.VMEM((jobs, 48, WIDTH), jnp.bfloat16),
-            pltpu.VMEM((jobs, 48, WIDTH), jnp.bfloat16),
-            pltpu.VMEM((layers, 48, WIDTH), jnp.bfloat16),
-            pltpu.VMEM((layers, 48, WIDTH), jnp.bfloat16),
-            pltpu.SemaphoreType.DMA((slots,)),
-            pltpu.SemaphoreType.DMA((slots,)),
+            held(1, 2, 768, WIDTH),
+            held(MODEL, SEQ_ROWS),
+            held(MODEL, SEQ_ROWS),
+            held(4, SEQ_ROWS, 128),
+            held(2, SEQ_ROWS, 128),
+            held(2, SEQ_ROWS, 128),
+            held(4, SEQ_ROWS, SEQ_ROWS),
+            held(SEQ_ROWS, 384),
+            held(SEQ_ROWS, 1024, kind=KEEP),
+            held(SEQ_ROWS, 1024, kind=KEEP),
+            held(SEQ_ROWS, 1024),
+            held(2, SEQ_ROWS, MODEL),
+            held(MODEL, SEQ_ROWS),
+            held(SEQ_ROWS, 2048),
+            held(4, SEQ_ROWS, 128),
+            held(2, 128, SEQ_ROWS, kind=float32),
+            held(2, 128, SEQ_ROWS, kind=float32),
+            held(SEQ_ROWS, 768),
+            held(2, OWN, MODEL, kind=float32),
+            held(SEQ_ROWS, MODEL),
+            held(2, OWN, MODEL),
+            held(2, OWN, MODEL),
+            held(2, OWN, MODEL),
+            held(2, 2, SIDE, SIDE, 48, 256),
+            held(SETS, 2, SIDE, 48, JOB_WIDTH),
+            held(SETS, 2, SIDE, 48, JOB_WIDTH),
+            held(SETS, 2, SIDE, 48, JOB_WIDTH),
+            held(SETS, 2, 48, JOB_WIDTH),
+            held(SETS, 2, 48, JOB_WIDTH),
+            held(SETS, 2, 48, JOB_WIDTH),
+            held(SETS, 2, SIDE, 48, JOB_WIDTH),
+            held(SETS, 2, SIDE, 48, JOB_WIDTH),
+            held(8, 48, JOB_WIDTH),
+            held(8, 48, JOB_WIDTH),
+            held(9, 8, MODEL, kind=float32),
+            pltpu.SemaphoreType.DMA((wires,)),
+            pltpu.SemaphoreType.DMA((wires,)),
+            pltpu.SemaphoreType.DMA((28 + 40 + 48,)),
+            pltpu.SemaphoreType.REGULAR((4,)),
         ],
         compiler_params=pltpu.CompilerParams(
-            collective_id=1, has_side_effects=True, vmem_limit_bytes=60 * 2**20
+            collective_id=1, has_side_effects=True, vmem_limit_bytes=62 * 2**20
         ),
-        name="scatter_grads",
-    )(grads)
+        name="backward",
+    )(gains, grad_out, tokens, cosine, sine, x_second, h, *kept)
 
 
 def pack_rows(arrays):
@@ -1012,17 +1404,6 @@
     turned_out = jnp.swapaxes(out, 1, 2)
     turned_down = jnp.swapaxes(down, 1, 2)
     return jnp.concatenate([query, key, value, turned_out, gate, up, turned_down], axis=2)
-
-
-def norm_backward(rows_in, gain, grad_normed):
-    inverse = lax.rsqrt(jnp.mean(rows_in * rows_in, axis=-1, keepdims=True) + norm_eps)
-    scaled = rows_in * inverse
-    grad_gain = jnp.sum(grad_normed * scaled, axis=0)
-    grad_scaled = grad_normed * gain
-    grad_input = inverse * (
-        grad_scaled - scaled * jnp.mean(grad_scaled * scaled, axis=-1, keepdims=True)
-    )
-    return (grad_input, grad_gain)
 
 
 def body(
@@ -1037,7 +1418,6 @@
     norm_gains,
     grad_out,
 ):
-    layers = 2
     packed = pack_rows(
         (query_weight, key_weight, value_weight, out_weight, gate_weight, up_weight, down_weight)
     )
@@ -1048,69 +1428,13 @@
         (0, dp * 48),
     )
     cosine, sine = rope_tables(4)
-    (
-        w_kept, gains, output, n1, n2, q, k, v, p, o, g, u, a, x_second, h,
-    ) = run_forward(packed, gains_placed, tokens, cosine, sine)
-    w_kept = w_kept.reshape(2, MODEL, WIDTH)
-    grad_residual = grad_out.astype(jnp.float32)
-    layer_results = [None] * layers
-    tri = jnp.tril(jnp.ones((512, 512), bool))
-    def gat(r):
-        return lax.all_gather(r.astype(jnp.bfloat16), "tensor", axis=0, tiled=True)
-    def rs(r):
-        return lax.psum_scatter(r.astype(jnp.bfloat16), "tensor", scatter_dimension=0, tiled=True).astype(jnp.float32)
-    f32 = jnp.float32
-    def unrot(vals):
-        c, s = cosine[:, : vals.shape[1]], sine[:, : vals.shape[1]]
-        v4 = vals.reshape(512, -1, 2, 48)
-        sw = v4[:, :, ::-1].reshape(vals.shape)
-        return vals * c - sw * s
-    for l in (1, 0):
-        W = w_kept[l]
-        residual = tokens.astype(f32) if l == 0 else x_second
-        dm = gat(grad_residual)
-        da = nn(dm, W[:, 3200:4224])
-        gd = tn(dm, a[l])
-        G, U = g[l].astype(f32), u[l].astype(f32)
-        sg = jax.nn.sigmoid(G)
-        dg = (da * U * sg * (1 + G * (1 - sg))).astype(jnp.bfloat16)
-        du = (da * G * sg).astype(jnp.bfloat16)
-        gg, gu = tn(n2[l], dg), tn(n2[l], du)
-        dn2 = rs(nt(dg, W[:, 1152:2176]) + nt(du, W[:, 2176:3200]))
-        gn, gain2 = norm_backward(h[l], gains[2 * l + 1], dn2)
-        gmid = grad_residual + gn
-        dhb = gat(gmid)
-        do = nn(dhb, W[:, 768:1152]).astype(jnp.bfloat16)
-        go = tn(dhb, o[l])
-        dqs, dks, dvs = [], [], []
-        for kv in range(2):
-            dk = dv = 0
-            for hh in (2 * kv, 2 * kv + 1):
-                P_ = jnp.where(tri, p[l, hh], 0).astype(f32)
-                doh = do[:, hh * 96 : hh * 96 + 96]
-                dP = nt(doh, v[l, kv, :, :96])
-                dS = (P_ * (dP - jnp.sum(dP * P_, -1, keepdims=True))).astype(jnp.bfloat16)
-                dqs.append(nn(dS, k[l, kv, :, :96]) * SCALING)
-                dk = dk + tn(dS, q[l, hh, :, :96]) * SCALING
-                dv = dv + tn(P_.astype(jnp.bfloat16), doh)
-            dks.append(dk)
-            dvs.append(dv)
-        dq = unrot(jnp.concatenate(dqs, 1)).astype(jnp.bfloat16)
-        dk = unrot(jnp.concatenate(dks, 1)).astype(jnp.bfloat16)
-        dv = jnp.concatenate(dvs, 1).astype(jnp.bfloat16)
-        dqkv = jnp.concatenate([dq, dk, dv], 1)
-        gqkv = tn(n1[l], dqkv)
-        dn1 = rs(nt(dqkv, W[:, :768]))
-        gn, gain1 = norm_backward(residual, gains[2 * l], dn1)
-        grad_residual = gmid + gn
-        layer_results[l] = (gqkv, go, gg, gu, gd, jnp.stack([gain1, gain2]))
-    grads = jnp.stack(
-        [jnp.concatenate([t.astype(jnp.bfloat16) for t in r[:5]], axis=1) for r in layer_results]
-    ).reshape(layers, 2, SIDE, SIDE, 48, WIDTH)
-    summed = scatter_grads(grads)
-    gains_summed = lax.psum_scatter(
-        lax.psum(jnp.stack([r[5] for r in layer_results]), "tensor"), "dp", scatter_dimension=2, tiled=True
+    w_kept, gains, output, *kept, x_second, h = run_forward(
+        packed, gains_placed, tokens, cosine, sine
     )
+    input_grad, summed, gains_grad, _ = run_backward(
+        gains, grad_out, tokens, cosine, sine, x_second, h, (w_kept, *kept)
+    )
+    gains_own = lax.dynamic_slice(gains_grad, (0, dp * 48), (4, 48)).reshape(2, 2, 48)
     pieces, start = [], 0
     for width in COLS:
         pieces.append(summed[:, :, start : start + width])
@@ -1118,7 +1442,7 @@
     query, key, value, out, gate, up, down = pieces
     return (
         output,
-        grad_residual,
+        input_grad,
         query,
         key,
         value,
@@ -1126,7 +1450,7 @@
         gate,
         up,
         jnp.swapaxes(down, 1, 2),
-        gains_summed,
+        gains_own,
     )
 
 

time: 975 us -> 472 us (0.48)
  waiting for transfers between devices: 338 us -> 0 us
  matrix products: 108 us -> 0 us
  Pallas kernels: 358 us -> 450 us
  local copies, waits for them, and re-layouts: 82.4 us -> 12.7 us
  other arithmetic: 54.7 us -> 1.15 us
  between operations: 15.5 us -> 1.09 us
    unnamed x10 -> x0, waiting for transfers between devices: 218 us -> none
    dot_general x52 -> x0, matrix products: 108 us -> none  [the longest x26 57.4 us: tn(): lax.dot_general(left, right, (((0,), (0,)), ((), ())), preferred_element_...]
    pallas_call x1, Pallas kernels: 157 us -> 259 us  [run_backward(): pl.pallas_call(backward_kernel, out_shape=(jax.ShapeDtypeStruct((OWN, MOD...]
    reduce_scatter x4 -> x0, waiting for transfers between devices: 67.8 us -> none  [rs(): lax.psum_scatter(r.astype(jnp.bfloat16), 'tensor', scatter_dimension=0, t...]
    all_gather x4 -> x0, waiting for transfers between devices: 51.7 us -> none  [gat(): return lax.all_gather(r.astype(jnp.bfloat16), 'tensor', axis=0, tiled=True)]
    concatenate x2 -> x0, local copies, waits for them, and re-layouts: 33.7 us -> none  [body(): jnp.concatenate([t.astype(jnp.bfloat16) for t in r[:5]], axis=1)]
    another operation x4 -> x0, other arithmetic: 23 us -> none  [the longest x1 21.1 us: body(): jnp.stack([jnp.concatenate([t.astype(jnp.bfloat16) for t in r[:5]], axis=...]
    slice x2 -> x0, local copies, waits for them, and re-layouts: 18.3 us -> none  [the longest x1 17.7 us: body(): W = w_kept[l]]
  transfers between devices with their start and end apart: 9 -> 0, of which waited for: 6 -> 0; matrix products, arithmetic and copies ran while one was open for 13% -> 0% of each run, Pallas kernels for 37% -> 0%
where the time goes in v3:
time: 472 us; the launch traced here: 465 us
  Pallas kernels  450 us (95%)
  local copies, waits for them, and re-layouts  12.7 us (3%)
    pallas_call x1, Pallas kernels, run_backward(): pl.pallas_call(backward_kernel, out_shape=(jax.ShapeDtypeStruct((OWN, MOD...  259 us
    pallas_call x1, Pallas kernels, run_forward(): pl.pallas_call(forward_kernel, out_shape=(kept(2, 2, 768, WIDTH), kept(8,...  191 us

profile of v3, /device:TPU:0, one launch (start us, length us, event | category | flops | bytes accessed | tf_op | source)
XLA Modules:
  0.0 465.0 jit_solution(3812508154770223130)
XLA Ops:
  0.7 0.7 convert.1
  1.4 0.3 dynamic_update_slice.3.gains_placed
  1.7 0.0 copy-start.5
  1.7 0.4 fusion.2
  2.1 0.1 tile.8
  2.2 0.0 copy-start.2
  2.3 0.0 copy-start.3
  2.3 0.0 copy-start.4
  2.3 0.0 copy-start.6
  2.3 0.0 copy-start.7
  2.3 0.0 copy-start.8
  2.3 0.0 copy-start.9
  2.3 1.1 copy.20.cosine
  3.5 0.1 tile.20
  3.6 0.0 copy-done.5
  3.6 1.1 copy.21.sine
  4.7 0.0 copy-done.2
  4.7 0.0 copy-done.3
  4.7 0.0 copy-done.4
  4.7 0.0 copy-done.6
  4.7 0.0 copy-done.7
  4.7 0.0 copy-done.8
  4.8 0.0 copy-done.9
  4.8 1.1 concatenate.9.shard
  5.9 190.7 %forward.1 = (bf16[2,2,768,4224]{3,2,1,0:T(8,128)(2,1)}, f32[8,1536]{1,0:T(8,128)}, bf16[128,1536]{1,0:T(8,128)(2,1)}, bf16[2,1536,512]{2,1,0:T(8,128)(2,1)}, bf...) custom-call(bf16[2,48,4224]{2,1,0:T(8,128)(2,1)} %concatenate.9.shar, ...), custom_call_target="tpu_custom_call" | custom-call | tf_op jit(solution)/shard_map/forward/pallas_call | solution.py:740
  196.5 259.4 %backward.1 = (f32[128,1536]{1,0:T(8,128)}, f32[2,48,4224]{2,1,0:T(8,128)}, f32[8,1536]{1,0:T(8,128)}, bf16[2,2,4,4,48,4224]{5,4,3,2,1,0:T(8,128)(2,1)}) custom-call(f32[8,1536]{1,0:T(8,128)} %get-tuple-element.29.gains, bf16[128,1536]{1,0:T(8,128)(2,1)} %grad_out.1, bf16[128,1536]{1,0:T(8,128)(2,1)} %tokens.3, f32[512,384]{1,0:T(8,128)} %copy.20.cosine, ...), custom_call_target="tpu_custom_call" | custom-call | tf_op jit(solution)/shard_map/backward/pallas_call | solution.py:1344
  456.0 0.0 copy-start.1
  456.0 0.0 copy-start
  456.0 1.4 constant_dynamic-slice_fusion
  457.4 1.7 fusion.3
  459.1 1.7 slice_bitcast_fusion.1
  460.8 2.3 slice_bitcast_fusion
  463.1 0.0 copy-done.1
  463.1 0.7 copy.27
  463.9 0.0 copy-done
  463.9 0.9 copy.28
  (3 shorter events, 0.0 us)
Async XLA Ops:
  1.7 1.9 copy-start.5
  2.2 2.5 copy-start.2
  2.3 2.5 copy-start.3
  2.3 2.5 copy-start.4
  2.3 2.5 copy-start.6
  2.3 2.5 copy-start.7
  2.3 2.4 copy-start.8
  2.3 2.4 copy-start.9
  456.0 7.2 %copy-start.1 = (bf16[128,1536]{1,0:T(8,128)(2,1)S(1)}, bf16[128,1536]{1,0:T(8,128)(2,1)}, u32[]{:S(2)}) copy-start(bf16[128,1536]{1,0:T(8,128)(2,1)} %get-tuple-element.68) | copy-start | bytes 1179652
  456.0 7.9 %copy-start = (f32[128,1536]{1,0:T(8,128)S(1)}, f32[128,1536]{1,0:T(8,128)}, u32[]{:S(2)}) copy-start(f32[128,1536]{1,0:T(8,128)} %get-tuple-element.69) | copy-start | bytes 2359300

commit v4 on v3

--- a/solution.py
+++ b/solution.py
@@ -21,7 +21,8 @@
 COLS = (384, 192, 192, 384, 1024, 1024, 1024)
 WIDTH = 4224
 ATTN_PARTS = (((0, 256), (256, 512)), ((512, 768), (768, 1152)))
-MLP_PARTS = (((1152, 1920), (1920, 2688)), ((2688, 3456), (3456, 4224)))
+GU_PARTS = (((1152, 1664), (1664, 2176)), ((2176, 2688), (2688, 3200)))
+DOWN_PARTS = (((3200, 3456), (3456, 3712)), ((3712, 3968), (3968, 4224)))
 
 norm_eps = 1e-05
 rope_base = 100000.0
@@ -158,113 +159,128 @@
     yield
 
 
+PIECES = 2
+PIECE = OWN // PIECES
+
+
 class Spread:
-    pieces = 2
-
     def __init__(self, wire, at, rows_ref):
         self.wire, self.at, self.rows_ref = wire, at, rows_ref
-        self.near = wire.slot()
-        self.over = [wire.slot() for _ in range(self.pieces)]
-        self.passed = [wire.slot() for _ in range(self.pieces)]
-        self.size = OWN // self.pieces
+        self.near = [wire.slot() for _ in range(PIECES)]
+        self.over = [wire.slot() for _ in range(PIECES)]
+        self.passed = [wire.slot() for _ in range(PIECES)]
         self.copies = []
 
-    def rows(self, tensor, piece=None):
-        start = pl.multiple_of(tensor * OWN, OWN)
-        if piece is None:
-            return self.rows_ref.at[pl.ds(start, OWN)]
-        return self.rows_ref.at[
-            pl.ds(pl.multiple_of(start + piece * self.size, self.size), self.size)
-        ]
-
-    def start(self):
+    def rows(self, tensor, piece):
+        start = pl.multiple_of(tensor * OWN + piece * PIECE, PIECE)
+        return self.rows_ref.at[pl.ds(start, PIECE)]
+
+    def send(self, piece):
         at, wire = self.at, self.wire
-        own = at.tensor
-        for piece in range(self.pieces):
-            block = self.rows(own, piece)
-            self.copies.append(wire.send(self.over[piece], block, block, at.above()))
-        self.copies.append(wire.send(self.near, self.rows(own), self.rows(own), at.twin()))
+        block = self.rows(at.tensor, piece)
+        self.copies.append(wire.send(self.over[piece], block, block, at.above()))
+        self.copies.append(wire.send(self.near[piece], block, block, at.twin()))
 
     def near_done(self):
         at = self.at
-        self.wire.arrive(self.near, self.rows(at.z_lo * 2 + 1 - at.core), at.twin())
-
-    def pass_on(self):
+        for piece in range(PIECES):
+            block = self.rows(at.z_lo * 2 + 1 - at.core, piece)
+            self.wire.arrive(self.near[piece], block, at.twin())
+
+    def pass_on(self, piece):
         at, wire = self.at, self.wire
-        there = (1 - at.z_lo) * 2 + at.core
-        for piece in range(self.pieces):
-            block = self.rows(there, piece)
-            wire.arrive(self.over[piece], block, at.above())
-            self.copies.append(wire.send(self.passed[piece], block, block, at.twin()))
-
-    def far_done(self):
+        block = self.rows((1 - at.z_lo) * 2 + at.core, piece)
+        wire.arrive(self.over[piece], block, at.above())
+        self.copies.append(wire.send(self.passed[piece], block, block, at.twin()))
+
+    def far_done(self, piece):
         at = self.at
-        there = (1 - at.z_lo) * 2 + 1 - at.core
-        for piece in range(self.pieces):
-            self.wire.arrive(self.passed[piece], self.rows(there, piece), at.twin())
-        for copy in self.copies:
-            self.wire.release(copy)
+        block = self.rows((1 - at.z_lo) * 2 + 1 - at.core, piece)
+        self.wire.arrive(self.passed[piece], block, at.twin())
+        if piece == PIECES - 1:
+            for copy in self.copies:
+                self.wire.release(copy)
 
 
 class Collect:
-    pieces = 2
-
     def __init__(self, wire, at, part, help_ref, near_ref, over_ref):
         self.wire, self.at, self.part = wire, at, part
         self.help_ref, self.near_ref, self.over_ref = help_ref, near_ref, over_ref
-        self.help = wire.slot()
+        self.help = [wire.slot() for _ in range(PIECES)]
         self.near = wire.slot()
-        self.over = [wire.slot() for _ in range(self.pieces)]
+        self.over = [wire.slot() for _ in range(PIECES)]
         self.copies = []
-        self.size = OWN // self.pieces
-
-    def rows(self, z_lo, core):
-        return pl.ds(pl.multiple_of((z_lo * 2 + core) * OWN, OWN), OWN)
-
-    def other_ready(self):
+
+    def rows(self, z_lo, core, piece):
+        start = (z_lo * 2 + core) * OWN + piece * PIECE
+        return pl.ds(pl.multiple_of(start, PIECE), PIECE)
+
+    def other_ready(self, piece):
         at = self.at
-        block = self.part.at[self.rows(1 - at.z_lo, 1 - at.core)]
-        self.copies.append(self.wire.send(self.help, block, self.help_ref, at.twin()))
+        block = self.part.at[self.rows(1 - at.z_lo, 1 - at.core, piece)]
+        landing = self.help_ref.at[pl.ds(piece * PIECE, PIECE)]
+        self.copies.append(self.wire.send(self.help[piece], block, landing, at.twin()))
 
     def own_ready(self):
         at = self.at
-        block = self.part.at[self.rows(at.z_lo, 1 - at.core)]
+        start = pl.multiple_of((at.z_lo * 2 + 1 - at.core) * OWN, OWN)
+        block = self.part.at[pl.ds(start, OWN)]
         self.copies.append(self.wire.send(self.near, block, self.near_ref, at.twin()))
 
-    def send_over(self):
+    def send_over(self, piece):
         at = self.at
-        self.wire.arrive(self.help, self.help_ref, at.twin())
-        for piece in range(self.pieces):
-            window = pl.ds(piece * self.size, self.size)
-            start = ((1 - at.z_lo) * 2 + at.core) * OWN + piece * self.size
-            rows = pl.ds(pl.multiple_of(start, self.size), self.size)
-            total = self.part[rows, :].astype(jnp.float32) + self.help_ref[window, :].astype(
-                jnp.float32
+        window = pl.ds(piece * PIECE, PIECE)
+        self.wire.arrive(self.help[piece], self.help_ref.at[window], at.twin())
+        rows = self.rows(1 - at.z_lo, at.core, piece)
+        total = self.part[rows, :].astype(jnp.float32) + self.help_ref[window, :].astype(
+            jnp.float32
+        )
+        self.part[rows, :] = total.astype(jnp.bfloat16)
+        self.copies.append(
+            self.wire.send(
+                self.over[piece], self.part.at[rows], self.over_ref.at[window], at.above()
             )
-            self.part[rows, :] = total.astype(jnp.bfloat16)
-            self.copies.append(
-                self.wire.send(
-                    self.over[piece],
-                    self.part.at[rows],
-                    self.over_ref.at[window],
-                    at.above(),
-                )
-            )
-
-    def result(self):
+        )
+
+    def result(self, piece):
         at = self.at
-        self.wire.arrive(self.near, self.near_ref, at.twin())
-        total = self.part[self.rows(at.z_lo, at.core), :].astype(jnp.float32) + self.near_ref[
-            ...
-        ].astype(jnp.float32)
-        for piece in range(self.pieces):
-            window = pl.ds(piece * self.size, self.size)
-            self.wire.arrive(self.over[piece], self.over_ref.at[window], at.above())
-        total = total + self.over_ref[...].astype(jnp.float32)
-        for copy in self.copies:
-            self.wire.release(copy)
-        self.copies = []
+        window = pl.ds(piece * PIECE, PIECE)
+        if piece == 0:
+            self.wire.arrive(self.near, self.near_ref, at.twin())
+        total = self.part[self.rows(at.z_lo, at.core, piece), :].astype(
+            jnp.float32
+        ) + self.near_ref[window, :].astype(jnp.float32)
+        self.wire.arrive(self.over[piece], self.over_ref.at[window], at.above())
+        total = total + self.over_ref[window, :].astype(jnp.float32)
+        if piece == PIECES - 1:
+            for copy in self.copies:
+                self.wire.release(copy)
         return total
+
+
+def here_rows(at):
+    return ((at.z_lo * 2 * OWN, 2 * OWN),)
+
+
+def there_rows(at, piece):
+    start = (1 - at.z_lo) * 2 * OWN + piece * PIECE
+    return ((start, PIECE), (start + OWN, PIECE))
+
+
+def windows(rows):
+    return [pl.ds(pl.multiple_of(start, size), size) for start, size in rows]
+
+
+def take(ref, rows, cols=slice(None)):
+    pieces = [ref[window, cols] for window in windows(rows)]
+    return pieces[0] if len(pieces) == 1 else jnp.concatenate(pieces, axis=0)
+
+
+def put(ref, rows, cols, value):
+    place = 0
+    for window, (_, size) in zip(windows(rows), rows):
+        ref[window, cols] = value[place : place + size]
+        place += size
 
 
 def nn(left, right):
@@ -327,10 +343,6 @@
             total = moved if total is None else total + moved
         tiles.append(total)
     return jnp.concatenate(tiles, axis=1)
-
-
-def chip_rows(z_lo):
-    return pl.ds(pl.multiple_of(z_lo * 256, 256), 256)
 
 
 def weight(w_ref, layer, cols):
@@ -444,21 +456,28 @@
     yield
 
 
+LAG = 2
+
+
 class Gather:
     def __init__(self, wire, local, at, shard, full, kept):
         self.wire, self.local, self.at, self.shard = wire, local, at, shard
         self.full, self.kept = full, kept
         self.groups = [
-            (layer, group) for layer in range(2) for group in (ATTN_PARTS, MLP_PARTS)
+            (layer, group)
+            for layer in range(2)
+            for group in (ATTN_PARTS, GU_PARTS, DOWN_PARTS)
         ]
         self.jobs = [gather_job(wire, at, full, *pair) for pair in self.groups]
         self.slots = [wire.slot() for _ in self.groups]
         self.own = []
-        order = [(0, 0), (0, 1)]
-        for index in range(len(self.jobs)):
-            order += [(index, 2), (index + 1, 0), (index, 3), (index, 4), (index + 1, 1)]
-            order += [(index, 5)]
-        self.order = [pair for pair in order if pair[0] < len(self.jobs)]
+        count = len(self.jobs)
+        self.order = [
+            (index, turn - LAG * index)
+            for turn in range(LAG * count + 6)
+            for index in range(count)
+            if 0 <= turn - LAG * index < 6
+        ]
         self.done = 0
 
     def columns(self, index):
@@ -509,21 +528,23 @@
 
 
 def project_heads(layer, rows, n1, w, cosine, sine, q_ref, k_ref, v_ref):
-    left = n1[layer, rows, :]
-    cosine_rows, sine_rows = cosine[rows, :], sine[rows, :]
+    left = take(n1.at[layer], rows)
+    cosine_rows, sine_rows = take(cosine, rows), take(sine, rows)
+    every = slice(None)
     query = nn(left, weight(w, layer, pl.ds(0, 384)))
     turned = query * cosine_rows + swap_halves(query) * sine_rows
     for head in range(4):
-        q_ref[layer, head, rows, :] = head_of(turned, head * HD).astype(jnp.bfloat16)
+        put(q_ref.at[layer, head], rows, every, head_of(turned, head * HD).astype(jnp.bfloat16))
     both = nn(left, weight(w, layer, pl.ds(384, 384)))
     turned = both * cosine_rows + swap_halves(both) * sine_rows
     for head in range(2):
-        k_ref[layer, head, rows, :] = head_of(turned, head * HD).astype(jnp.bfloat16)
-        v_ref[layer, head, rows, :] = head_of(both, 192 + head * HD).astype(jnp.bfloat16)
-
-
-def attend(layer, q_ref, k_ref, v_ref, p_ref, o_ref):
-    for block in range(4):
+        put(k_ref.at[layer, head], rows, every, head_of(turned, head * HD).astype(jnp.bfloat16))
+        value = head_of(both, 192 + head * HD).astype(jnp.bfloat16)
+        put(v_ref.at[layer, head], rows, every, value)
+
+
+def attend(layer, blocks, q_ref, k_ref, v_ref, p_ref, o_ref):
+    for block in blocks:
         rows = pl.ds(block * 128, 128)
         keys = (block + 1) * 128
         outputs = []
@@ -546,54 +567,48 @@
         o_ref[layer, rows, :] = side_by_side(outputs).astype(jnp.bfloat16)
 
 
-def out_partial(layer, rows, o_ref, w, part):
-    left = o_ref[layer, rows, :]
+def rows_partial(layer, rows, left_ref, w, cols, part):
+    left = take(left_ref, rows)
     for half in range(2):
-        for tile in range(3):
-            right = w[layer, half, pl.ds(tile * 256, 256), cut(OUT)]
-            part[rows, pl.ds(half * 768 + tile * 256, 256)] = nt(left, right).astype(jnp.bfloat16)
+
+        def tile(index, carry, half=half):
+            start = pl.multiple_of(index * 256, 256)
+            right = w[layer, half, pl.ds(start, 256), cut(cols)]
+            column = pl.ds(pl.multiple_of(half * 768 + start, 256), 256)
+            put(part, rows, column, nt(left, right).astype(jnp.bfloat16))
+            return carry
+
+        lax.fori_loop(0, 3, tile, 0)
 
 
 def hidden_rows(layer, rows, n2, w, g_ref, u_ref, a_ref):
-    left = n2[layer, rows, :]
+    left = take(n2.at[layer], rows)
 
     def tile(index, carry):
         start = pl.multiple_of(index * 256, 256)
+        column = pl.ds(start, 256)
         gate = nn(left, weight(w, layer, pl.ds(GATE[0] + start, 256)))
         up = nn(left, weight(w, layer, pl.ds(UP[0] + start, 256)))
         hidden = gate * up / (1.0 + jnp.exp(-gate))
-        g_ref[layer, rows, pl.ds(start, 256)] = gate.astype(g_ref.dtype)
-        u_ref[layer, rows, pl.ds(start, 256)] = up.astype(u_ref.dtype)
-        a_ref[layer, rows, pl.ds(start, 256)] = hidden.astype(jnp.bfloat16)
+        put(g_ref.at[layer], rows, column, gate.astype(g_ref.dtype))
+        put(u_ref.at[layer], rows, column, up.astype(u_ref.dtype))
+        put(a_ref.at[layer], rows, column, hidden.astype(jnp.bfloat16))
         return carry
 
     lax.fori_loop(0, 4, tile, 0)
-
-
-def down_partial(layer, rows, a_ref, w, part):
-    left = a_ref[layer, rows, :]
-    for half in range(2):
-
-        def tile(index, carry, half=half):
-            start = pl.multiple_of(index * 256, 256)
-            right = w[layer, half, pl.ds(start, 256), cut(DOWN)]
-            part[rows, pl.ds(pl.multiple_of(half * 768 + start, 256), 256)] = nt(
-                left, right
-            ).astype(jnp.bfloat16)
-            return carry
-
-        lax.fori_loop(0, 3, tile, 0)
 
 
 def forward_kernel(
     shard,
     gains_placed,
     tokens,
+    grad_out,
     cosine,
     sine,
     w_kept,
     gains,
-    output,
+    dm_kept,
+    dm_turned_kept,
     n1_kept,
     n2_kept,
     q_kept,
@@ -619,6 +634,7 @@
     a_ref,
     x_ref,
     h_ref,
+    dm,
     n1_turned,
     n2_turned,
     part,
@@ -641,9 +657,6 @@
     rounds = sum_small(wire, at, gains, gains_landing, False)
     for _ in rounds:
         gather.step()
-    x_ref[0] = tokens[...].astype(jnp.float32)
-    own = pl.ds(pl.multiple_of(at.tensor * OWN, OWN), OWN)
-    here, there = chip_rows(at.z_lo), chip_rows(1 - at.z_lo)
     turn = 0
 
     def collector():
@@ -654,47 +667,105 @@
             wire, at, part, help_ref.at[slot], near_ref.at[slot], over_ref.at[slot]
         )
 
+    def own(piece):
+        return pl.ds(pl.multiple_of(at.tensor * OWN + piece * PIECE, PIECE), PIECE)
+
+    def window(piece):
+        return pl.ds(piece * PIECE, PIECE)
+
+    here = here_rows(at)
     turning = [None, None]
+    spread = Spread(wire, at, n1.at[0])
+    for piece in range(PIECES):
+        x_rows = tokens[window(piece), :].astype(jnp.float32)
+        x_ref[0, window(piece), :] = x_rows
+        n1[0, own(piece), :] = normed(x_rows, gains[pl.ds(0, 1), :])
+        spread.send(piece)
     for layer in range(2):
-        n1[layer, own, :] = normed(x_ref[layer], gains[pl.ds(2 * layer, 1), :])
-        spread = Spread(wire, at, n1.at[layer])
-        spread.start()
-        gather.until(2 * layer)
         heads = (n1, w, cosine, sine, q_ref, k_ref, v_ref)
         spread.near_done()
+        gather.until(3 * layer)
         project_heads(layer, here, *heads)
+        spread.pass_on(0)
         gather.step()
-        spread.pass_on()
-        spread.far_done()
-        project_heads(layer, there, *heads)
+        spread.far_done(0)
+        project_heads(layer, there_rows(at, 0), *heads)
+        spread.pass_on(1)
+        spread.far_done(1)
+        project_heads(layer, there_rows(at, 1), *heads)
         for source, target in ((q_ref, q_kept), (k_ref, k_kept), (v_ref, v_kept)):
             local.start(source.at[layer], target.at[layer])
+        collect = collector()
+        around = (q_ref, k_ref, v_ref, p_ref, o_ref)
+
+        def blocks(first, second, layer=layer, around=around):
+            @pl.when(at.z_lo == 0)
+            def _():
+                attend(layer, first, *around)
+
+            @pl.when(at.z_lo == 1)
+            def _():
+                attend(layer, second, *around)
+
+        blocks((2, 3), (0, 1))
+        for piece in range(PIECES):
+            rows_partial(layer, there_rows(at, piece), o_ref.at[layer], w, OUT, part)
+            collect.other_ready(piece)
         gather.step()
-        attend(layer, q_ref, k_ref, v_ref, p_ref, o_ref)
+        collect.send_over(0)
+        collect.send_over(1)
+        blocks((0, 1), (2, 3))
+        rows_partial(layer, here, o_ref.at[layer], w, OUT, part)
+        collect.own_ready()
         for source, target in ((p_ref, p_kept), (o_ref, o_kept)):
             local.start(source.at[layer], target.at[layer])
-        collect = collector()
-        out_partial(layer, there, o_ref, w, part)
-        collect.other_ready()
-        out_partial(layer, here, o_ref, w, part)
-        collect.own_ready()
-        collect.send_over()
+        gather.step()
+        spread = Spread(wire, at, n2.at[layer])
+        for piece in range(PIECES):
+            h_rows = x_ref[layer, window(piece), :] + collect.result(piece)
+            h_ref[layer, window(piece), :] = h_rows
+            n2[layer, own(piece), :] = normed(h_rows, gains[pl.ds(2 * layer + 1, 1), :])
+            spread.send(piece)
+        if layer == 1:
+            spread_back = Spread(wire, at, dm)
+            for piece in range(PIECES):
+                dm[own(piece), :] = grad_out[window(piece), :]
+                spread_back.send(piece)
         if layer == 1:
             local.wait(turning[0])
         turn_rows(n1.at[layer], n1_turned)
         turning[0] = local.start(n1_turned, n1_kept.at[layer])
-        gather.step()
-        h_ref[layer] = x_ref[layer] + collect.result()
-        n2[layer, own, :] = normed(h_ref[layer], gains[pl.ds(2 * layer + 1, 1), :])
-        spread = Spread(wire, at, n2.at[layer])
-        spread.start()
-        gather.until(2 * layer + 1)
         spread.near_done()
-        hidden_rows(layer, here, n2, w, g_ref, u_ref, a_ref)
-        gather.step()
-        spread.pass_on()
-        spread.far_done()
-        hidden_rows(layer, there, n2, w, g_ref, u_ref, a_ref)
+        gather.until(3 * layer + 1)
+        mlp = (n2, w, g_ref, u_ref, a_ref)
+        hidden_rows(layer, here, *mlp)
+        if layer == 1:
+            spread.pass_on(0)
+            spread_back.pass_on(0)
+            spread.far_done(0)
+            hidden_rows(layer, there_rows(at, 0), *mlp)
+            spread.pass_on(1)
+            spread_back.pass_on(1)
+            spread.far_done(1)
+            hidden_rows(layer, there_rows(at, 1), *mlp)
+            spread_back.near_done()
+            spread_back.far_done(0)
+            spread_back.far_done(1)
+        else:
+            collect = collector()
+            spread.pass_on(0)
+            gather.until(2)
+            rows_partial(layer, here, a_ref.at[layer], w, DOWN, part)
+            collect.own_ready()
+            gather.step()
+            for piece in range(PIECES):
+                spread.far_done(piece)
+                hidden_rows(layer, there_rows(at, piece), *mlp)
+                rows_partial(layer, there_rows(at, piece), a_ref.at[layer], w, DOWN, part)
+                collect.other_ready(piece)
+                if piece + 1 < PIECES:
+                    spread.pass_on(piece + 1)
+                collect.send_over(piece)
         for source, target in (
             (h_ref, h_kept),
             (g_ref, g_kept),
@@ -702,23 +773,25 @@
             (a_ref, a_kept),
         ):
             local.start(source.at[layer], target.at[layer])
-        collect = collector()
-        down_partial(layer, there, a_ref, w, part)
-        collect.other_ready()
-        down_partial(layer, here, a_ref, w, part)
-        collect.own_ready()
-        collect.send_over()
         if layer == 1:
             local.wait(turning[1])
         turn_rows(n2.at[layer], n2_turned)
         turning[1] = local.start(n2_turned, n2_kept.at[layer])
         gather.step()
-        total = h_ref[layer] + collect.result()
-        if layer == 0:
-            x_ref[1] = total
-            local.start(x_ref.at[1], x_kept)
-        else:
-            output[...] = total.astype(jnp.bfloat16)
+        if layer == 1:
+            local.start(dm, dm_kept)
+            local.wait(turning[0])
+            turn_rows(dm, n1_turned)
+            local.start(n1_turned, dm_turned_kept)
+            break
+        spread = Spread(wire, at, n1.at[1])
+        for piece in range(PIECES):
+            total = h_ref[layer, window(piece), :] + collect.result(piece)
+            x_ref[1, window(piece), :] = total
+            n1[1, own(piece), :] = normed(total, gains[pl.ds(2, 1), :])
+            spread.send(piece)
+        local.start(x_ref.at[1], x_kept)
+    gather.until(5)
     local.drain()
     wire.drain()
 
@@ -726,7 +799,7 @@
 KEEP = jnp.bfloat16
 
 
-def run_forward(shard, gains_placed, tokens, cosine, sine):
+def run_forward(shard, gains_placed, tokens, grad_out, cosine, sine):
     def kept(*shape, kind=jnp.bfloat16):
         return jax.ShapeDtypeStruct(shape, kind)
 
@@ -736,13 +809,14 @@
     vmem = pl.BlockSpec(memory_space=pltpu.VMEM)
     hbm = pl.BlockSpec(memory_space=pl.ANY)
     float32 = jnp.float32
-    wires = 4 * 41 + 7 + 8 * 5 + 4
+    wires = 6 * 41 + 7 + 5 * 6 + 3 * 5
     return pl.pallas_call(
         forward_kernel,
         out_shape=(
             kept(2, 2, 768, WIDTH),
             kept(8, MODEL, kind=float32),
-            kept(OWN, MODEL),
+            kept(SEQ_ROWS, MODEL),
+            kept(MODEL, SEQ_ROWS),
             kept(2, MODEL, SEQ_ROWS),
             kept(2, MODEL, SEQ_ROWS),
             kept(2, 4, SEQ_ROWS, 128),
@@ -756,8 +830,8 @@
             kept(OWN, MODEL, kind=float32),
             kept(2, OWN, MODEL, kind=float32),
         ),
-        in_specs=[vmem] * 5,
-        out_specs=(hbm, vmem, vmem) + (hbm,) * 12,
+        in_specs=[vmem] * 6,
+        out_specs=(hbm, vmem) + (hbm,) * 14,
         scratch_shapes=[
             held(2, 2, 768, WIDTH),
             held(2, SEQ_ROWS, MODEL),
@@ -772,6 +846,7 @@
             held(2, SEQ_ROWS, 1024),
             held(2, OWN, MODEL, kind=float32),
             held(2, OWN, MODEL, kind=float32),
+            held(SEQ_ROWS, MODEL),
             held(MODEL, SEQ_ROWS),
             held(MODEL, SEQ_ROWS),
             held(SEQ_ROWS, MODEL),
@@ -781,13 +856,13 @@
             held(7, 8, MODEL, kind=float32),
             pltpu.SemaphoreType.DMA((wires,)),
             pltpu.SemaphoreType.DMA((wires,)),
-            pltpu.SemaphoreType.DMA((40,)),
+            pltpu.SemaphoreType.DMA((48,)),
         ],
         compiler_params=pltpu.CompilerParams(
             collective_id=0, has_side_effects=True, vmem_limit_bytes=62 * 2**20
         ),
         name="forward",
-    )(shard, gains_placed, tokens, cosine, sine)
+    )(shard, gains_placed, tokens, grad_out, cosine, sine)
 
 
 JOBS = (
@@ -797,7 +872,8 @@
     (((0, 256), (256, 512)), ((512, 768), (768, 1152))),
 )
 JOB_WIDTH = 1152
-SETS = 2
+SETS = 3
+LAG_BACK = 2
 
 
 def add_rows(target, terms):
@@ -882,9 +958,10 @@
             )
             cols = half(part, step)
             near[number, step] = local.start(part["region"](step, cols), big(near_side, cols))
+    yield
+    for number, part in enumerate(parts):
         cols = part["whole"]
         near[number, 0] = local.start(part["region"](0, cols), big(near_own, cols))
-    yield
     for step in (1, -1):
         for number, part in enumerate(parts):
             cols = half(part, step)
@@ -959,19 +1036,19 @@
         self.last = []
         self.jobs = []
         for index, (layer, group) in enumerate(self.groups):
-            bufs = tuple(ref.at[index % SETS] for ref in sets)
+            bufs = tuple(ref.at[index % ref.shape[0]] for ref in sets)
             self.jobs.append(
                 scatter_job(
                     wire, local, at, grads, layer, group, bufs, self.finisher(index, layer, group)
                 )
             )
-        order = [(0, 0), (0, 1)]
         count = len(self.jobs)
-        for index in range(count):
-            order += [(index + 1, 0), (index, 2), (index, 3), (index + 1, 1), (index, 4)]
-            order += [(index - 1, 5)]
-        order += [(count - 1, 5)]
-        self.order = [pair for pair in order if 0 <= pair[0] < count]
+        self.order = [
+            (index, turn - LAG_BACK * index)
+            for turn in range(LAG_BACK * count + 6)
+            for index in range(count)
+            if 0 <= turn - LAG_BACK * index < 6
+        ]
         self.done = 0
         self.ready = 0
 
@@ -992,6 +1069,16 @@
             self.last.append((index, slot, landing, target))
 
         return finish
+
+    def turn(self):
+        if self.done < len(self.order):
+            index, stage = self.order[self.done]
+            now = LAG_BACK * index + stage
+            while self.done < len(self.order):
+                index, stage = self.order[self.done]
+                if LAG_BACK * index + stage != now or index >= self.ready:
+                    return
+                self.step()
 
     def step(self, count=1):
         at = self.at
@@ -1035,36 +1122,22 @@
 
 
 def hidden_back(rows, dm, w, g_ref, u_ref, dgu):
-    left = dm[rows, :]
+    left = take(dm, rows)
 
     def tile(index, carry):
         start = pl.multiple_of(index * 256, 256)
+        column = pl.ds(start, 256)
         grad = nn(left, weight(w, 0, pl.ds(DOWN[0] + start, 256)))
-        gate = g_ref[rows, pl.ds(start, 256)].astype(jnp.float32)
-        up = u_ref[rows, pl.ds(start, 256)].astype(jnp.float32)
+        gate = take(g_ref, rows, column).astype(jnp.float32)
+        up = take(u_ref, rows, column).astype(jnp.float32)
         sigma = 1.0 / (1.0 + jnp.exp(-gate))
-        dgu[rows, pl.ds(start, 256)] = (
-            grad * up * sigma * (1.0 + gate * (1.0 - sigma))
-        ).astype(jnp.bfloat16)
-        dgu[rows, pl.ds(1024 + start, 256)] = (grad * gate * sigma).astype(jnp.bfloat16)
+        grad_gate = grad * up * sigma * (1.0 + gate * (1.0 - sigma))
+        put(dgu, rows, column, grad_gate.astype(jnp.bfloat16))
+        column = pl.ds(pl.multiple_of(1024 + start, 256), 256)
+        put(dgu, rows, column, (grad * gate * sigma).astype(jnp.bfloat16))
         return carry
 
     lax.fori_loop(0, 4, tile, 0)
-
-
-def rows_partial(rows, left_ref, w, cols, part):
-    left = left_ref[rows, :]
-    for half in range(2):
-
-        def tile(index, carry, half=half):
-            start = pl.multiple_of(index * 256, 256)
-            right = w[0, half, pl.ds(start, 256), cut(cols)]
-            part[rows, pl.ds(pl.multiple_of(half * 768 + start, 256), 256)] = nt(
-                left, right
-            ).astype(jnp.bfloat16)
-            return carry
-
-        lax.fori_loop(0, 3, tile, 0)
 
 
 def attend_back(q_ref, k_ref, v_ref, p_ref, do_ref, dk_ref, dv_ref, cosine, sine, dqkv):
@@ -1107,6 +1180,8 @@
     x_second,
     h_ref,
     w_kept,
+    dm_kept,
+    dm_turned_kept,
     n1_kept,
     n2_kept,
     q_kept,
@@ -1117,6 +1192,7 @@
     g_kept,
     u_kept,
     a_kept,
+    output,
     input_grad,
     summed,
     gains_grad,
@@ -1167,8 +1243,6 @@
     local = Local(local_sems)
     sets = (one, two_up, two_down, small_one, small_up, small_down, near_side, near_own)
     scatter = Scatter(wire, local, at, grads, summed, sets, leaving, landed, credits)
-    own = pl.ds(pl.multiple_of(at.tensor * OWN, OWN), OWN)
-    here, there = chip_rows(at.z_lo), chip_rows(1 - at.z_lo)
     turn = 0
 
     def collector():
@@ -1193,6 +1267,8 @@
             g=(g_kept, g_ref),
             u=(u_kept, u_ref),
             a=(a_kept, a_ref),
+            dm=(dm_kept, dm.at[0]),
+            turned=(dm_turned_kept, turned),
         )
         columns = dict(down=DOWN, gu=(GATE[0], UP[1]), out=OUT, qkv=QKV)
         for name in names:
@@ -1201,7 +1277,8 @@
                 loads[name] = local.start(w_kept.at[layer, :, :, cols], w.at[0, :, :, cols])
             else:
                 kept, held = pairs[name]
-                loads[name] = local.start(kept.at[layer], held)
+                source = kept if name in ("dm", "turned") else kept.at[layer]
+                loads[name] = local.start(source, held)
 
     def ready(*names):
         for name in names:
@@ -1209,26 +1286,34 @@
 
     mlp_names = ("down", "g", "u", "gu", "a", "n2")
     attn_names = ("out", "v", "p", "k", "q", "qkv", "o", "n1")
-    load(1, mlp_names)
+    load(1, ("a", "down", "turned", "dm", "g", "u", "gu", "n2"))
     load(1, attn_names)
     staging = [None, None]
     tiles = 0
+    behind = []
+
+    def keep_tile(layer, left, right_ref, start, size, column):
+        nonlocal tiles
+        slot = tiles % 2
+        tiles += 1
+        if staging[slot] is not None:
+            local.wait(staging[slot])
+        product = nn(left[...], right_ref[:, pl.ds(start, size)])
+        staged[slot, :, :, :, :, pl.ds(0, size)] = product.astype(jnp.bfloat16).reshape(
+            2, SIDE, SIDE, 48, size
+        )
+        staging[slot] = local.start(
+            staged.at[slot, :, :, :, :, pl.ds(0, size)],
+            grads.at[layer, :, :, :, :, pl.ds(column, size)],
+        )
 
     def keep_grads(layer, left, right_ref, start, width, column):
-        nonlocal tiles
         for tile in range(0, width, 256):
             size = min(256, width - tile)
-            slot = tiles % 2
-            tiles += 1
-            if staging[slot] is not None:
-                local.wait(staging[slot])
-            product = nn(left[...], right_ref[:, pl.ds(start + tile, size)])
-            staged[slot, :, :, :, :, pl.ds(0, size)] = product.astype(jnp.bfloat16).reshape(
-                2, SIDE, SIDE, 48, size
-            )
-            staging[slot] = local.start(
-                staged.at[slot, :, :, :, :, pl.ds(0, size)],
-                grads.at[layer, :, :, :, :, pl.ds(column + tile, size)],
+            behind.append(
+                lambda tile=tile, size=size: keep_tile(
+                    layer, left, right_ref, start + tile, size, column + tile
+                )
             )
 
     def grads_kept():
@@ -1238,95 +1323,183 @@
                 staging[slot] = None
         scatter.ready += 1
 
+    def fill(count):
+        for _ in range(min(count, len(behind))):
+            behind.pop(0)()
+
+    def own(piece):
+        return pl.ds(pl.multiple_of(at.tensor * OWN + piece * PIECE, PIECE), PIECE)
+
+    def window(piece):
+        return pl.ds(piece * PIECE, PIECE)
+
+    here = here_rows(at)
     gains_grad[...] = jnp.zeros_like(gains_grad)
+    every = ((0, SEQ_ROWS),)
     dx[0] = grad_out[...].astype(jnp.float32)
+    mlp = (dm.at[0], w, g_ref, u_ref, dgu)
+    gu_columns = (GATE[0], UP[1])
+    spread = None
     for layer in (1, 0):
-        dm[0, own, :] = dx[0].astype(jnp.bfloat16)
-        spread = Spread(wire, at, dm.at[0])
-        spread.start()
+        if layer == 1:
+            collect_out = collector()
+            ready("a", "down")
+            for piece in range(PIECES):
+                rows_partial(0, there_rows(at, piece), a_ref, w, DOWN, part)
+                collect_out.other_ready(piece)
+            ready("turned")
+            keep_grads(layer, turned, a_ref, 0, 1024, DOWN[0])
+            behind.append(grads_kept)
+            fill(3)
+            collect_out.send_over(0)
+            collect_out.send_over(1)
+            rows_partial(0, here, a_ref, w, DOWN, part)
+            collect_out.own_ready()
+            fill(len(behind))
+            scatter.turn()
+            ready("dm", "g", "u")
+            hidden_back(every, *mlp)
+            ready("n2")
+            keep_grads(layer, n2_turned, dgu, 0, 1024, GATE[0])
+            behind.append(grads_kept)
+            keep_grads(layer, n2_turned, dgu, 1024, 1024, UP[0])
+            behind.append(grads_kept)
+            fill(2)
+            for piece in range(PIECES):
+                total = h_ref[1, window(piece), :] + collect_out.result(piece)
+                output[window(piece), :] = total.astype(jnp.bfloat16)
+            scatter.turn()
+            ready("gu")
+            collect = collector()
+            for piece in range(PIECES):
+                rows_partial(0, there_rows(at, piece), dgu, w, gu_columns, part)
+                collect.other_ready(piece)
+            fill(1)
+            collect.send_over(0)
+            collect.send_over(1)
+            rows_partial(0, here, dgu, w, gu_columns, part)
+            collect.own_ready()
+            scatter.turn()
+        else:
+            spread.near_done()
+            ready("down", "g", "u")
+            hidden_back(here, *mlp)
+            scatter.turn()
+            fill(2)
+            spread.pass_on(0)
+            fill(1)
+            collect = collector()
+            for piece in range(PIECES):
+                spread.far_done(piece)
+                hidden_back(there_rows(at, piece), *mlp)
+                if piece == 0:
+                    ready("gu")
+                rows_partial(0, there_rows(at, piece), dgu, w, gu_columns, part)
+                collect.other_ready(piece)
+                if piece + 1 < PIECES:
+                    spread.pass_on(piece + 1)
+                    fill(2)
+                    scatter.turn()
+                collect.send_over(piece)
+            rows_partial(0, here, dgu, w, gu_columns, part)
+            collect.own_ready()
+            fill(len(behind))
+            load(0, attn_names)
+            ready("a", "n2")
+            turn_rows(dm.at[0], turned)
+            scatter.turn()
+            keep_grads(layer, turned, a_ref, 0, 1024, DOWN[0])
+            behind.append(grads_kept)
+            keep_grads(layer, n2_turned, dgu, 0, 1024, GATE[0])
+            behind.append(grads_kept)
+            keep_grads(layer, n2_turned, dgu, 1024, 1024, UP[0])
+            behind.append(grads_kept)
+        fill(3)
+        spread = Spread(wire, at, dm.at[1])
+        gain_rows = None
+        for piece in range(PIECES):
+            normed_grad, gain_row = norm_backward(
+                h_ref[layer, window(piece), :],
+                gains[pl.ds(2 * layer + 1, 1), :],
+                collect.result(piece),
+            )
+            gain_rows = gain_row if gain_rows is None else gain_rows + gain_row
+            dh = dx[0, window(piece), :] + normed_grad
+            dx[1, window(piece), :] = dh
+            dm[1, own(piece), :] = dh.astype(jnp.bfloat16)
+            spread.send(piece)
+            if piece + 1 < PIECES:
+                fill(2)
+        gains_grad[pl.ds(2 * layer + 1, 1), :] = gain_rows
+        scatter.turn()
+        ready("out")
+
+        def heads_back(rows):
+            grad = nn(take(dm.at[1], rows), weight(w, 0, cut(OUT)))
+            for head in range(4):
+                put(do_ref.at[head], rows, slice(None), head_of(grad, head * HD).astype(jnp.bfloat16))
+
         spread.near_done()
-        ready("down", "g", "u")
-        hidden_back(here, dm.at[0], w, g_ref, u_ref, dgu)
-        if layer == 0:
-            scatter.step()
-        spread.pass_on()
-        spread.far_done()
-        hidden_back(there, dm.at[0], w, g_ref, u_ref, dgu)
-        collect = collector()
-        ready("gu")
-        rows_partial(there, dgu, w, (GATE[0], UP[1]), part)
-        collect.other_ready()
-        rows_partial(here, dgu, w, (GATE[0], UP[1]), part)
-        collect.own_ready()
-        collect.send_over()
-        if layer == 0:
-            scatter.step(2)
-        turn_rows(dm.at[0], turned)
-        ready("a")
-        keep_grads(layer, turned, a_ref, 0, 1024, DOWN[0])
-        grads_kept()
-        scatter.step()
-        if layer == 1:
-            total = collect.result()
-        ready("n2")
-        keep_grads(layer, n2_turned, dgu, 0, 1024, GATE[0])
-        grads_kept()
-        if layer == 0:
-            total = collect.result()
-        normed_grad, gain_row = norm_backward(
-            h_ref[layer], gains[pl.ds(2 * layer + 1, 1), :], total
-        )
-        gains_grad[pl.ds(2 * layer + 1, 1), :] = gain_row
-        dx[1] = dx[0] + normed_grad
-        dm[1, own, :] = dx[1].astype(jnp.bfloat16)
-        spread = Spread(wire, at, dm.at[1])
-        spread.start()
-        scatter.step(2)
-        keep_grads(layer, n2_turned, dgu, 1024, 1024, UP[0])
-        grads_kept()
+        heads_back(here)
+        fill(4)
+        spread.pass_on(0)
+        fill(3)
+        spread.far_done(0)
+        heads_back(there_rows(at, 0))
+        scatter.turn()
+        spread.pass_on(1)
+        fill(len(behind))
         if layer == 1:
             load(0, mlp_names)
-        ready("out")
-        spread.near_done()
-
-        def heads_back(rows):
-            grad = nn(dm[1, rows, :], weight(w, 0, cut(OUT)))
-            for head in range(4):
-                do_ref[head, rows, :] = head_of(grad, head * HD).astype(jnp.bfloat16)
-
-        heads_back(here)
-        spread.pass_on()
-        spread.far_done()
-        heads_back(there)
+        spread.far_done(1)
+        heads_back(there_rows(at, 1))
         ready("v", "p", "k", "q")
         attend_back(
             q_ref, k_ref, v_ref, p_ref, do_ref, dk_ref, dv_ref, cosine, sine, dqkv
         )
-        scatter.step()
         collect = collector()
         ready("qkv")
-        rows_partial(there, dqkv, w, QKV, part)
-        collect.other_ready()
-        rows_partial(here, dqkv, w, QKV, part)
+        for piece in range(PIECES):
+            rows_partial(0, there_rows(at, piece), dqkv, w, QKV, part)
+            collect.other_ready(piece)
+        scatter.turn()
+        collect.send_over(0)
+        collect.send_over(1)
+        rows_partial(0, here, dqkv, w, QKV, part)
         collect.own_ready()
-        collect.send_over()
         turn_rows(dm.at[1], turned)
         ready("o", "n1")
         keep_grads(layer, turned, o_ref, 0, 384, OUT[0])
         keep_grads(layer, n1_turned, dqkv, 0, 768, QKV[0])
-        grads_kept()
-        if layer == 1:
-            load(0, attn_names)
-        scatter.step(2)
-        total = collect.result()
-        rows_in = tokens[...].astype(jnp.float32) if layer == 0 else x_second[...]
-        normed_grad, gain_row = norm_backward(rows_in, gains[pl.ds(2 * layer, 1), :], total)
-        gains_grad[pl.ds(2 * layer, 1), :] = gain_row
-        dx[0] = dx[1] + normed_grad
-    input_grad[...] = dx[0]
+        behind.append(grads_kept)
+        fill(2)
+        if layer == 0:
+            scatter.turn()
+        rows_in = tokens if layer == 0 else x_second
+        spread = Spread(wire, at, dm.at[0]) if layer == 1 else None
+        gain_rows = None
+        for piece in range(PIECES):
+            normed_grad, gain_row = norm_backward(
+                rows_in[window(piece), :].astype(jnp.float32),
+                gains[pl.ds(2 * layer, 1), :],
+                collect.result(piece),
+            )
+            gain_rows = gain_row if gain_rows is None else gain_rows + gain_row
+            dx_rows = dx[1, window(piece), :] + normed_grad
+            if layer == 1:
+                dx[0, window(piece), :] = dx_rows
+                dm[0, own(piece), :] = dx_rows.astype(jnp.bfloat16)
+                spread.send(piece)
+                if piece == 0:
+                    fill(1)
+                    scatter.turn()
+            else:
+                input_grad[window(piece), :] = dx_rows
+        gains_grad[pl.ds(2 * layer, 1), :] = gain_rows
+    fill(len(behind))
     rounds = sum_small(wire, at, gains_grad, gains_landing, True)
     for _ in rounds:
-        scatter.step()
+        scatter.turn()
     while scatter.done < len(scatter.order):
         scatter.step()
     local.drain()
@@ -1340,17 +1513,18 @@
     vmem = pl.BlockSpec(memory_space=pltpu.VMEM)
     hbm = pl.BlockSpec(memory_space=pl.ANY)
     float32 = jnp.float32
-    wires = 8 * 26 + 9 + 8 * 5 + 4
+    wires = 8 * 26 + 9 + 3 * 6 + 5 * 5
     return pl.pallas_call(
         backward_kernel,
         out_shape=(
+            jax.ShapeDtypeStruct((OWN, MODEL), jnp.bfloat16),
             jax.ShapeDtypeStruct((OWN, MODEL), float32),
             jax.ShapeDtypeStruct((2, 48, WIDTH), float32),
             jax.ShapeDtypeStruct((8, MODEL), float32),
             jax.ShapeDtypeStruct((2, 2, SIDE, SIDE, 48, WIDTH), jnp.bfloat16),
         ),
         in_specs=[vmem] * 7 + [hbm] * len(kept),
-        out_specs=(vmem, vmem, vmem, hbm),
+        out_specs=(vmem, vmem, vmem, vmem, hbm),
         scratch_shapes=[
             held(1, 2, 768, WIDTH),
             held(MODEL, SEQ_ROWS),
@@ -1382,18 +1556,18 @@
             held(SETS, 2, 48, JOB_WIDTH),
             held(SETS, 2, 48, JOB_WIDTH),
             held(SETS, 2, 48, JOB_WIDTH),
-            held(SETS, 2, SIDE, 48, JOB_WIDTH),
-            held(SETS, 2, SIDE, 48, JOB_WIDTH),
+            held(1, 2, SIDE, 48, JOB_WIDTH),
+            held(1, 2, SIDE, 48, JOB_WIDTH),
             held(8, 48, JOB_WIDTH),
             held(8, 48, JOB_WIDTH),
             held(9, 8, MODEL, kind=float32),
             pltpu.SemaphoreType.DMA((wires,)),
             pltpu.SemaphoreType.DMA((wires,)),
-            pltpu.SemaphoreType.DMA((28 + 40 + 48,)),
+            pltpu.SemaphoreType.DMA((30 + 40 + 48,)),
             pltpu.SemaphoreType.REGULAR((4,)),
         ],
         compiler_params=pltpu.CompilerParams(
-            collective_id=1, has_side_effects=True, vmem_limit_bytes=62 * 2**20
+            collective_id=1, has_side_effects=True, vmem_limit_bytes=63 * 2**20
         ),
         name="backward",
     )(gains, grad_out, tokens, cosine, sine, x_second, h, *kept)
@@ -1428,10 +1602,10 @@
         (0, dp * 48),
     )
     cosine, sine = rope_tables(4)
-    w_kept, gains, output, *kept, x_second, h = run_forward(
-        packed, gains_placed, tokens, cosine, sine
+    w_kept, gains, *kept, x_second, h = run_forward(
+        packed, gains_placed, tokens, grad_out, cosine, sine
     )
-    input_grad, summed, gains_grad, _ = run_backward(
+    output, input_grad, summed, gains_grad, _ = run_backward(
         gains, grad_out, tokens, cosine, sine, x_second, h, (w_kept, *kept)
     )
     gains_own = lax.dynamic_slice(gains_grad, (0, dp * 48), (4, 48)).reshape(2, 2, 48)

time: 472 us -> 413 us (0.88)
  Pallas kernels: 450 us -> 390 us
    pallas_call x1, Pallas kernels: 259 us -> 205 us  [run_backward(): pl.pallas_call(backward_kernel, out_shape=(jax.ShapeDtypeStruct((OWN, MOD...]
    pallas_call x1, Pallas kernels: 191 us -> 185 us  [run_forward(): pl.pallas_call(forward_kernel, out_shape=(kept(2, 2, 768, WIDTH), kept(8,...]
where the time goes in v4:
time: 413 us; the launch traced here: 405 us
  Pallas kernels  390 us (94%)
  local copies, waits for them, and re-layouts  12.7 us (3%)
    pallas_call x1, Pallas kernels, run_backward(): pl.pallas_call(backward_kernel, out_shape=(jax.ShapeDtypeStruct((OWN, MOD...  205 us
    pallas_call x1, Pallas kernels, run_forward(): pl.pallas_call(forward_kernel, out_shape=(kept(2, 2, 768, WIDTH), kept(8,...  185 us

profile of v4, /device:TPU:0, one launch (start us, length us, event | category | flops | bytes accessed | tf_op | source)
XLA Modules:
  0.0 404.8 jit_solution(17752521998803347891)
XLA Ops:
  0.7 0.7 convert.1
  1.4 0.3 dynamic_update_slice.3.gains_placed
  1.7 0.0 copy-start.5
  1.7 0.4 fusion.2
  2.1 0.1 tile.8
  2.2 0.0 copy-start.2
  2.3 0.0 copy-start.3
  2.3 0.0 copy-start.4
  2.3 0.0 copy-start.6
  2.3 0.0 copy-start.7
  2.3 0.0 copy-start.8
  2.3 0.0 copy-start.9
  2.3 1.1 copy.20.cosine
  3.5 0.1 tile.20
  3.6 0.0 copy-done.5
  3.6 1.1 copy.21.sine
  4.7 0.0 copy-done.2
  4.7 0.0 copy-done.3
  4.7 0.0 copy-done.4
  4.7 0.0 copy-done.6
  4.7 0.0 copy-done.7
  4.7 0.0 copy-done.8
  4.8 0.0 copy-done.9
  4.8 1.1 concatenate.9.shard
  5.9 184.7 %forward.1 = (bf16[2,2,768,4224]{3,2,1,0:T(8,128)(2,1)}, f32[8,1536]{1,0:T(8,128)}, bf16[512,1536]{1,0:T(8,128)(2,1)}, bf16[1536,512]{1,0:T(8,128)(2,1)}, bf16[2...) custom-call(bf16[2,48,4224]{2,1,0:T(8,128)(2,1)} %concatenate.9.shar, ...), custom_call_target="tpu_custom_call" | custom-call | tf_op jit(solution)/shard_map/forward/pallas_call | solution.py:813
  190.5 205.0 %backward.1 = (bf16[128,1536]{1,0:T(8,128)(2,1)}, f32[128,1536]{1,0:T(8,128)}, f32[2,48,4224]{2,1,0:T(8,128)}, f32[8,1536]{1,0:T(8,128)}, bf16[2,2,4,4,48,4224]{5,4,3,2,1,0:T(8,128)(2,1)}) custom-call(f32[8,1536]{1,0:T(8,128)} %get-tuple-element.30.gains, bf16[128,1536]{1,0:T(8,128)(2,1)} %grad_out.3, bf16[128,1536]{1,0:T(8,128)(2,1)} %tokens.3, ...), custom_call_target="tpu_custom_call" | custom-call | tf_op jit(solution)/shard_map/backward/pallas_call | solution.py:1517
  395.5 0.0 copy-start.1
  395.5 0.0 copy-start
  395.6 1.4 constant_dynamic-slice_fusion
  397.0 1.7 fusion.3
  398.7 1.7 slice_bitcast_fusion.1
  400.4 2.3 slice_bitcast_fusion
  402.7 0.0 copy-done.1
  402.7 0.7 copy.27
  403.4 0.0 copy-done
  403.4 0.9 copy.28
  (3 shorter events, 0.0 us)
Async XLA Ops:
  1.7 1.9 copy-start.5
  2.2 2.5 copy-start.2
  2.3 2.5 copy-start.3
  2.3 2.5 copy-start.4
  2.3 2.5 copy-start.6
  2.3 2.4 copy-start.7
  2.3 2.4 copy-start.8
  2.3 2.4 copy-start.9
  395.5 7.2 %copy-start.1 = (bf16[128,1536]{1,0:T(8,128)(2,1)S(1)}, bf16[128,1536]{1,0:T(8,128)(2,1)}, u32[]{:S(2)}) copy-start(bf16[128,1536]{1,0:T(8,128)(2,1)} %get-tuple-element.72) | copy-start | bytes 1179652
  395.5 7.9 %copy-start = (f32[128,1536]{1,0:T(8,128)S(1)}, f32[128,1536]{1,0:T(8,128)}, u32[]{:S(2)}) copy-start(f32[128,1536]{1,0:T(8,128)} %get-tuple-element.73) | copy-start | bytes 2359300

commit v5 on v4

--- a/solution.py
+++ b/solution.py
@@ -456,6 +456,7 @@
     yield
 
 
+STEPS = (1, 2, 1, 2)
 LAG = 2
 
 
@@ -603,8 +604,8 @@
     gains_placed,
     tokens,
     grad_out,
-    cosine,
-    sine,
+    cosine_kept,
+    sine_kept,
     w_kept,
     gains,
     dm_kept,
@@ -621,6 +622,8 @@
     a_kept,
     x_kept,
     h_kept,
+    cosine,
+    sine,
     w,
     n1,
     n2,
@@ -652,6 +655,7 @@
     local = Local(local_sems)
     gather = Gather(wire, local, at, shard, w, w_kept)
     gather.begin()
+    tables = [local.start(cosine_kept, cosine), local.start(sine_kept, sine)]
     gather.step()
     gains[...] = gains_placed[...]
     rounds = sum_small(wire, at, gains, gains_landing, False)
@@ -685,9 +689,11 @@
         heads = (n1, w, cosine, sine, q_ref, k_ref, v_ref)
         spread.near_done()
         gather.until(3 * layer)
+        while tables:
+            local.wait(tables.pop())
         project_heads(layer, here, *heads)
+        gather.step(STEPS[0])
         spread.pass_on(0)
-        gather.step()
         spread.far_done(0)
         project_heads(layer, there_rows(at, 0), *heads)
         spread.pass_on(1)
@@ -711,7 +717,6 @@
         for piece in range(PIECES):
             rows_partial(layer, there_rows(at, piece), o_ref.at[layer], w, OUT, part)
             collect.other_ready(piece)
-        gather.step()
         collect.send_over(0)
         collect.send_over(1)
         blocks((0, 1), (2, 3))
@@ -719,7 +724,7 @@
         collect.own_ready()
         for source, target in ((p_ref, p_kept), (o_ref, o_kept)):
             local.start(source.at[layer], target.at[layer])
-        gather.step()
+        gather.step(STEPS[1])
         spread = Spread(wire, at, n2.at[layer])
         for piece in range(PIECES):
             h_rows = x_ref[layer, window(piece), :] + collect.result(piece)
@@ -739,33 +744,37 @@
         gather.until(3 * layer + 1)
         mlp = (n2, w, g_ref, u_ref, a_ref)
         hidden_rows(layer, here, *mlp)
+        gather.step(STEPS[2])
         if layer == 1:
             spread.pass_on(0)
             spread_back.pass_on(0)
             spread.far_done(0)
             hidden_rows(layer, there_rows(at, 0), *mlp)
+            gather.step()
             spread.pass_on(1)
             spread_back.pass_on(1)
             spread.far_done(1)
             hidden_rows(layer, there_rows(at, 1), *mlp)
+            gather.step()
             spread_back.near_done()
             spread_back.far_done(0)
             spread_back.far_done(1)
         else:
+            spread.pass_on(0)
+            spread.far_done(0)
+            hidden_rows(layer, there_rows(at, 0), *mlp)
+            spread.pass_on(1)
+            spread.far_done(1)
+            hidden_rows(layer, there_rows(at, 1), *mlp)
+            gather.until(2)
             collect = collector()
-            spread.pass_on(0)
-            gather.until(2)
+            for piece in range(PIECES):
+                rows_partial(layer, there_rows(at, piece), a_ref.at[layer], w, DOWN, part)
+                collect.other_ready(piece)
+            collect.send_over(0)
             rows_partial(layer, here, a_ref.at[layer], w, DOWN, part)
             collect.own_ready()
-            gather.step()
-            for piece in range(PIECES):
-                spread.far_done(piece)
-                hidden_rows(layer, there_rows(at, piece), *mlp)
-                rows_partial(layer, there_rows(at, piece), a_ref.at[layer], w, DOWN, part)
-                collect.other_ready(piece)
-                if piece + 1 < PIECES:
-                    spread.pass_on(piece + 1)
-                collect.send_over(piece)
+            collect.send_over(1)
         for source, target in (
             (h_ref, h_kept),
             (g_ref, g_kept),
@@ -777,7 +786,7 @@
             local.wait(turning[1])
         turn_rows(n2.at[layer], n2_turned)
         turning[1] = local.start(n2_turned, n2_kept.at[layer])
-        gather.step()
+        gather.step(STEPS[3])
         if layer == 1:
             local.start(dm, dm_kept)
             local.wait(turning[0])
@@ -830,9 +839,11 @@
             kept(OWN, MODEL, kind=float32),
             kept(2, OWN, MODEL, kind=float32),
         ),
-        in_specs=[vmem] * 6,
+        in_specs=[hbm] + [vmem] * 3 + [hbm] * 2,
         out_specs=(hbm, vmem) + (hbm,) * 14,
         scratch_shapes=[
+            held(SEQ_ROWS, 384, kind=float32),
+            held(SEQ_ROWS, 384, kind=float32),
             held(2, 2, 768, WIDTH),
             held(2, SEQ_ROWS, MODEL),
             held(2, SEQ_ROWS, MODEL),
@@ -1175,10 +1186,10 @@
     gains,
     grad_out,
     tokens,
-    cosine,
-    sine,
-    x_second,
-    h_ref,
+    cosine_kept,
+    sine_kept,
+    x_kept,
+    h_kept,
     w_kept,
     dm_kept,
     dm_turned_kept,
@@ -1197,6 +1208,10 @@
     summed,
     gains_grad,
     grads,
+    cosine,
+    sine,
+    x_second,
+    h_ref,
     w,
     n1_turned,
     n2_turned,
@@ -1288,6 +1303,15 @@
     attn_names = ("out", "v", "p", "k", "q", "qkv", "o", "n1")
     load(1, ("a", "down", "turned", "dm", "g", "u", "gu", "n2"))
     load(1, attn_names)
+    tables = [
+        local.start(*pair)
+        for pair in (
+            (h_kept, h_ref),
+            (x_kept, x_second),
+            (cosine_kept, cosine),
+            (sine_kept, sine),
+        )
+    ]
     staging = [None, None]
     tiles = 0
     behind = []
@@ -1365,6 +1389,8 @@
             keep_grads(layer, n2_turned, dgu, 1024, 1024, UP[0])
             behind.append(grads_kept)
             fill(2)
+            while tables:
+                local.wait(tables.pop())
             for piece in range(PIECES):
                 total = h_ref[1, window(piece), :] + collect_out.result(piece)
                 output[window(piece), :] = total.astype(jnp.bfloat16)
@@ -1523,9 +1549,13 @@
             jax.ShapeDtypeStruct((8, MODEL), float32),
             jax.ShapeDtypeStruct((2, 2, SIDE, SIDE, 48, WIDTH), jnp.bfloat16),
         ),
-        in_specs=[vmem] * 7 + [hbm] * len(kept),
+        in_specs=[vmem] * 3 + [hbm] * (4 + len(kept)),
         out_specs=(vmem, vmem, vmem, vmem, hbm),
         scratch_shapes=[
+            held(SEQ_ROWS, 384, kind=float32),
+            held(SEQ_ROWS, 384, kind=float32),
+            held(OWN, MODEL, kind=float32),
+            held(2, OWN, MODEL, kind=float32),
             held(1, 2, 768, WIDTH),
             held(MODEL, SEQ_ROWS),
             held(MODEL, SEQ_ROWS),
@@ -1563,7 +1593,7 @@
             held(9, 8, MODEL, kind=float32),
             pltpu.SemaphoreType.DMA((wires,)),
             pltpu.SemaphoreType.DMA((wires,)),
-            pltpu.SemaphoreType.DMA((30 + 40 + 48,)),
+            pltpu.SemaphoreType.DMA((34 + 40 + 48,)),
             pltpu.SemaphoreType.REGULAR((4,)),
         ],
         compiler_params=pltpu.CompilerParams(

time: 413 us -> 408 us (0.988)
  no operation moved by 1% of the time
where the time goes in v5:
time: 408 us; the launch traced here: 401 us
  Pallas kernels  386 us (95%)
  local copies, waits for them, and re-layouts  12.7 us (3%)
    pallas_call x1, Pallas kernels, run_backward(): pl.pallas_call(backward_kernel, out_shape=(jax.ShapeDtypeStruct((OWN, MOD...  205 us
    pallas_call x1, Pallas kernels, run_forward(): pl.pallas_call(forward_kernel, out_shape=(kept(2, 2, 768, WIDTH), kept(8,...  181 us

profile of v5, /device:TPU:0, one launch (start us, length us, event | category | flops | bytes accessed | tf_op | source)
XLA Modules:
  0.0 400.8 jit_solution(763939818839931533)
XLA Ops:
  0.7 0.7 convert.1
  1.4 0.3 dynamic_update_slice.3.gains_placed
  1.7 0.0 copy-start.5
  1.7 0.4 fusion.2
  2.1 0.1 tile.8
  2.2 0.0 copy-start.2
  2.3 0.0 copy-start.3
  2.3 0.0 copy-start.4
  2.3 0.0 copy-start.6
  2.3 0.0 copy-start.7
  2.3 0.0 copy-start.8
  2.3 0.0 copy-start.9
  2.3 1.1 copy.20.cosine_kept
  3.5 0.1 tile.20
  3.6 0.0 copy-done.5
  3.6 1.1 copy.21.sine_kept
  4.7 0.0 copy-done.2
  4.7 0.0 copy-done.3
  4.7 0.0 copy-done.4
  4.7 0.0 copy-done.6
  4.7 0.0 copy-done.7
  4.7 0.0 copy-done.8
  4.8 0.0 copy-done.9
  4.8 1.1 concatenate.9.shard
  5.9 180.9 %forward.1 = (bf16[2,2,768,4224]{3,2,1,0:T(8,128)(2,1)}, f32[8,1536]{1,0:T(8,128)}, bf16[512,1536]{1,0:T(8,128)(2,1)}, bf16[1536,512]{1,0:T(8,128)(2,1)}, bf16[2...) custom-call(bf16[2,48,4224]{2,1,0:T(8,128)(2,1)} %concatenate.9.shar, ...), custom_call_target="tpu_custom_call" | custom-call | tf_op jit(solution)/shard_map/forward/pallas_call | solution.py:822
  186.7 204.9 %backward.1 = (bf16[128,1536]{1,0:T(8,128)(2,1)}, f32[128,1536]{1,0:T(8,128)}, f32[2,48,4224]{2,1,0:T(8,128)}, f32[8,1536]{1,0:T(8,128)}, bf16[2,2,4,4,48,4224]{5,4,3,2,1,0:T(8,128)(2,1)}) custom-call(f32[8,1536]{1,0:T(8,128)} %get-tuple-element.30.gains, bf16[128,1536]{1,0:T(8,128)(2,1)} %grad_out.3, bf16[128,1536]{1,0:T(8,128)(2,1)} %tokens.3, ...), custom_call_target="tpu_custom_call" | custom-call | tf_op jit(solution)/shard_map/backward/pallas_call | solution.py:1543
  391.6 0.0 copy-start.1
  391.6 0.0 copy-start
  391.6 1.4 constant_dynamic-slice_fusion
  393.1 1.7 fusion.3
  394.8 1.7 slice_bitcast_fusion.1
  396.5 2.3 slice_bitcast_fusion
  398.8 0.0 copy-done.1
  398.8 0.7 copy.27
  399.5 0.0 copy-done
  399.5 0.9 copy.28
  (3 shorter events, 0.0 us)
Async XLA Ops:
  1.7 1.9 copy-start.5
  2.2 2.5 copy-start.2
  2.3 2.5 copy-start.3
  2.3 2.5 copy-start.4
  2.3 2.5 copy-start.6
  2.3 2.4 copy-start.7
  2.3 2.4 copy-start.8
  2.3 2.4 copy-start.9
  391.6 7.2 %copy-start.1 = (bf16[128,1536]{1,0:T(8,128)(2,1)S(1)}, bf16[128,1536]{1,0:T(8,128)(2,1)}, u32[]{:S(2)}) copy-start(bf16[128,1536]{1,0:T(8,128)(2,1)} %get-tuple-element.72) | copy-start | bytes 1179652
  391.6 7.9 %copy-start = (f32[128,1536]{1,0:T(8,128)S(1)}, f32[128,1536]{1,0:T(8,128)}, u32[]{:S(2)}) copy-start(f32[128,1536]{1,0:T(8,128)} %get-tuple-element.73) | copy-start | bytes 2359300

commit v6 on v5

--- a/solution.py
+++ b/solution.py
@@ -1388,7 +1388,7 @@
             behind.append(grads_kept)
             keep_grads(layer, n2_turned, dgu, 1024, 1024, UP[0])
             behind.append(grads_kept)
-            fill(2)
+            fill(5)
             while tables:
                 local.wait(tables.pop())
             for piece in range(PIECES):
@@ -1498,7 +1498,7 @@
         keep_grads(layer, turned, o_ref, 0, 384, OUT[0])
         keep_grads(layer, n1_turned, dqkv, 0, 768, QKV[0])
         behind.append(grads_kept)
-        fill(2)
+        fill(6 if layer == 1 else 2)
         if layer == 0:
             scatter.turn()
         rows_in = tokens if layer == 0 else x_second

time: 408 us -> 416 us (1.020)
  Pallas kernels: 386 us -> 394 us
    pallas_call x1, Pallas kernels: 205 us -> 213 us  [run_backward(): pl.pallas_call(backward_kernel, out_shape=(jax.ShapeDtypeStruct((OWN, MOD...]
where the time goes in v6:
time: 416 us; the launch traced here: 408 us
  Pallas kernels  394 us (95%)
  local copies, waits for them, and re-layouts  12.7 us (3%)
    pallas_call x1, Pallas kernels, run_backward(): pl.pallas_call(backward_kernel, out_shape=(jax.ShapeDtypeStruct((OWN, MOD...  213 us
    pallas_call x1, Pallas kernels, run_forward(): pl.pallas_call(forward_kernel, out_shape=(kept(2, 2, 768, WIDTH), kept(8,...  181 us

profile of v6, /device:TPU:0, one launch (start us, length us, event | category | flops | bytes accessed | tf_op | source)
XLA Modules:
  0.0 408.3 jit_solution(7290380697451139780)
XLA Ops:
  0.7 0.7 convert.1
  1.4 0.3 dynamic_update_slice.3.gains_placed
  1.7 0.0 copy-start.5
  1.7 0.4 fusion.2
  2.1 0.1 tile.8
  2.2 0.0 copy-start.2
  2.3 0.0 copy-start.3
  2.3 0.0 copy-start.4
  2.3 0.0 copy-start.6
  2.3 0.0 copy-start.7
  2.3 0.0 copy-start.8
  2.3 0.0 copy-start.9
  2.3 1.1 copy.20.cosine_kept
  3.5 0.1 tile.20
  3.6 0.0 copy-done.5
  3.6 1.1 copy.21.sine_kept
  4.7 0.0 copy-done.2
  4.7 0.0 copy-done.3
  4.7 0.0 copy-done.4
  4.7 0.0 copy-done.6
  4.7 0.0 copy-done.7
  4.7 0.0 copy-done.8
  4.8 0.0 copy-done.9
  4.8 1.1 concatenate.9.shard
  5.9 180.9 %forward.1 = (bf16[2,2,768,4224]{3,2,1,0:T(8,128)(2,1)}, f32[8,1536]{1,0:T(8,128)}, bf16[512,1536]{1,0:T(8,128)(2,1)}, bf16[1536,512]{1,0:T(8,128)(2,1)}, bf16[2...) custom-call(bf16[2,48,4224]{2,1,0:T(8,128)(2,1)} %concatenate.9.shar, ...), custom_call_target="tpu_custom_call" | custom-call | tf_op jit(solution)/shard_map/forward/pallas_call | solution.py:822
  186.8 212.6 %backward.1 = (bf16[128,1536]{1,0:T(8,128)(2,1)}, f32[128,1536]{1,0:T(8,128)}, f32[2,48,4224]{2,1,0:T(8,128)}, f32[8,1536]{1,0:T(8,128)}, bf16[2,2,4,4,48,4224]{5,4,3,2,1,0:T(8,128)(2,1)}) custom-call(f32[8,1536]{1,0:T(8,128)} %get-tuple-element.30.gains, bf16[128,1536]{1,0:T(8,128)(2,1)} %grad_out.3, bf16[128,1536]{1,0:T(8,128)(2,1)} %tokens.3, ...), custom_call_target="tpu_custom_call" | custom-call | tf_op jit(solution)/shard_map/backward/pallas_call | solution.py:1543
  399.4 0.0 copy-start.1
  399.4 0.0 copy-start
  399.4 1.4 constant_dynamic-slice_fusion
  400.8 1.7 fusion.3
  402.5 1.7 slice_bitcast_fusion.1
  404.3 2.3 slice_bitcast_fusion
  406.5 0.0 copy-done.1
  406.5 0.7 copy.27
  407.3 0.0 copy-done
  407.3 0.9 copy.28
  (3 shorter events, 0.0 us)
Async XLA Ops:
  1.7 1.9 copy-start.5
  2.2 2.5 copy-start.2
  2.3 2.5 copy-start.3
  2.3 2.5 copy-start.4
  2.3 2.5 copy-start.6
  2.3 2.4 copy-start.7
  2.3 2.4 copy-start.8
  2.3 2.4 copy-start.9
  399.4 7.2 %copy-start.1 = (bf16[128,1536]{1,0:T(8,128)(2,1)S(1)}, bf16[128,1536]{1,0:T(8,128)(2,1)}, u32[]{:S(2)}) copy-start(bf16[128,1536]{1,0:T(8,128)(2,1)} %get-tuple-element.72) | copy-start | bytes 1179652
  399.4 7.9 %copy-start = (f32[128,1536]{1,0:T(8,128)S(1)}, f32[128,1536]{1,0:T(8,128)}, u32[]{:S(2)}) copy-start(f32[128,1536]{1,0:T(8,128)} %get-tuple-element.73) | copy-start | bytes 2359300
